TPU v7x, 32 devices: a whole 2x2x4 slice. The times are simulated.
32 devices in a mesh: dp: 16 (over z, y, core), mp: 2 (over x).
Axes of the slice: x: 2, y: 2, z: 4, core: 2. Of those that a mesh axis runs over, the one named last changes fastest.
Arguments:
- tokens: bfloat16 [20480, 1280], P(('dp', 'mp')), may hold values from -6 to 6
- segment_ids: int32 [128, 160], P('dp'), may hold values from 0 to 3, never falling along the last dimension, each value on 1 to 80 neighbouring positions
- game_ids: int32 [128], P('dp'), may hold values from 0 to 40
- return_bins: int32 [20480], P(('dp', 'mp')), may hold values from 0 to 119
- action_bins: int32 [20480], P(('dp', 'mp')), may hold values from 0 to 17
- reward_bins: int32 [20480], P(('dp', 'mp')), may hold values from 0 to 3
- valid_flags: int32 [20480, 3], P(('dp', 'mp')), may hold values 0 or 1
- step_count: int32 [1], replicated, may hold values from 1 to 20
- entry_weight: float32 [3, 1280, 1280], P(None, 'dp', 'mp'), may hold values from -0.15625 to 0.15625
- entry_state: float32 [2, 3, 1280, 1280], P(None, None, 'dp', 'mp')
- exit_weight: float32 [1280, 1280], P(('mp', 'dp')), may hold values from -0.5 to 0.5
- exit_state: float32 [2, 1280, 1280], P(None, ('mp', 'dp'))
- up_weight: float32 [1280, 5120], P('dp', 'mp'), may hold values from -0.15625 to 0.15625
- up_state: float32 [2, 1280, 5120], P(None, 'dp', 'mp')
- down_weight: float32 [5120, 1280], P(('mp', 'dp')), may hold values from -0.078125 to 0.078125
- down_state: float32 [2, 5120, 1280], P(None, ('mp', 'dp'))
- head_weight: float32 [142, 1280], replicated, may hold values from -0.15625 to 0.15625
- head_state: float32 [2, 142, 1280], replicated
- norm_params: float32 [6, 1280], replicated
- norm_state: float32 [2, 6, 1280], replicated
Outputs:
- entry_new: float32 [3, 1280, 1280], P(None, 'dp', 'mp')
- entry_moments: float32 [2, 3, 1280, 1280], P(None, None, 'dp', 'mp')
- entry_half: bfloat16 [3, 1280, 1280], P(None, 'dp', 'mp')
- exit_new: float32 [1280, 1280], P(('mp', 'dp'))
- exit_moments: float32 [2, 1280, 1280], P(None, ('mp', 'dp'))
- exit_half: bfloat16 [1280, 1280], P(('mp', 'dp'))
- up_new: float32 [1280, 5120], P('dp', 'mp')
- up_moments: float32 [2, 1280, 5120], P(None, 'dp', 'mp')
- up_half: bfloat16 [1280, 5120], P('dp', 'mp')
- down_new: float32 [5120, 1280], P(('mp', 'dp'))
- down_moments: float32 [2, 5120, 1280], P(None, ('mp', 'dp'))
- down_half: bfloat16 [5120, 1280], P(('mp', 'dp'))
- head_new: float32 [142, 1280], replicated
- head_moments: float32 [2, 142, 1280], replicated
- norm_new: float32 [6, 1280], replicated
- norm_moments: float32 [2, 6, 1280], replicated
- total_loss: float32 [], replicated
- grad_norm: float32 [], replicated
- matrix_norms: float32 [2, 5], replicated
Inputs may be any that keep to these rules, and one draw needn't show every extreme that they name: `segment_ids`: within each sequence of 160 tokens the segment numbers never fall.
All inputs are finite; a program needn't handle non-finite values. No bound on the sum of `valid_flags` on one device may be relied on, other than what follows from the above.
Results may differ from a plain program's by a relative error of at most 0.007.
Values may be sent and summed in bfloat16 or wider, within the bound.
No kernel may reach another device: no remote copies, remote signals or barrier semaphores. Data moves between devices by JAX's collectives and lax.ppermute only.
A program may use at most 384 MiB of HBM per device.

v0:
```python
import jax
import jax.numpy as jnp
from jax import lax
from jax.sharding import PartitionSpec as P

HD = 64
RB = 120
AB = 18
WB = 4
GAMES = 41
LEN = 160


clip_limit = 0.05
learn_rate = 0.5
beta_first = 0.5
beta_second = 0.5
weight_decay = 0.01
adam_eps = 1e-08
norm_eps = 1e-05
masked_score = -1e30


def layer_norm(rows, gain, shift):
    centred = rows - jnp.mean(rows, -1, keepdims=True)
    spread = jnp.mean(centred * centred, -1, keepdims=True)
    return centred * lax.rsqrt(spread + norm_eps) * gain + shift


def norm_back(rows, gain, shift, upstream):
    _, pullback = jax.vjp(layer_norm, rows, gain, shift)
    return pullback(upstream)


def matmul(left, right):
    return jnp.dot(left, right, preferred_element_type=jnp.float32)


def matmul_t(left, right):
    return jnp.einsum("ti,ji->tj", left, right, preferred_element_type=jnp.float32)


def contract(left, right):
    return jnp.einsum("ti,tj->ij", left, right, preferred_element_type=jnp.float32)


def gather_normed(rows, gain, shift):
    return lax.all_gather(
        layer_norm(rows, gain, shift).astype(jnp.bfloat16), "mp", axis=0, tiled=True
    )


def branch_out(summand):
    return lax.psum_scatter(summand, "mp", scatter_dimension=0, tiled=True)


def gather_grad(rows):
    return lax.all_gather(rows.astype(jnp.bfloat16), "mp", axis=0, tiled=True)


def scatter_grad(summand):
    return lax.psum_scatter(
        summand.astype(jnp.bfloat16), "mp", scatter_dimension=0, tiled=True
    ).astype(jnp.float32)


def part_loss(logits, targets, flags, token_scale):
    summed = jnp.zeros((), jnp.float32)
    offset = 0
    for column, span_cols in enumerate((RB, AB, WB)):
        section = logits[:, offset : offset + span_cols]
        log_probs = jax.nn.log_softmax(section, axis=-1)
        picked = (targets[column][:, None] == jnp.arange(span_cols)[None, :]).astype(jnp.float32)
        cross = -jnp.sum(log_probs * picked, -1)
        summed = summed + jnp.sum(flags[:, column].astype(jnp.float32) * token_scale * cross)
        offset = offset + span_cols
    return summed


def masked_scores(queries, key_rows, allowed):
    scores = jnp.einsum(
        "ihd,jhd->hij", queries, key_rows, preferred_element_type=jnp.float32
    ) * HD ** (-0.5)
    return jnp.where(allowed[None], scores, masked_score)


def attend_forward(queries, key_rows, values, allowed):
    scores = masked_scores(queries, key_rows, allowed)
    log_total = jax.nn.logsumexp(scores, axis=-1, keepdims=True)
    probs = jnp.exp(scores - log_total).astype(jnp.bfloat16)
    context = jnp.einsum("hij,jhd->ihd", probs, values, preferred_element_type=jnp.float32)
    return (context.astype(jnp.bfloat16), log_total)


def attend_backward(queries, key_rows, values, allowed, log_total, d_context):
    probs = jnp.exp(masked_scores(queries, key_rows, allowed) - log_total)
    d_probs = jnp.einsum("ihd,jhd->hij", d_context, values, preferred_element_type=jnp.float32)
    d_values = jnp.einsum(
        "hij,ihd->jhd", probs.astype(jnp.bfloat16), d_context, preferred_element_type=jnp.float32
    )
    d_scores = (probs * (d_probs - jnp.sum(probs * d_probs, -1, keepdims=True))).astype(
        jnp.bfloat16
    )
    d_queries = jnp.einsum(
        "hij,jhd->ihd", d_scores, key_rows, preferred_element_type=jnp.float32
    ) * HD ** (-0.5)
    d_keys = jnp.einsum(
        "hij,ihd->jhd", d_scores, queries, preferred_element_type=jnp.float32
    ) * HD ** (-0.5)
    return (d_queries, d_keys, d_values)


def adam_moments(state, grad, clip_factor, corr_first, corr_second):
    clipped = clip_factor * grad
    first = beta_first * state[0] + (1.0 - beta_first) * clipped
    second = beta_second * state[1] * state[1] + (1.0 - beta_second) * clipped * clipped
    direction = first / corr_first / (jnp.sqrt(second / corr_second) + adam_eps)
    return (jnp.stack([first, jnp.sqrt(second)]), direction)


def per_device(
    tokens,
    segment_ids,
    game_ids,
    return_bins,
    action_bins,
    reward_bins,
    valid_flags,
    step_count,
    entry_weight,
    entry_state,
    exit_weight,
    exit_state,
    up_weight,
    up_state,
    down_weight,
    down_state,
    head_weight,
    head_state,
    norm_params,
    norm_state,
):
    own_rows = tokens.shape[0]
    group_rows = segment_ids.shape[0] * segment_ids.shape[1]
    row_start = lax.axis_index("mp") * own_rows
    row_games = lax.dynamic_slice_in_dim(jnp.repeat(game_ids, LEN), row_start, own_rows)
    game_match = (row_games[:, None] == jnp.arange(GAMES)[None, :]).astype(jnp.float32)
    flag_float = valid_flags.astype(jnp.float32)
    local_counts = jnp.sum(game_match * jnp.sum(flag_float, -1, keepdims=True), 0)
    counts = lax.psum(local_counts, ("dp", "mp"))
    inverse = 1.0 / (GAMES * jnp.maximum(counts, 1.0))
    token_scale = jnp.sum(game_match * inverse[None, :], -1)
    entry_all, exit_all, up_all, down_all = (
        lax.all_gather(entry_weight.astype(jnp.bfloat16), "dp", axis=1, tiled=True),
        lax.all_gather(exit_weight.astype(jnp.bfloat16), "dp", axis=0, tiled=True),
        lax.all_gather(up_weight.astype(jnp.bfloat16), "dp", axis=0, tiled=True),
        lax.all_gather(down_weight.astype(jnp.bfloat16), "dp", axis=0, tiled=True),
    )
    heads_here = exit_all.shape[0] // HD
    order_ids = jnp.arange(group_rows)
    combined = (jnp.arange(segment_ids.shape[0])[:, None] * LEN + segment_ids).reshape(-1)
    allowed = (combined[:, None] == combined[None, :]) & (order_ids[None, :] <= order_ids[:, None])
    resid = tokens.astype(jnp.float32)
    normed_one = gather_normed(resid, norm_params[0], norm_params[3])
    projected = jnp.einsum(
        "td,sdc->stc", normed_one, entry_all, preferred_element_type=jnp.float32
    ).astype(jnp.bfloat16)
    shaped = projected.reshape(3, group_rows, heads_here, HD)
    context, log_total = attend_forward(shaped[0], shaped[1], shaped[2], allowed)
    context = context.reshape(group_rows, -1)
    after_attn = resid + branch_out(matmul(context, exit_all))
    normed_two = gather_normed(after_attn, norm_params[1], norm_params[4])
    up_pre = matmul(normed_two, up_all)
    activated = jax.nn.gelu(up_pre).astype(jnp.bfloat16)
    after_mlp = after_attn + branch_out(matmul(activated, down_all))
    final_norm = layer_norm(after_mlp, norm_params[2], norm_params[5]).astype(jnp.bfloat16)
    head_half = head_weight.astype(jnp.bfloat16)
    logits = matmul_t(final_norm, head_half)
    targets = (return_bins, action_bins, reward_bins)
    loss_local, loss_pull = jax.vjp(
        lambda values: part_loss(values, targets, valid_flags, token_scale), logits
    )
    loss_sum = lax.psum(loss_local, ("dp", "mp"))
    d_logits = loss_pull(jnp.ones_like(loss_local))[0].astype(jnp.bfloat16)
    d_head = contract(d_logits, final_norm)
    d_final = matmul(d_logits, head_half)
    d_mlp_in, d_gain_three, d_shift_three = norm_back(
        after_mlp, norm_params[2], norm_params[5], d_final
    )
    d_mlp_out = gather_grad(d_mlp_in)
    d_down = contract(activated, d_mlp_out)
    d_activated = matmul_t(d_mlp_out, down_all)
    _, gelu_pull = jax.vjp(jax.nn.gelu, up_pre)
    d_up_pre = gelu_pull(d_activated)[0].astype(jnp.bfloat16)
    d_up = contract(normed_two, d_up_pre)
    d_normed_two = scatter_grad(matmul_t(d_up_pre, up_all))
    d_ln_two, d_gain_two, d_shift_two = norm_back(
        after_attn, norm_params[1], norm_params[4], d_normed_two
    )
    d_after_attn = d_mlp_in + d_ln_two
    d_attn_out = gather_grad(d_after_attn)
    d_exit = contract(context, d_attn_out)
    d_context = (
        matmul_t(d_attn_out, exit_all).astype(jnp.bfloat16).reshape(group_rows, heads_here, HD)
    )
    d_queries, d_keys, d_values = attend_backward(
        shaped[0], shaped[1], shaped[2], allowed, log_total, d_context
    )
    d_projected = (
        jnp.stack([d_queries, d_keys, d_values]).reshape(3, group_rows, -1).astype(jnp.bfloat16)
    )
    d_entry = jnp.einsum("td,stc->sdc", normed_one, d_projected, preferred_element_type=jnp.float32)
    d_normed_one = scatter_grad(
        jnp.einsum("stc,sdc->td", d_projected, entry_all, preferred_element_type=jnp.float32)
    )
    _, d_gain_one, d_shift_one = norm_back(resid, norm_params[0], norm_params[3], d_normed_one)
    red_entry, red_exit, red_up, red_down = (
        lax.psum_scatter(d_entry, "dp", scatter_dimension=1, tiled=True),
        lax.psum_scatter(d_exit, "dp", scatter_dimension=0, tiled=True),
        lax.psum_scatter(d_up, "dp", scatter_dimension=0, tiled=True),
        lax.psum_scatter(d_down, "dp", scatter_dimension=0, tiled=True),
    )
    d_norms = jnp.stack(
        [d_gain_one, d_gain_two, d_gain_three, d_shift_one, d_shift_two, d_shift_three]
    )
    red_head, red_norms = lax.psum((d_head, d_norms), ("dp", "mp"))
    reduced = (red_entry, red_exit, red_up, red_down)
    masters = (entry_weight, exit_weight, up_weight, down_weight)
    states = (entry_state, exit_state, up_state, down_state)
    local_square = sum((jnp.sum(grad_part * grad_part) for grad_part in reduced))
    weight_local = jnp.stack([jnp.sum(master * master) for master in masters])
    small_square = jnp.sum(red_head * red_head) + jnp.sum(red_norms * red_norms)
    grad_total = lax.psum(local_square, ("dp", "mp"))
    grad_norm = jnp.sqrt(grad_total + small_square)
    clip_factor = jnp.minimum(1.0, clip_limit / grad_norm)
    step_float = step_count[0].astype(jnp.float32)
    corr_first = 1.0 - jnp.power(beta_first, step_float)
    corr_second = 1.0 - jnp.power(beta_second, step_float)
    new_states = []
    directions = []
    for matrix_id in range(4):
        state_new, direction = adam_moments(
            states[matrix_id], reduced[matrix_id], clip_factor, corr_first, corr_second
        )
        new_states.append(state_new)
        directions.append(direction + weight_decay * masters[matrix_id])
    update_local = jnp.stack([jnp.sum(direction * direction) for direction in directions])
    update_sums, weight_sums = lax.psum((update_local, weight_local), ("dp", "mp"))
    weight_norms = jnp.sqrt(weight_sums)
    update_norms = jnp.sqrt(update_sums)
    new_weights = [
        masters[matrix_id]
        - learn_rate * (weight_norms[matrix_id] / update_norms[matrix_id]) * directions[matrix_id]
        for matrix_id in range(4)
    ]
    head_moments, head_direction = adam_moments(
        head_state, red_head, clip_factor, corr_first, corr_second
    )
    head_direction = head_direction + weight_decay * head_weight
    head_wnorm = jnp.sqrt(jnp.sum(head_weight * head_weight))
    head_unorm = jnp.sqrt(jnp.sum(head_direction * head_direction))
    head_new = head_weight - learn_rate * (head_wnorm / head_unorm) * head_direction
    norm_moments, norm_direction = adam_moments(
        norm_state, red_norms, clip_factor, corr_first, corr_second
    )
    norm_new = norm_params - learn_rate * norm_direction
    matrix_norms = jnp.stack(
        [
            jnp.concatenate([weight_norms, head_wnorm[None]]),
            jnp.concatenate([update_norms, head_unorm[None]]),
        ]
    )
    return (
        new_weights[0],
        new_states[0],
        new_weights[0].astype(jnp.bfloat16),
        new_weights[1],
        new_states[1],
        new_weights[1].astype(jnp.bfloat16),
        new_weights[2],
        new_states[2],
        new_weights[2].astype(jnp.bfloat16),
        new_weights[3],
        new_states[3],
        new_weights[3].astype(jnp.bfloat16),
        head_new,
        head_moments,
        norm_new,
        norm_moments,
        loss_sum,
        grad_norm,
        matrix_norms,
    )


def solution(mesh):
    in_specs = (
        P(("dp", "mp"), None),
        P("dp", None),
        P("dp"),
        P(("dp", "mp")),
        P(("dp", "mp")),
        P(("dp", "mp")),
        P(("dp", "mp"), None),
        P(),
        P(None, "dp", "mp"),
        P(None, None, "dp", "mp"),
        P(("mp", "dp"), None),
        P(None, ("mp", "dp"), None),
        P("dp", "mp"),
        P(None, "dp", "mp"),
        P(("mp", "dp"), None),
        P(None, ("mp", "dp"), None),
        P(),
        P(),
        P(),
        P(),
    )
    out_specs = (
        P(None, "dp", "mp"),
        P(None, None, "dp", "mp"),
        P(None, "dp", "mp"),
        P(("mp", "dp"), None),
        P(None, ("mp", "dp"), None),
        P(("mp", "dp"), None),
        P("dp", "mp"),
        P(None, "dp", "mp"),
        P("dp", "mp"),
        P(("mp", "dp"), None),
        P(None, ("mp", "dp"), None),
        P(("mp", "dp"), None),
        P(),
        P(),
        P(),
        P(),
        P(),
        P(),
        P(),
    )
    return jax.shard_map(
        per_device, mesh=mesh, in_specs=in_specs, out_specs=out_specs, check_vma=False
    )
```

profile of v0, /device:TPU:0, one launch (start us, length us, event | category | flops | bytes accessed | tf_op | source)
XLA Modules:
  0.0 1808.7 jit_solution(1048469917227829961)
XLA Ops:
  18.0 45.0 %all-gather.9.cloned.1.call-done = bf16[1280,1280]{1,0:T(8,128)(2,1)} async-done(((bf16[640,1280]{1,0:T(8,128)(2,1)}), bf16[1280,1280]{1,0:T(8,128)(2,1)}) %all-gather.9.cloned.1.call-update) | async-done | bytes 3276816 | tf_op jit(solution)/shard_map/all_gather | solution.py:48
  63.0 57.2 %all-gather.11.cloned.1.call-done = bf16[3,1280,640]{2,1,0:T(8,128)(2,1)} async-done(((bf16[3,80,640]{2,1,0:T(8,128)(2,1)}), bf16[3,1280,640]{2,1,0:T(8,128)(2,1)}) %all-gather.11.cloned.1.call-update) | async-done | bytes 4915216 | tf_op jit(solution)/shard_map/all_gather | solution.py:154
  130.6 23.3 %fusion.77 = (f32[10,1280]{1,0:T(8,128)S(1)}, f32[10,1280,1280]{1,2,0:T(8,128)}) fusion(bf16[1280,10,64]{0,2,1:T(8,128)(2,1)S(1)} %bitcast.203, bf16[1280,10,64]{0,2,1:T(8,128)(2,1)S(1)} %bitcast.199, pred[1280,1280]{0,1:T(8,128)(4,1)S(1)} %fusion.14), kind=kOutput, calls=%fused_computation.233 | convolution fusion | flops 2146291200 | bytes 70502400 | tf_op jit(solution)/shard_map/ihd,jhd->hij/dot_general | solution.py:81
  153.9 20.9 %exponential_reduce_fusion = f32[10,1280]{1,0:T(8,128)S(1)} fusion(f32[10,1280,1280]{1,2,0:T(8,128)} %get-tuple-element.197, f32[10,1280]{1,0:T(8,128)S(1)} %is-finite_select_fusion), kind=kLoop, calls=%fused_computation.5 | loop fusion | flops 32755200 | bytes 65638400 | tf_op jit(solution)/shard_map/reduce_sum | solution.py:89
  174.8 22.5 %fusion.31 = bf16[10,64,1280]{2,1,0:T(8,128)(2,1)S(1)} fusion(bf16[1280,10,64]{0,2,1:T(8,128)(2,1)S(1)} %bitcast.197, f32[10,1280,1280]{1,2,0:T(8,128)} %get-tuple-element.197, f32[10,1280]{1,0:T(8,128)S(1)} %log_add_fusion), kind=kOutput, calls=%fused_computation.62 | convolution fusion | flops 2130739200 | bytes 68864000 | tf_op jit(solution)/shard_map/hij,jhd->ihd/dot_general | solution.py:91
  206.1 76.8 %reduce-scatter.8.cloned.1.call-done = f32[640,1280]{1,0:T(8,128)} async-done(((f32[1280,1280]{1,0:T(8,128)}), f32[640,1280]{1,0:T(8,128)}) %reduce-scatter.8.cloned.1.call-update) | async-done | bytes 3276816 | tf_op jit(solution)/shard_map/reduce_scatter | solution.py:54
  290.1 59.2 %all-gather.17.cloned.1.call-done = bf16[1280,2560]{1,0:T(8,128)(2,1)} async-done(((bf16[80,2560]{1,0:T(8,128)(2,1)}), bf16[1280,2560]{1,0:T(8,128)(2,1)}) %all-gather.17.cloned.1.call-update) | async-done | bytes 6553616 | tf_op jit(solution)/shard_map/all_gather | solution.py:156
  349.3 47.0 %all-gather.15.cloned.1.call-done = bf16[1280,1280]{1,0:T(8,128)(2,1)} async-done(((bf16[640,1280]{1,0:T(8,128)(2,1)}), bf16[1280,1280]{1,0:T(8,128)(2,1)}) %all-gather.15.cloned.1.call-update) | async-done | bytes 3276816 | tf_op jit(solution)/shard_map/all_gather | solution.py:48
  396.4 14.5 fusion.79
  410.9 52.1 %all-gather.19.cloned.1.call-done = bf16[2560,1280]{1,0:T(8,128)(2,1)} async-done(((bf16[160,1280]{1,0:T(8,128)(2,1)}), bf16[2560,1280]{1,0:T(8,128)(2,1)}) %all-gather.19.cloned.1.call-update) | async-done | bytes 6553616 | tf_op jit(solution)/shard_map/all_gather | solution.py:157
  462.9 17.7 fusion.63
  481.6 39.6 %psum.50 = f32[41]{0:T(128)S(1)} all-reduce(f32[41]{0:T(128)S(1)} %select_reduce_fusion.3), channel_id=1, replica_groups=mesh['dp'=16,'mp'=2] {'dp','mp'}, use_global_device_ids=true, to_apply=%region_11.12 | all-reduce | flops 41 | bytes 328 | tf_op jit(solution)/shard_map/psum | solution.py:150
  521.4 39.3 %reduce-scatter.10.cloned.1.call-done = f32[640,1280]{1,0:T(8,128)} async-done(((f32[1280,1280]{1,0:T(8,128)}), f32[640,1280]{1,0:T(8,128)}) %reduce-scatter.10.cloned.1.call-update) | async-done | bytes 3276816 | tf_op jit(solution)/shard_map/reduce_scatter | solution.py:54
  572.7 46.3 %all-gather.21.cloned.1.call-done = bf16[1280,1280]{1,0:T(8,128)(2,1)} async-done(((bf16[640,1280]{1,0:T(8,128)(2,1)}), bf16[1280,1280]{1,0:T(8,128)(2,1)}) %all-gather.21.cloned.1.call-update) | async-done | bytes 3276816 | tf_op jit(solution)/shard_map/all_gather | solution.py:58
  619.0 30.2 %fusion.8 = bf16[1280,2560]{1,0:T(8,128)(2,1)S(1)} fusion(f32[1280,2560]{1,0:T(8,128)} %fusion.79, bf16[1280,1280]{1,0:T(8,128)(2,1)} %all-gather.21.cloned.1.call-done, bf16[2560,1280]{1,0:T(8,128)(2,1)} %all-gather.19.cloned.1.call-done), kind=kOutput, calls=%fused_computation.15 | convolution fusion | flops 8454144000 | bytes 29491200 | tf_op jit(solution)/shard_map/ti,ji->tj/dot_general | solution.py:40
  665.0 44.9 %reduce-scatter.12.cloned.1.call-done = bf16[640,1280]{1,0:T(8,128)(2,1)} async-done(((bf16[1280,1280]{1,0:T(8,128)(2,1)}), bf16[640,1280]{1,0:T(8,128)(2,1)}) %reduce-scatter.12.cloned.1.call-update) | async-done | bytes 1638416 | tf_op jit(solution)/shard_map/reduce_scatter | solution.py:62
  717.3 46.5 %all-gather.23.cloned.1.call-done = bf16[1280,1280]{1,0:T(8,128)(2,1)} async-done(((bf16[640,1280]{1,0:T(8,128)(2,1)}), bf16[1280,1280]{1,0:T(8,128)(2,1)}) %all-gather.23.cloned.1.call-update) | async-done | bytes 3276816 | tf_op jit(solution)/shard_map/all_gather | solution.py:58
  775.1 48.0 %multiply_reduce_fusion = (f32[10,1280]{1,0:T(8,128)S(1)}, f32[10,1280,1280]{1,2,0:T(8,128)}) fusion(f32[10,1280,1280]{1,2,0:T(8,128)} %get-tuple-element.197, f32[10,1280]{1,0:T(8,128)S(1)} %log_add_fusion, bf16[1280,10,64]{0,2,1:T(8,128)(2,1)S(1)} %bitcast.201, bf16[1280,10,64]{0,2,1:T(8,128)(2,1)S(1)} %bitcast.198), kind=kOutput, calls=%fused_computation.3 | convolution fusion | flops 2146291200 | bytes 134451200 | tf_op jit(solution)/shard_map/ihd,jhd->hij/dot_general | solution.py:97
  823.1 52.3 %multiply_convert_fusion = bf16[10,1280,1280]{1,2,0:T(8,128)(2,1)} fusion(f32[10,1280,1280]{1,2,0:T(8,128)} %get-tuple-element.200, f32[10,1280,1280]{1,2,0:T(8,128)} %get-tuple-element.197, f32[10,1280]{1,0:T(8,128)S(1)} %get-tuple-element.199, f32[10,1280]{1,0:T(8,128)S(1)} %log_add_fusion), kind=kLoop, calls=%fused_computation.2 | loop fusion | flops 65536000 | bytes 163942400 | tf_op jit(solution)/shard_map/convert_element_type | solution.py:101
  875.4 18.2 %fusion.30 = bf16[10,64,1280]{2,1,0:T(8,128)(2,1)} fusion(bf16[1280,10,64]{0,2,1:T(8,128)(2,1)} %bitcast.204, bf16[10,1280,1280]{1,2,0:T(8,128)(2,1)} %multiply_convert_fusion), kind=kOutput, calls=%fused_computation.61 | convolution fusion | flops 2098790400 | bytes 36044800 | tf_op jit(solution)/shard_map/hij,ihd->jhd/dot_general | solution.py:107
  893.7 17.2 fusion.29
  910.9 23.5 %fusion.34 = bf16[10,64,1280]{2,1,0:T(8,128)(2,1)} fusion(bf16[1280,10,64]{0,2,1:T(8,128)(2,1)S(1)} %bitcast.202, f32[10,1280,1280]{1,2,0:T(8,128)} %get-tuple-element.197, f32[10,1280]{1,0:T(8,128)S(1)} %log_add_fusion), kind=kOutput, calls=%fused_computation.63 | convolution fusion | flops 2130739200 | bytes 68864000 | tf_op jit(solution)/shard_map/hij,ihd->jhd/dot_general | solution.py:98
  946.0 14.7 copy.99
  975.3 13.7 fusion.81
  990.9 16.4 fusion.62
  1021.2 181.2 %all-reduce.11.cloned.1.call-done = f32[3,1280,640]{2,0,1:T(4,128)} async-done(((f32[3,1280,640]{2,0,1:T(4,128)}), f32[3,1280,640]{2,0,1:T(4,128)}) %all-reduce.11.cloned.1.call-update) | async-done | bytes 9830416
  1206.0 43.1 %reduce-scatter.20.cloned.1.call-done = bf16[640,1280]{1,0:T(8,128)(2,1)} async-done(((bf16[1280,1280]{1,0:T(8,128)(2,1)}), bf16[640,1280]{1,0:T(8,128)(2,1)}) %reduce-scatter.20.cloned.1.call-update) | async-done | bytes 1638416 | tf_op jit(solution)/shard_map/reduce_scatter | solution.py:62
  1251.4 140.6 %reduce-scatter.16.cloned.1.call-done = f32[80,2560]{1,0:T(8,128)} async-done(((f32[1280,2560]{1,0:T(8,128)}), f32[80,2560]{1,0:T(8,128)}) %reduce-scatter.16.cloned.1.call-update) | async-done | bytes 819216 | tf_op jit(solution)/shard_map/reduce_scatter | solution.py:220
  1394.6 138.9 %reduce-scatter.18.cloned.1.call-done = f32[160,1280]{1,0:T(8,128)} async-done(((f32[2560,1280]{1,0:T(8,128)}), f32[160,1280]{1,0:T(8,128)}) %reduce-scatter.18.cloned.1.call-update) | async-done | bytes 819216 | tf_op jit(solution)/shard_map/reduce_scatter | solution.py:221
  1536.1 130.9 %all-reduce.9.cloned.1.call-done = f32[142,1280]{1,0:T(8,128)} async-done(((f32[142,1280]{1,0:T(8,128)}), f32[142,1280]{1,0:T(8,128)}) %all-reduce.9.cloned.1.call-update) | async-done | bytes 727056 | tf_op jit(solution)/shard_map/psum | solution.py:226
  1668.9 41.4 %all-reduce.5 = (f32[]{:T(128)}, f32[6,1280]{1,0:T(8,128)S(1)}) all-reduce(f32[]{:T(128)S(6)} %add.265, f32[6,1280]{1,0:T(8,128)S(1)} %stack.123), channel_id=1, replica_groups=mesh['dp'=16,'mp'=2] {'dp','mp'}, use_global_device_ids=true, to_apply=%region_42.43 | all-reduce | flops 7681 | bytes 61448 | tf_op jit(solution)/shard_map/psum | solution.py:233
  1740.4 39.9 %all-reduce.4 = (f32[4]{0:T(128)S(1)}, f32[4]{0:T(128)S(1)}, f32[]{:T(128)}) all-reduce(f32[4]{0:T(128)S(1)} %pad_maximum_fusion.10, f32[4]{0:T(128)S(1)} %pad_maximum_fusion.11, f32[]{:T(128)S(6)} %add.298), channel_id=1, replica_groups=mesh['dp'=16,'mp'=2] {'dp','mp'}, use_global_device_ids=true, to_apply=%region_4.0 | all-reduce | flops 9 | bytes 72 | tf_op jit(solution)/shard_map/psum | solution.py:248
  (292 shorter events, 174.3 us)
Async XLA Ops:
  7.2 55.8 %all-gather.9.cloned.1.call-start = ((), (), s32[]{:S(2)}) async-start(), calls=%async_computation.7 | async-start | bytes 4915200 | tf_op jit(solution)/shard_map/all_gather | solution.py:48
  13.8 106.5 %all-gather.11.cloned.1.call-start = ((), (), s32[]{:S(2)}) async-start(), calls=%async_computation.8 | async-start | bytes 5222400 | tf_op jit(solution)/shard_map/all_gather | solution.py:154
  15.3 182.1 %all-gather.13.cloned.1.call-start = ((), (), s32[]{:S(2)}) async-start(), calls=%async_computation.9 | async-start | bytes 1740800 | tf_op jit(solution)/shard_map/all_gather | solution.py:155
  16.0 266.9 %reduce-scatter.8.cloned.1.call-start = ((), (), s32[]{:S(2)}) async-start(), calls=%async_computation.10 | async-start | bytes 9830400 | tf_op jit(solution)/shard_map/reduce_scatter | solution.py:54
  130.5 23.3 %copy-start.11 = (bf16[1,1280,640]{1,2,0:T(8,128)(2,1)}, bf16[1,1280,640]{1,2,0:T(8,128)(2,1)S(1)}, u32[]{:S(2)}) copy-start(bf16[1,1280,640]{1,2,0:T(8,128)(2,1)S(1)} %get-tuple-element.153) | copy-start | bytes 4915204
  130.5 23.3 %copy-start.16 = (bf16[1,1280,640]{1,2,0:T(8,128)(2,1)}, bf16[1,1280,640]{1,2,0:T(8,128)(2,1)S(1)}, u32[]{:S(2)}) copy-start(bf16[1,1280,640]{1,2,0:T(8,128)(2,1)S(1)} %get-tuple-element.155) | copy-start | bytes 4915204
  130.6 44.3 %copy-start.4 = (bf16[1,1280,640]{1,2,0:T(8,128)(2,1)}, bf16[1,1280,640]{1,2,0:T(8,128)(2,1)S(1)}, u32[]{:S(2)}) copy-start(bf16[1,1280,640]{1,2,0:T(8,128)(2,1)S(1)} %get-tuple-element.154) | copy-start | bytes 4915204
  204.1 145.2 %all-gather.17.cloned.1.call-start = ((), (), s32[]{:S(2)}) async-start(), calls=%async_computation.12 | async-start | bytes 6963200 | tf_op jit(solution)/shard_map/all_gather | solution.py:156
  206.1 190.3 %all-gather.15.cloned.1.call-start = ((), (), s32[]{:S(2)}) async-start(), calls=%async_computation.11 | async-start | bytes 4915200 | tf_op jit(solution)/shard_map/all_gather | solution.py:48
  288.0 174.9 %all-gather.19.cloned.1.call-start = ((), (), s32[]{:S(2)}) async-start(), calls=%async_computation.13 | async-start | bytes 6963200 | tf_op jit(solution)/shard_map/all_gather | solution.py:157
  290.1 270.6 %reduce-scatter.10.cloned.1.call-start = ((), (), s32[]{:S(2)}) async-start(), calls=%async_computation.14 | async-start | bytes 9830400 | tf_op jit(solution)/shard_map/reduce_scatter | solution.py:54
  480.7 138.4 %all-gather.21.cloned.1.call-start = ((), (), s32[]{:S(2)}) async-start(), calls=%async_computation.15 | async-start | bytes 4915200 | tf_op jit(solution)/shard_map/all_gather | solution.py:58
  572.7 137.2 %reduce-scatter.12.cloned.1.call-start = ((), (), s32[]{:S(2)}) async-start(), calls=%async_computation.16 | async-start | bytes 4915200 | tf_op jit(solution)/shard_map/reduce_scatter | solution.py:62
  664.9 98.9 %all-gather.23.cloned.1.call-start = ((), (), s32[]{:S(2)}) async-start(), calls=%async_computation.17 | async-start | bytes 4915200 | tf_op jit(solution)/shard_map/all_gather | solution.py:58
  717.2 302.4 %reduce-scatter.14.cloned.1.call-start = ((), (), s32[]{:S(2)}) async-start(), calls=%async_computation.18 | async-start | bytes 3481600 | tf_op jit(solution)/shard_map/reduce_scatter | solution.py:219
  770.2 432.2 %all-reduce.11.cloned.1.call-start = ((), (), s32[]{:S(2)}) async-start(), calls=%async_computation.23 | async-start | bytes 26214400
  875.4 18.2 %copy-start.12 = (bf16[1,1280,640]{1,2,0:T(8,128)(2,1)S(1)}, bf16[1,1280,640]{1,2,0:T(8,128)(2,1)}, u32[]{:S(2)}) copy-start(bf16[1,1280,640]{1,2,0:T(8,128)(2,1)} %copy-done.11) | copy-start | bytes 4915204
  910.9 23.5 %copy-start.30 = (bf16[10,64,1280]{2,1,0:T(8,128)(2,1)S(1)}, bf16[10,64,1280]{2,1,0:T(8,128)(2,1)}, u32[]{:S(2)}) copy-start(bf16[10,64,1280]{2,1,0:T(8,128)(2,1)} %fusion.29) | copy-start | bytes 4915204
  960.7 288.3 %reduce-scatter.20.cloned.1.call-start = ((), (), s32[]{:S(2)}) async-start(), calls=%async_computation.22 | async-start | bytes 4915200 | tf_op jit(solution)/shard_map/reduce_scatter | solution.py:62
  973.3 418.7 %reduce-scatter.16.cloned.1.call-start = ((), (), s32[]{:S(2)}) async-start(), calls=%async_computation.19 | async-start | bytes 13926400 | tf_op jit(solution)/shard_map/reduce_scatter | solution.py:220
  989.0 544.5 %reduce-scatter.18.cloned.1.call-start = ((), (), s32[]{:S(2)}) async-start(), calls=%async_computation.20 | async-start | bytes 13926400 | tf_op jit(solution)/shard_map/reduce_scatter | solution.py:221
  1007.4 9.8 copy-start.7
  1007.4 9.8 copy-start.40
  1007.4 9.8 copy-start.46
  1007.4 659.6 %all-reduce.9.cloned.1.call-start = ((), (), s32[]{:S(2)}) async-start(), calls=%async_computation.21 | async-start | bytes 1474560 | tf_op jit(solution)/shard_map/psum | solution.py:226
  1010.7 8.9 copy-start.54
  1010.7 238.3 %copy-start.1 = (bf16[640,1280]{1,0:T(8,128)(2,1)S(1)}, bf16[640,1280]{1,0:T(8,128)(2,1)}, u32[]{:S(2)}) copy-start(bf16[640,1280]{1,0:T(8,128)(2,1)} %param.20) | copy-start | bytes 4915204
  1010.7 238.3 %copy-start.48 = (f32[640]{0:T(1024)S(1)}, f32[640]{0:T(1024)}, u32[]{:S(2)}) copy-start(f32[640]{0:T(1024)} %copy-done.47) | copy-start | bytes 7684
  1010.8 238.3 %copy-start.51 = (f32[640]{0:T(1024)S(1)}, f32[640]{0:T(1024)}, u32[]{:S(2)}) copy-start(f32[640]{0:T(1024)} %copy-done.50) | copy-start | bytes 7684
  1021.2 691.7 %copy-start.44 = (f32[6,1280]{1,0:T(8,128)S(1)}, f32[6,1280]{1,0:T(8,128)}, u32[]{:S(2)}) copy-start(f32[6,1280]{1,0:T(8,128)} %param.38) | copy-start | bytes 92164
  1204.5 509.7 %copy-start.10 = (f32[142,1280]{1,0:T(8,128)S(1)}, f32[142,1280]{1,0:T(8,128)}, u32[]{:S(2)}) copy-start(f32[142,1280]{1,0:T(8,128)} %param.36) | copy-start | bytes 2181124
  1204.5 509.7 %copy-start.27 = (f32[1,142,1280]{2,0,1:T(1,128)S(1)}, f32[1,142,1280]{2,0,1:T(1,128)}, u32[]{:S(2)}) copy-start(f32[1,142,1280]{2,0,1:T(1,128)} %get-tuple-element.166) | copy-start | bytes 2181124
  (52 other events, 181.7 us)
Sparse Core Ops, SparseCore 0:
  13.9 49.0 all-gather.8
  65.8 54.4 all-gather.10
  123.0 38.4 all-gather.12
  204.3 78.6 reduce-scatter.7
  285.9 63.3 all-gather.16
  351.4 44.9 all-gather.14
  399.5 63.3 all-gather.18
  480.8 79.8 reduce-scatter.9
  572.8 46.2 all-gather.20
  665.0 44.7 reduce-scatter.11
  717.3 46.4 all-gather.22
  770.3 66.8 reduce-scatter.13
  960.8 241.4 all-reduce.10
  1204.5 44.5 reduce-scatter.19
  1253.6 138.3 reduce-scatter.15
  1395.9 137.4 reduce-scatter.17
  1540.0 126.9 all-reduce.8
where the time goes:
time: 1820 us; the launch traced here: 1810 us
  waiting for transfers between devices  1150 us (63%)
  matrix products  314 us (17%)
  other arithmetic  153 us (8%)
  blocking collectives  121 us (7%)
  local copies, waits for them, and re-layouts  40.3 us (2%)
  between operations  31.3 us (2%)
    unnamed x18, waiting for transfers between devices  181 us
    reduce_scatter x1, waiting for transfers between devices, per_device(): lax.psum_scatter(d_up, 'dp', scatter_dimension=0, tiled=True)  141 us
    reduce_scatter x1, waiting for transfers between devices, per_device(): lax.psum_scatter(d_down, 'dp', scatter_dimension=0, tiled=True)  139 us
    psum x1, waiting for transfers between devices, per_device(): red_head, red_norms = lax.psum((d_head, d_norms), ('dp', 'mp'))  131 us
    reduce_scatter x2, waiting for transfers between devices, branch_out(): return lax.psum_scatter(summand, 'mp', scatter_dimension=0, tiled=True)  116 us
    all_gather x2, waiting for transfers between devices, gather_grad(): return lax.all_gather(rows.astype(jnp.bfloat16), 'mp', axis=0, tiled=True)  92.9 us
    all_gather x2, waiting for transfers between devices, gather_normed(): lax.all_gather(layer_norm(rows, gain, shift).astype(jnp.bfloat16), 'mp',...  92 us
    reduce_scatter x2, waiting for transfers between devices, scatter_grad(): lax.psum_scatter(summand.astype(jnp.bfloat16), 'mp', scatter_dimension=0,...  88 us
  transfers between devices with their start and end apart: 17, of which 15 were waited for; matrix products, arithmetic and copies ran while one was open for 20% of the time, Pallas kernels for 0%

commit v1 on v0

v1 whole, which is shorter than its diff:
```python
import functools

import jax
import jax.numpy as jnp
import numpy as np
from jax import lax
from jax.experimental import pallas as pl
from jax.experimental.pallas import tpu as pltpu
from jax.sharding import PartitionSpec as P

HD = 64
RB = 120
AB = 18
WB = 4
GAMES = 41
LEN = 160


clip_limit = 0.05
learn_rate = 0.5
beta_first = 0.5
beta_second = 0.5
weight_decay = 0.01
adam_eps = 1e-08
norm_eps = 1e-05
masked_score = -1e30


def layer_norm(rows, gain, shift):
    centred = rows - jnp.mean(rows, -1, keepdims=True)
    spread = jnp.mean(centred * centred, -1, keepdims=True)
    return centred * lax.rsqrt(spread + norm_eps) * gain + shift


def norm_back(rows, gain, shift, upstream):
    _, pullback = jax.vjp(layer_norm, rows, gain, shift)
    return pullback(upstream)


def matmul(left, right):
    return jnp.dot(left, right, preferred_element_type=jnp.float32)


def matmul_t(left, right):
    return jnp.einsum("ti,ji->tj", left, right, preferred_element_type=jnp.float32)


def contract(left, right):
    return jnp.einsum("ti,tj->ij", left, right, preferred_element_type=jnp.float32)


def part_loss(logits, targets, flags, token_scale):
    summed = jnp.zeros((), jnp.float32)
    offset = 0
    for column, span_cols in enumerate((RB, AB, WB)):
        section = logits[:, offset : offset + span_cols]
        log_probs = jax.nn.log_softmax(section, axis=-1)
        picked = (targets[column][:, None] == jnp.arange(span_cols)[None, :]).astype(jnp.float32)
        cross = -jnp.sum(log_probs * picked, -1)
        summed = summed + jnp.sum(flags[:, column].astype(jnp.float32) * token_scale * cross)
        offset = offset + span_cols
    return summed


AXES = ("dp", "mp")
VMEM_LIMIT = 60 * 2**20
ANY = pl.BlockSpec(memory_space=pl.ANY)


class Plan:
    def __init__(self, dp, mp):
        self.dp, self.mp = dp, mp
        self.core = 2 if dp % 2 == 0 else 1
        self.y = 2 if dp % (2 * self.core) == 0 else 1
        self.z = dp // (self.core * self.y)
        self.n = dp * mp
        self.grid = np.arange(self.n).reshape(self.z, self.y, self.core, mp)
        self.place = [tuple(int(v) for v in np.argwhere(self.grid == i)[0]) for i in range(self.n)]

    def pairs(self, move):
        found = []
        for i, spot in enumerate(self.place):
            target = move(*spot)
            if target is not None and 0 <= target[0] < self.z:
                found.append((i, int(self.grid[target])))
        return found

    def flip_core(self):
        return self.pairs(lambda z, y, c, x: (z, y, 1 - c, x))

    def flip_first(self):
        return self.pairs(lambda z, y, c, x: (z, 1 - y, c, x) if c == 0 else (z, y, c, 1 - x))

    def flip_second(self):
        return self.pairs(lambda z, y, c, x: (z, y, c, 1 - x) if c == 0 else (z, 1 - y, c, x))

    def flip_z(self, bits):
        return self.pairs(lambda z, y, c, x: (z ^ bits, y, c, x))

    def z_moves(self):
        return [self.flip_z(bits) for bits in range(1, self.z)]


def moved(table, pairs):
    got = np.full_like(table, -1)
    for source, target in pairs:
        got[target] = table[source]
    return got


def send(value, pairs):
    return lax.ppermute(value, AXES, pairs)


def add_all(parts, dtype=jnp.bfloat16):
    total = parts[0].astype(jnp.float32)
    for part in parts[1:]:
        total = total + part.astype(jnp.float32)
    return total.astype(dtype)


class Travel:
    def __init__(self, name, steps, quiet=False):
        self.name, self.steps, self.quiet = name, steps, quiet
        self.result, self.going = None, None
        self.wanted = next(steps)


class Clock:
    def __init__(self):
        self.gates = []

    def hold(self, values):
        flat, tree = jax.tree.flatten(values)
        passed = lax.optimization_barrier(tuple(flat) + tuple(self.gates))
        return jax.tree.unflatten(tree, passed[: len(flat)])

    def start(self, travels, more=()):
        values, more = self.hold(([[v for v, _ in travel.wanted] for travel in travels], more))
        self.gates = []
        for travel, ready in zip(travels, values):
            with jax.named_scope(travel.name):
                travel.going = [send(v, pairs) for v, (_, pairs) in zip(ready, travel.wanted)]
        return more

    def wait(self, travels):
        for travel in travels:
            if not travel.quiet:
                self.gates = self.gates + travel.going
            try:
                travel.wanted = travel.steps.send(travel.going)
            except StopIteration as end:
                travel.wanted, travel.result = None, end.value
            travel.going = None

    def also(self, *values):
        self.gates = self.gates + list(values)


def path_table(plan):
    first, second, core = plan.flip_first(), plan.flip_second(), plan.flip_core()
    own = np.arange(plan.n)[:, None]
    line = np.concatenate([own] + [moved(own, pairs) for pairs in plan.z_moves()], 1)
    near, side = moved(line, first), moved(line, second)
    table = np.concatenate([line, near, side, moved(near, second)], 1)
    return np.concatenate([table, moved(table, core)], 1)


def gather_shards(plan, shard):
    first, second, core = plan.flip_first(), plan.flip_second(), plan.flip_core()
    got = yield [(shard[None], pairs) for pairs in plan.z_moves()]
    line = jnp.concatenate([shard[None]] + got)
    near, side = yield [(line, first), (line, second)]
    far, line_twin, near_twin = yield [(near, second), (line, core), (near, core)]
    side_twin, far_twin = yield [(side, core), (far, core)]
    return [line, near, side, far, line_twin, near_twin, side_twin, far_twin]


def scatter_counts(plan):
    return [4 * plan.z, 3 * plan.z, plan.z]


def scatter_shards(plan, pieces):
    first, second, core = plan.flip_first(), plan.flip_second(), plan.flip_core()
    own, rest_twin, far_twin = pieces
    size = plan.z

    def quarter(value, k):
        return value[k * size : (k + 1) * size]

    far_got, rest_got = yield [(far_twin, core), (rest_twin, core)]
    (far_got,) = yield [(add_all([quarter(own, 3), far_got]), second)]
    near = add_all([quarter(own, 1), quarter(rest_got, 1), far_got])
    side = add_all([quarter(own, 2), quarter(rest_got, 2)])
    near_got, side_got = yield [(near, first), (side, second)]
    terms = [quarter(own, 0), quarter(rest_got, 0), near_got, side_got]
    got = yield [
        (add_all([term[k + 1 : k + 2] for term in terms]), pairs)
        for k, pairs in enumerate(plan.z_moves())
    ]
    return add_all([term[:1] for term in terms] + got, jnp.float32)[0]


def total_steps(plan, value, halves=False):
    if halves:
        half = value.shape[0] // 2
        upper = lax.axis_index("dp") % 2 == 1
        keep = jnp.where(upper, value[half:], value[:half])
        (got,) = yield [(jnp.where(upper, value[:half], value[half:]), plan.flip_core())]
        value = keep + got
    else:
        (got,) = yield [(value, plan.flip_core())]
        value = value + got
    moves = [
        plan.pairs(lambda z, y, c, x: (z, y, c, 1 - x)),
        plan.pairs(lambda z, y, c, x: (z, 1 - y, c, x)),
    ]
    bit = 1
    while bit < plan.z:
        moves.append(plan.flip_z(bit))
        bit *= 2
    for pairs in moves:
        (got,) = yield [(value, pairs)]
        value = value + got
    if halves:
        (got,) = yield [(value, plan.flip_core())]
        return jnp.where(upper, jnp.concatenate([got, value]), jnp.concatenate([value, got]))
    return value


def total_over_devices(plan, value):
    travel, clock = Travel("small_sum", total_steps(plan, value)), Clock()
    while travel.wanted:
        clock.start([travel])
        clock.wait([travel])
    return travel.result


def slot_counts(pieces):
    counts = [piece.shape[0] for piece in pieces]
    return counts, [sum(counts[:i]) for i in range(len(counts))]


def spot_of(device, plan, split_columns):
    if split_columns:
        return device // plan.mp, device % plan.mp
    return (device % plan.mp) * plan.dp + device // plan.mp, 0


def assemble(plan, pieces, slots, split_columns):
    counts, offsets = slot_counts(pieces)
    total = sum(counts)
    rows, width = pieces[0].shape[1:]
    groups = plan.mp if split_columns else 1
    blocks = total // groups
    if rows % 16 and groups > 1 or width % 128:
        stacked = jnp.concatenate(pieces)
        stacked = lax.fori_loop(
            0,
            total,
            lambda i, held: lax.dynamic_update_index_in_dim(held, stacked[i], slots[i], 0),
            stacked,
        ).reshape(plan.dp, plan.mp, rows, width)
        if split_columns:
            return stacked.transpose(0, 2, 1, 3).reshape(plan.dp * rows, plan.mp * width)
        return stacked.transpose(1, 0, 2, 3).reshape(total * rows, width)
    depth = 8

    def kernel(slots_ref, *refs):
        sources, out = refs[: len(pieces)], refs[len(pieces)]
        held, in_sems, out_sems = refs[len(pieces) + 1 :]
        steps = [(a, s) for a in range(len(pieces)) for s in range(counts[a])]
        reads, writes = [], []
        for i, (a, s) in enumerate(steps):
            block, group = spot_of(slots_ref[i], plan, split_columns)
            columns = pl.ds(pl.multiple_of(group * width, 128), width)
            reads.append(pltpu.make_async_copy(sources[a].at[s], held.at[i], in_sems.at[i]))
            writes.append(
                pltpu.make_async_copy(held.at[i], out.at[block, :, columns], out_sems.at[i])
            )
        for i in range(total):
            reads[i].start()
        for i in range(total):
            reads[i].wait()
            writes[i].start()
        for i in range(total):
            writes[i].wait()

    whole = pl.pallas_call(
        kernel,
        out_shape=jax.ShapeDtypeStruct((blocks, rows, groups * width), pieces[0].dtype),
        grid_spec=pltpu.PrefetchScalarGridSpec(
            num_scalar_prefetch=1,
            grid=(1,),
            in_specs=[ANY] * len(pieces),
            out_specs=ANY,
            scratch_shapes=[
                pltpu.VMEM((total, rows, width), pieces[0].dtype),
                pltpu.SemaphoreType.DMA((total,)),
                pltpu.SemaphoreType.DMA((total,)),
            ],
        ),
        compiler_params=pltpu.CompilerParams(vmem_limit_bytes=VMEM_LIMIT),
        cost_estimate=pl.CostEstimate(
            flops=0, bytes_accessed=4 * total * rows * width, transcendentals=0
        ),
    )(slots, *pieces)
    return whole.reshape(blocks * rows, groups * width)


def disassemble(plan, whole, shard_shape, counts, slots, split_columns):
    total = sum(counts)
    rows, width = shard_shape
    groups = plan.mp if split_columns else 1
    offsets = [sum(counts[:i]) for i in range(len(counts))]
    if rows % 16 and groups > 1 or width % 128:
        if split_columns:
            shards = whole.reshape(plan.dp, rows, plan.mp, width).transpose(0, 2, 1, 3)
        else:
            shards = whole.reshape(plan.mp, plan.dp, rows, width).transpose(1, 0, 2, 3)
        source = shards.reshape(total, rows, width)
        shards = lax.fori_loop(
            0,
            total,
            lambda i, held: lax.dynamic_update_index_in_dim(held, source[slots[i]], i, 0),
            source,
        )
        return [shards[o : o + c] for o, c in zip(offsets, counts)]
    blocks = total // groups

    def kernel(slots_ref, source, *refs):
        outs = refs[: len(counts)]
        held, in_sems, out_sems = refs[len(counts) :]
        steps = [(a, s) for a in range(len(counts)) for s in range(counts[a])]
        reads, writes = [], []
        for i, (a, s) in enumerate(steps):
            block, group = spot_of(slots_ref[i], plan, split_columns)
            columns = pl.ds(pl.multiple_of(group * width, 128), width)
            reads.append(
                pltpu.make_async_copy(source.at[block, :, columns], held.at[i], in_sems.at[i])
            )
            writes.append(pltpu.make_async_copy(held.at[i], outs[a].at[s], out_sems.at[i]))
        for i in range(total):
            reads[i].start()
        for i in range(total):
            reads[i].wait()
            writes[i].start()
        for i in range(total):
            writes[i].wait()

    return pl.pallas_call(
        kernel,
        out_shape=[jax.ShapeDtypeStruct((c, rows, width), whole.dtype) for c in counts],
        grid_spec=pltpu.PrefetchScalarGridSpec(
            num_scalar_prefetch=1,
            grid=(1,),
            in_specs=[ANY],
            out_specs=[ANY] * len(counts),
            scratch_shapes=[
                pltpu.VMEM((total, rows, width), whole.dtype),
                pltpu.SemaphoreType.DMA((total,)),
                pltpu.SemaphoreType.DMA((total,)),
            ],
        ),
        compiler_params=pltpu.CompilerParams(vmem_limit_bytes=VMEM_LIMIT),
        cost_estimate=pl.CostEstimate(
            flops=0, bytes_accessed=4 * total * rows * width, transcendentals=0
        ),
    )(slots, whole.reshape(blocks, rows, groups * width))


PAIR = 2 * HD


def pair_blocks(ref, offset, group, pair, pairs):
    start = group * 3 * pairs * PAIR + pair * PAIR
    span = pairs * PAIR
    return [ref[:, start + part * span : start + part * span + PAIR] for part in range(3)]


def both_heads(block):
    low_lane = lax.broadcasted_iota(jnp.int32, block.shape, 1) < HD
    zero = jnp.zeros_like(block)
    return jnp.concatenate([jnp.where(low_lane, block, zero), jnp.where(low_lane, zero, block)])


def own_columns(stacked):
    rows = stacked.shape[0] // 2
    low_lane = lax.broadcasted_iota(jnp.int32, (rows, PAIR), 1) < HD
    return jnp.where(low_lane, stacked[:rows], stacked[rows:])


def rows_by_rows(left, right):
    return lax.dot_general(left, right, (((1,), (1,)), ((), ())), preferred_element_type=jnp.float32)


def rows_of_both(left, right):
    return lax.dot_general(left, right, (((0,), (0,)), ((), ())), preferred_element_type=jnp.float32)


def pair_probs(stacked_queries, keys, allowed):
    scores = rows_by_rows(stacked_queries, keys) * HD ** (-0.5)
    scores = jnp.where(allowed, scores, masked_score)
    raised = jnp.exp(scores - jnp.max(scores, -1, keepdims=True))
    return raised * (1.0 / jnp.sum(raised, -1, keepdims=True))


def allowed_pairs(column_ref, row_ref):
    same = column_ref[0] == row_ref[0]
    shape = same.shape
    causal = lax.broadcasted_iota(jnp.int32, shape, 1) <= lax.broadcasted_iota(jnp.int32, shape, 0)
    one = (same & causal).astype(jnp.float32)
    return jnp.concatenate([one, one]) > 0.5


def attend_kernel(groups, pairs, column_ref, row_ref, qkv_ref, context_ref):
    allowed = allowed_pairs(column_ref, row_ref)
    for group in range(groups):
        for pair in range(pairs):
            queries, keys, values = pair_blocks(qkv_ref, 0, group, pair, pairs)
            probs = pair_probs(both_heads(queries), keys, allowed).astype(jnp.bfloat16)
            context = own_columns(matmul(probs, values))
            start = (group * pairs + pair) * PAIR
            context_ref[:, start : start + PAIR] = context.astype(jnp.bfloat16)


def attend_back_kernel(groups, pairs, column_ref, row_ref, qkv_ref, d_context_ref, d_qkv_ref):
    allowed = allowed_pairs(column_ref, row_ref)
    span = pairs * PAIR
    for group in range(groups):
        for pair in range(pairs):
            queries, keys, values = pair_blocks(qkv_ref, 0, group, pair, pairs)
            start = (group * pairs + pair) * PAIR
            d_context = both_heads(d_context_ref[:, start : start + PAIR])
            queries = both_heads(queries)
            probs = pair_probs(queries, keys, allowed)
            d_probs = rows_by_rows(d_context, values)
            d_values = rows_of_both(probs.astype(jnp.bfloat16), d_context)
            mean = jnp.sum(probs * d_probs, -1, keepdims=True)
            d_scores = (probs * (d_probs - mean)).astype(jnp.bfloat16)
            d_queries = own_columns(matmul(d_scores, keys)) * HD ** (-0.5)
            d_keys = rows_of_both(d_scores, queries) * HD ** (-0.5)
            start = group * 3 * span + pair * PAIR
            for part, value in enumerate((d_queries, d_keys, d_values)):
                at = start + part * span
                d_qkv_ref[:, at : at + PAIR] = value.astype(jnp.bfloat16)


def attend_call(kernel, segments, qkv, others, out_columns, groups, scale):
    count = segments.shape[0]
    columns = qkv.shape[1]
    pairs = columns // (3 * groups * PAIR)
    rows = lambda wide: pl.BlockSpec((LEN, wide), lambda i: (i, 0))
    return pl.pallas_call(
        functools.partial(kernel, groups, pairs),
        out_shape=jax.ShapeDtypeStruct((qkv.shape[0], out_columns), jnp.bfloat16),
        grid=(count,),
        in_specs=[
            pl.BlockSpec((1, LEN, 1), lambda i: (i, 0, 0)),
            pl.BlockSpec((1, 1, LEN), lambda i: (i, 0, 0)),
            rows(columns),
        ]
        + [rows(other.shape[1]) for other in others],
        out_specs=rows(out_columns),
        compiler_params=pltpu.CompilerParams(vmem_limit_bytes=VMEM_LIMIT),
        cost_estimate=pl.CostEstimate(
            flops=scale * count * 2 * LEN * LEN * columns // 3,
            bytes_accessed=scale * qkv.size * 2,
            transcendentals=count * LEN * LEN * columns // (3 * HD),
        ),
    )(segments[:, :, None], segments[:, None, :], qkv, *others)


class Spread:
    def __init__(self, plan, parts, split_columns):
        self.plan, self.parts, self.split_columns = plan, parts, split_columns
        self.pieces = [piece for pieces, _ in parts for piece in pieces]
        self.slots = jnp.concatenate([slots for _, slots in parts])
        self.rows = self.pieces[0].shape[1]
        widths = [pieces[0].shape[2] for pieces, _ in parts]
        self.offsets = [sum(widths[:k]) for k in range(len(widths))]
        self.stride = sum(widths)
        groups = plan.mp if split_columns else 1
        self.shape = (plan.n // groups * self.rows, groups * self.stride)
        self.aligned = self.rows % 16 == 0 and all(width % 128 == 0 for width in widths)

    def matrix(self):
        groups = self.plan.mp if self.split_columns else 1
        wholes = [
            assemble(self.plan, pieces, slots, self.split_columns).reshape(
                self.shape[0], groups, -1
            )
            for pieces, slots in self.parts
        ]
        return jnp.concatenate(wholes, 2).reshape(self.shape)

    def places(self):
        found, first = [], 0
        for (pieces, _), offset in zip(self.parts, self.offsets):
            for k, piece in enumerate(pieces):
                found = found + [(first + k, slot, offset) for slot in range(piece.shape[0])]
            first = first + len(pieces)
        return found


def spot_slice(matrix_ref, plan, device, rows, width, split_columns, offset, stride):
    block, group = spot_of(device, plan, split_columns)
    at_rows = pl.ds(pl.multiple_of(block * rows, rows), rows)
    start = offset if isinstance(group, int) else pl.multiple_of(group * stride + offset, 128)
    return matrix_ref.at[at_rows, pl.ds(start, width)]


def with_matrices(plan, body, spreads, operands, outs, steps, flops):
    sizes = [len(spread.pieces) for spread in spreads]
    total = sum(spread.slots.shape[0] for spread in spreads)

    def kernel(slots_ref, *refs):
        inputs, refs = refs[: len(operands)], refs[len(operands) :]
        sources, refs = refs[: sum(sizes)], refs[sum(sizes) :]
        results, refs = refs[: len(outs)], refs[len(outs) :]
        matrices, sems = refs[: len(spreads)], refs[len(spreads)]

        @pl.when(pl.program_id(0) == 0)
        def _():
            copies, first = [], 0
            for spread, matrix in zip(spreads, matrices):
                for which, slot, offset in spread.places():
                    i = len(copies)
                    spot = spot_slice(
                        matrix,
                        plan,
                        slots_ref[i],
                        spread.rows,
                        spread.pieces[which].shape[2],
                        spread.split_columns,
                        offset,
                        spread.stride,
                    )
                    source = sources[first + which].at[slot]
                    copies.append(pltpu.make_async_copy(source, spot, sems.at[i]))
                    copies[-1].start()
                first = first + len(spread.pieces)
            for copy in copies:
                copy.wait()

        body(inputs, matrices, results)

    moved_bytes = sum(2 * spread.shape[0] * spread.shape[1] for spread in spreads)
    moved_bytes += sum(array.size * array.dtype.itemsize for array, _, _ in operands)
    moved_bytes += sum(np.prod(shape) * np.dtype(dtype).itemsize for shape, dtype, _, _ in outs)
    return pl.pallas_call(
        kernel,
        out_shape=[jax.ShapeDtypeStruct(shape, dtype) for shape, dtype, _, _ in outs],
        grid_spec=pltpu.PrefetchScalarGridSpec(
            num_scalar_prefetch=1,
            grid=(steps,),
            in_specs=[pl.BlockSpec(block, index) for _, block, index in operands]
            + [ANY] * sum(sizes),
            out_specs=[pl.BlockSpec(block, index) for _, _, block, index in outs],
            scratch_shapes=[pltpu.VMEM(spread.shape, jnp.bfloat16) for spread in spreads]
            + [pltpu.SemaphoreType.DMA((total,))],
        ),
        compiler_params=pltpu.CompilerParams(vmem_limit_bytes=VMEM_LIMIT),
        cost_estimate=pl.CostEstimate(
            flops=flops, bytes_accessed=int(moved_bytes), transcendentals=0
        ),
    )(
        jnp.concatenate([spread.slots for spread in spreads]),
        *[array for array, _, _ in operands],
        *[piece for spread in spreads for piece in spread.pieces],
    )


def fixed(step, slots):
    return (0, 0)


def by_columns(step, slots):
    return (0, step)


def by_rows(step, slots):
    return (step, 0)


def step_slice(size):
    return pl.ds(pl.multiple_of(pl.program_id(0) * size, size), size)


def project(rows, spread, block):
    count, deep = rows.shape
    wide = spread.shape[1]
    if not spread.aligned or wide % block:
        return matmul(rows, spread.matrix()).astype(jnp.bfloat16)

    def body(inputs, matrices, results):
        product = matmul(inputs[0][...], matrices[0][:, step_slice(block)])
        results[0][...] = product.astype(jnp.bfloat16)

    return with_matrices(
        spread.plan,
        body,
        [spread],
        [(rows, (count, deep), fixed)],
        [((count, wide), jnp.bfloat16, (count, block), by_columns)],
        wide // block,
        2 * count * deep * wide,
    )[0]


def project_back(rows, spread, block):
    count, deep = rows.shape
    wide = spread.shape[0]
    if not spread.aligned or wide % block:
        return matmul_t(rows, spread.matrix())

    def body(inputs, matrices, results):
        results[0][...] = rows_by_rows(inputs[0][...], matrices[0][step_slice(block), :])

    return with_matrices(
        spread.plan,
        body,
        [spread],
        [(rows, (count, deep), fixed)],
        [((count, wide), jnp.float32, (count, block), by_columns)],
        wide // block,
        2 * count * deep * wide,
    )[0]


def hidden_forward(rows, spread, block):
    count, deep = rows.shape
    wide = spread.shape[1]
    if not spread.aligned or wide % block:
        up_pre = matmul(rows, spread.matrix())
        return up_pre, jax.nn.gelu(up_pre).astype(jnp.bfloat16)

    def body(inputs, matrices, results):
        up_pre = matmul(inputs[0][...], matrices[0][:, step_slice(block)])
        results[0][...] = up_pre
        results[1][...] = jax.nn.gelu(up_pre).astype(jnp.bfloat16)

    return with_matrices(
        spread.plan,
        body,
        [spread],
        [(rows, (count, deep), fixed)],
        [
            ((count, wide), jnp.float32, (count, block), by_columns),
            ((count, wide), jnp.bfloat16, (count, block), by_columns),
        ],
        wide // block,
        2 * count * deep * wide,
    )


def hidden_back(d_out, up_pre, spread, block):
    count, wide = up_pre.shape
    if not spread.aligned or wide % block:
        d_activated = matmul_t(d_out, spread.matrix())
        return jax.vjp(jax.nn.gelu, up_pre)[1](d_activated)[0].astype(jnp.bfloat16)

    def body(inputs, matrices, results):
        d_activated = rows_by_rows(inputs[0][...], matrices[0][step_slice(block), :])
        slope = jax.vjp(jax.nn.gelu, inputs[1][...])[1](d_activated)[0]
        results[0][...] = slope.astype(jnp.bfloat16)

    return with_matrices(
        spread.plan,
        body,
        [spread],
        [(d_out, d_out.shape, fixed), (up_pre, (count, block), by_columns)],
        [((count, wide), jnp.bfloat16, (count, block), by_columns)],
        wide // block,
        2 * count * d_out.shape[1] * wide,
    )[0]


def hidden_out(activated, base, spread, block):
    count, deep = activated.shape
    wide = base.shape[1]
    if not spread.aligned or count % block:
        return base + matmul(activated, spread.matrix())

    def body(inputs, matrices, results):
        results[0][...] = inputs[1][...] + matmul(inputs[0][...], matrices[0][...])

    return with_matrices(
        spread.plan,
        body,
        [spread],
        [(activated, (block, deep), by_rows), (base, (block, wide), by_rows)],
        [((count, wide), jnp.float32, (block, wide), by_rows)],
        count // block,
        2 * count * deep * wide,
    )[0]


def weight_grad(plan, left, right, rows, parts, split_columns, block):
    tokens, high = left.shape
    wide = right.shape[1]
    groups = plan.mp if split_columns else 1
    stride = wide // groups
    along = wide if split_columns else high
    unit = stride if split_columns else rows
    widths = [width for width, _, _ in parts]
    offsets = [sum(widths[:k]) for k in range(len(parts))]
    fits = along % block == 0 and (block % unit == 0 or unit % block == 0)
    if rows % 16 or any(width % 128 for width in widths) or not fits:
        whole = contract(left, right).astype(jnp.bfloat16).reshape(high, groups, stride)
        found = []
        for (width, counts, slots), offset in zip(parts, offsets):
            part = whole[:, :, offset : offset + width].reshape(high, groups * width)
            found.append(disassemble(plan, part, (rows, width), counts, slots, split_columns))
        return found
    tile = 256 if split_columns else block
    outs_of = [(width, count) for width, counts, _ in parts for count in counts]
    places = [
        (width, offset, slot)
        for (width, counts, _), offset in zip(parts, offsets)
        for count in counts
        for slot in range(count)
    ]

    def kernel(slots_ref, left_ref, right_ref, *refs):
        outs, gradient, sems = refs[: len(outs_of)], refs[len(outs_of)], refs[len(outs_of) + 1]
        step = pl.program_id(0)
        for start in range(0, high if split_columns else block, tile):
            lefts = left_ref[:, start : start + tile]
            product = rows_of_both(lefts, right_ref[...]).astype(jnp.bfloat16)
            if split_columns:
                gradient[start : start + tile, step_slice(block)] = product
            else:
                gradient[step_slice(block), :] = product
        targets = [out.at[slot] for out, (_, count) in zip(outs, outs_of) for slot in range(count)]
        copies = []
        for i, (width, offset, _) in enumerate(places):
            spot = spot_slice(
                gradient, plan, slots_ref[i], rows, width, split_columns, offset, stride
            )
            copies.append(pltpu.make_async_copy(spot, targets[i], sems.at[i]))
        for i, (width, offset, _) in enumerate(places):
            row_block, group = spot_of(slots_ref[i], plan, split_columns)
            if split_columns:
                done_in = (group * stride + offset + width - 1) // block
            else:
                done_in = (row_block * rows) // block

            @pl.when(done_in == step)
            def _(copy=copies[i]):
                copy.start()

        @pl.when(step == pl.num_programs(0) - 1)
        def _():
            for copy in copies:
                copy.wait()

    if split_columns:
        left_spec = pl.BlockSpec((tokens, high), fixed)
        right_spec = pl.BlockSpec((tokens, block), by_columns)
    else:
        left_spec = pl.BlockSpec((tokens, block), by_columns)
        right_spec = pl.BlockSpec((tokens, wide), fixed)
    flat = pl.pallas_call(
        kernel,
        out_shape=[
            jax.ShapeDtypeStruct((count, rows, width), jnp.bfloat16) for width, count in outs_of
        ],
        grid_spec=pltpu.PrefetchScalarGridSpec(
            num_scalar_prefetch=1,
            grid=(along // block,),
            in_specs=[left_spec, right_spec],
            out_specs=[ANY] * len(outs_of),
            scratch_shapes=[
                pltpu.VMEM((high, wide), jnp.bfloat16),
                pltpu.SemaphoreType.DMA((len(places),)),
            ],
        ),
        compiler_params=pltpu.CompilerParams(vmem_limit_bytes=VMEM_LIMIT),
        cost_estimate=pl.CostEstimate(
            flops=2 * tokens * high * wide,
            bytes_accessed=2 * (tokens * (high + wide) + high * wide),
            transcendentals=0,
        ),
    )(jnp.concatenate([slots for _, _, slots in parts]), left, right)
    found = []
    for _, counts, _ in parts:
        found.append(flat[: len(counts)])
        flat = flat[len(counts) :]
    return found


def adam_step(first, root, clipped, corr_first, corr_second):
    first = beta_first * first + (1.0 - beta_first) * clipped
    second = beta_second * root * root + (1.0 - beta_second) * clipped * clipped
    direction = first / corr_first / (jnp.sqrt(second / corr_second) + adam_eps)
    return first, jnp.sqrt(second), direction


def views(matrix, columns):
    width = matrix.shape[-1]
    if len(matrix.shape) == 3:
        return [((k,), 0, width) for k in range(matrix.shape[0])]
    starts = [sum(columns[:k]) for k in range(len(columns))]
    return [((), start, size) for start, size in zip(starts, columns)]


def moments_and_directions(scalars, gradients, states, masters, norms):
    count = len(masters)
    flat = [part for parts in gradients for part in parts]
    smem = pl.BlockSpec(memory_space=pltpu.SMEM)
    vmem = pl.BlockSpec(memory_space=pltpu.VMEM)

    def kernel(scalars_ref, *refs):
        parts, refs = list(refs[: len(flat)]), refs[len(flat) :]
        old, weights, refs = refs[:count], refs[count : 2 * count], refs[2 * count :]
        (norm_grad, norm_old, norm_weight), refs = refs[:3], refs[3:]
        fresh, ways, refs = refs[:count], refs[count : 2 * count], refs[2 * count :]
        norm_fresh, norm_out, squares = refs
        clip, corr_first, corr_second = scalars_ref[0], scalars_ref[1], scalars_ref[2]
        for k in range(count):
            mine = [parts.pop(0) for _ in gradients[k]]
            total = jnp.float32(0.0)
            for which, (lead, start, width) in enumerate(
                views(masters[k], [part.shape[1] for part in gradients[k]])
            ):
                columns = slice(start, start + width)
                if lead:
                    gradient = mine[0][:, which * width : (which + 1) * width]
                else:
                    gradient = mine[which][...]
                spot = lead + (slice(None), columns)
                first, root, direction = adam_step(
                    old[k][(0,) + spot],
                    old[k][(1,) + spot],
                    clip * gradient,
                    corr_first,
                    corr_second,
                )
                fresh[k][(0,) + spot] = first
                fresh[k][(1,) + spot] = root
                direction = direction + weight_decay * weights[k][spot]
                ways[k][spot] = direction
                total = total + jnp.sum(direction * direction)
            squares[k] = total
        first, root, direction = adam_step(
            norm_old[0], norm_old[1], clip * norm_grad[...], corr_first, corr_second
        )
        norm_fresh[0] = first
        norm_fresh[1] = root
        norm_out[...] = norm_weight[...] - learn_rate * direction

    like = lambda value: jax.ShapeDtypeStruct(value.shape, jnp.float32)
    found = pl.pallas_call(
        kernel,
        out_shape=[like(state) for state in states]
        + [like(master) for master in masters]
        + [like(norms[1]), like(norms[2]), jax.ShapeDtypeStruct((count,), jnp.float32)],
        in_specs=[smem] + [vmem] * (len(flat) + 2 * count + 3),
        out_specs=[vmem] * (2 * count + 2) + [smem],
        compiler_params=pltpu.CompilerParams(vmem_limit_bytes=VMEM_LIMIT),
    )(scalars, *flat, *states, *masters, *norms)
    return found[:count], found[count : 2 * count], *found[2 * count :]


def new_weights(steps, masters, directions):
    count = len(masters)
    smem = pl.BlockSpec(memory_space=pltpu.SMEM)
    vmem = pl.BlockSpec(memory_space=pltpu.VMEM)

    def kernel(steps_ref, *refs):
        weights, ways, refs = refs[:count], refs[count : 2 * count], refs[2 * count :]
        for k in range(count):
            value = weights[k][...] - steps_ref[k] * ways[k][...]
            refs[k][...] = value
            if k < count - 1:
                refs[count + k][...] = value.astype(jnp.bfloat16)

    found = pl.pallas_call(
        kernel,
        out_shape=[jax.ShapeDtypeStruct(master.shape, jnp.float32) for master in masters]
        + [jax.ShapeDtypeStruct(master.shape, jnp.bfloat16) for master in masters[:-1]],
        in_specs=[smem] + [vmem] * (2 * count),
        out_specs=[vmem] * (2 * count - 1),
        compiler_params=pltpu.CompilerParams(vmem_limit_bytes=VMEM_LIMIT),
    )(steps, *masters, *directions)
    return found[:count], found[count:]


BY_COLUMNS = ("entry", "up")


def per_device(
    plan,
    tokens,
    segment_ids,
    game_ids,
    return_bins,
    action_bins,
    reward_bins,
    valid_flags,
    step_count,
    entry_weight,
    entry_state,
    exit_weight,
    exit_state,
    up_weight,
    up_state,
    down_weight,
    down_state,
    head_weight,
    head_state,
    norm_params,
    norm_state,
):
    own_rows = tokens.shape[0]
    here = lax.axis_index("dp") * plan.mp + lax.axis_index("mp")
    row_start = lax.axis_index("mp") * own_rows
    own_seqs = own_rows // LEN
    segments = lax.dynamic_slice_in_dim(segment_ids, lax.axis_index("mp") * own_seqs, own_seqs)
    row_games = lax.dynamic_slice_in_dim(jnp.repeat(game_ids, LEN), row_start, own_rows)

    clock = Clock()
    masters = {"entry": entry_weight, "exit": exit_weight, "up": up_weight, "down": down_weight}
    rows_here, half_wide = entry_weight.shape[1:]
    halves = {name: value.astype(jnp.bfloat16) for name, value in masters.items()}
    down_half = down_weight.shape[1] // 2
    shards = {
        "entry": halves["entry"].transpose(1, 0, 2).reshape(rows_here, 3 * half_wide),
        "exit": halves["exit"],
        "up": halves["up"],
        "down_a": halves["down"][:, :down_half],
        "down_b": halves["down"][:, down_half:],
    }
    paths = {
        name: Travel("gather_" + name, gather_shards(plan, shard))
        for name, shard in shards.items()
        if name != "up"
    }
    up_gathered = lax.all_gather(shards["up"], AXES, axis=0)
    slots = jnp.asarray(path_table(plan), jnp.int32)[here]

    def chosen(names):
        return [paths[name] for name in names.split() if paths[name].wanted]

    def start(names, more=()):
        return clock.start(chosen(names), more)

    def wait(names):
        clock.wait([path for path in chosen(names) if path.going])

    def finish(name):
        while paths[name].wanted:
            start(name)
            wait(name)
        return paths[name].result

    def whole(*names):
        parts = [(finish(name), slots) for name in names]
        return Spread(plan, parts, names[0] in BY_COLUMNS)

    game_match = (row_games[:, None] == jnp.arange(GAMES)[None, :]).astype(jnp.float32)
    flag_float = valid_flags.astype(jnp.float32)
    local_counts = jnp.sum(game_match * jnp.sum(flag_float, -1, keepdims=True), 0)
    paths["games"] = Travel("game_counts", total_steps(plan, local_counts), True)

    start("games entry")
    resid, gains = clock.hold((tokens.astype(jnp.float32), norm_params))
    normed_one = layer_norm(resid, gains[0], gains[3]).astype(jnp.bfloat16)
    clock.also(normed_one)
    wait("entry games")
    start("entry exit")
    wait("entry exit")
    start("entry exit")
    wait("entry exit")
    (normed_one,) = start("entry down_a", (normed_one,))
    wait("entry")
    (normed_one,) = start("exit games", (normed_one,))
    entry_all = whole("entry")
    projected = project(normed_one, entry_all, 768)
    clock.also(projected)
    wait("down_a exit games")
    (projected,) = start("down_a down_b exit", (projected,))
    context = attend_call(
        attend_kernel, segments, projected, [], tokens.shape[1], plan.mp, 2
    )
    clock.also(context)
    wait("exit down_a down_b")
    (context,) = start("down_a down_b games", (context,))
    exit_all = whole("exit").matrix()
    after_attn = resid + matmul(context, exit_all)
    normed_two = layer_norm(after_attn, norm_params[1], norm_params[4]).astype(jnp.bfloat16)
    clock.also(normed_two)
    wait("down_a down_b games")
    start("down_a down_b games")
    up_all = Spread(plan, [([up_gathered], jnp.arange(plan.n, dtype=jnp.int32))], True)
    up_pre, activated = hidden_forward(normed_two, up_all, 512)
    wait("down_a down_b games")
    start("down_b games")
    wait("down_b games")
    counts_all = finish("games")
    inverse = 1.0 / (GAMES * jnp.maximum(counts_all, 1.0))
    token_scale = jnp.sum(game_match * inverse[None, :], -1)
    down_all = whole("down_a", "down_b")
    after_mlp = hidden_out(activated, after_attn, down_all, 320)
    final_norm = layer_norm(after_mlp, norm_params[2], norm_params[5]).astype(jnp.bfloat16)
    head_half = head_weight.astype(jnp.bfloat16)
    logits = matmul_t(final_norm, head_half)
    targets = (return_bins, action_bins, reward_bins)
    loss_local, loss_pull = jax.vjp(
        lambda values: part_loss(values, targets, valid_flags, token_scale), logits
    )
    d_logits = loss_pull(jnp.ones_like(loss_local))[0].astype(jnp.bfloat16)
    d_final = matmul(d_logits, head_half)
    d_mlp_in, d_gain_three, d_shift_three = norm_back(
        after_mlp, norm_params[2], norm_params[5], d_final
    )
    d_mlp_out = d_mlp_in.astype(jnp.bfloat16)

    def leave(name, left, right, block):
        rows, width = shards[name].shape
        (pieces,) = weight_grad(
            plan,
            left,
            right,
            rows,
            [(width, scatter_counts(plan), slots)],
            name in BY_COLUMNS,
            block,
        )
        paths[name] = Travel("scatter_" + name, scatter_shards(plan, pieces))

    def waiting(name):
        return [value for value, _ in paths[name].wanted]

    head_rows = head_weight.shape[0]
    leave("down_a", activated, d_mlp_out[:, :down_half], 1280)
    d_mlp_out, d_logits = start("down_a", (d_mlp_out, d_logits))
    wait("down_a")
    d_mlp_out, d_logits = start("down_a", (d_mlp_out, d_logits))
    leave("down_b", activated, d_mlp_out[:, down_half:], 1280)
    d_head = jnp.pad(contract(d_logits, final_norm), ((0, head_rows % 2), (0, 0)))
    paths["head"] = Travel("sum_head", total_steps(plan, d_head, halves=True), True)
    clock.also(*waiting("down_b"))
    wait("down_a")
    (d_mlp_out,) = start("down_a down_b head", (d_mlp_out,))
    d_up_pre = hidden_back(d_mlp_out, up_pre, down_all, 512)
    clock.also(d_up_pre)
    wait("down_a down_b head")
    (d_up_pre,) = start("down_a down_b head", (d_up_pre,))
    leave("up", normed_two, d_up_pre, 2560)
    clock.also(*waiting("up"))
    wait("down_a down_b head")
    (d_up_pre,) = start("down_b up head", (d_up_pre,))
    d_normed_two = project_back(d_up_pre, up_all, 256)
    clock.also(d_normed_two)
    wait("down_b up head")
    (d_normed_two,) = start("down_b up head", (d_normed_two,))
    d_ln_two, d_gain_two, d_shift_two = norm_back(
        after_attn, norm_params[1], norm_params[4], d_normed_two
    )
    d_attn_out = (d_mlp_in + d_ln_two).astype(jnp.bfloat16)
    leave("exit", context, d_attn_out, 1280)
    d_context = matmul_t(d_attn_out, exit_all).astype(jnp.bfloat16)
    clock.also(d_context, *waiting("exit"))
    wait("down_b up head")
    (d_context,) = start("up exit head", (d_context,))
    d_projected = attend_call(
        attend_back_kernel, segments, projected, [d_context], projected.shape[1], plan.mp, 5
    )
    clock.also(d_projected)
    wait("up exit head")
    (d_projected,) = start("up exit head", (d_projected,))
    leave("entry", normed_one, d_projected, 1920)
    clock.also(*waiting("entry"))
    wait("exit head")
    (d_projected,) = start("entry", (d_projected,))
    wait("entry")
    (d_projected,) = start("entry exit", (d_projected,))
    d_normed_one = project_back(d_projected, entry_all, 256)
    _, d_gain_one, d_shift_one = norm_back(resid, norm_params[0], norm_params[3], d_normed_one)
    clock.also(d_gain_one, d_shift_one)
    wait("entry exit up")
    start("entry exit")
    wait("entry exit")
    start("entry")
    wait("entry")
    reds = {name: finish(name) for name in shards}
    red_head = finish("head")[:head_rows]

    masters = [entry_weight, exit_weight, up_weight, down_weight, head_weight]
    states = [entry_state, exit_state, up_state, down_state, head_state]
    local_square = sum(jnp.sum(reds[name] * reds[name]) for name in shards)
    weight_local = jnp.stack([jnp.sum(master * master) for master in masters[:4]])
    wide = norm_params.shape[1]
    scalars = jnp.concatenate([jnp.stack([loss_local, local_square]), weight_local])
    small = total_over_devices(
        plan,
        jnp.stack(
            [
                d_gain_one,
                d_gain_two,
                d_gain_three,
                d_shift_one,
                d_shift_two,
                d_shift_three,
                jnp.pad(scalars, (0, wide - scalars.shape[0])),
            ]
        ),
    )
    red_norms = small[:6]
    loss_sum, grad_total, weight_sums = small[6, 0], small[6, 1], small[6, 2:6]
    small_square = jnp.sum(red_head * red_head) + jnp.sum(red_norms * red_norms)
    grad_norm = jnp.sqrt(grad_total + small_square)
    clip_factor = jnp.minimum(1.0, clip_limit / grad_norm)
    step_float = step_count[0].astype(jnp.float32)
    corr_first = 1.0 - jnp.power(beta_first, step_float)
    corr_second = 1.0 - jnp.power(beta_second, step_float)
    gradients = [
        [reds["entry"]],
        [reds["exit"]],
        [reds["up"]],
        [reds["down_a"], reds["down_b"]],
        [red_head],
    ]
    moments, directions, norm_moments, norm_new, squares = moments_and_directions(
        jnp.stack([clip_factor, corr_first, corr_second]),
        gradients,
        states,
        masters,
        (red_norms, norm_state, norm_params),
    )
    update_sums = total_over_devices(plan, squares[:4])
    weight_norms = jnp.sqrt(weight_sums)
    update_norms = jnp.sqrt(update_sums)
    head_wnorm = jnp.sqrt(jnp.sum(head_weight * head_weight))
    head_unorm = jnp.sqrt(squares[4])
    matrix_norms = jnp.stack(
        [
            jnp.concatenate([weight_norms, head_wnorm[None]]),
            jnp.concatenate([update_norms, head_unorm[None]]),
        ]
    )
    new, rounded = new_weights(
        learn_rate * (matrix_norms[0] / matrix_norms[1]), masters, directions
    )
    return (
        new[0],
        moments[0],
        rounded[0],
        new[1],
        moments[1],
        rounded[1],
        new[2],
        moments[2],
        rounded[2],
        new[3],
        moments[3],
        rounded[3],
        new[4],
        moments[4],
        norm_new,
        norm_moments,
        loss_sum,
        grad_norm,
        matrix_norms,
    )


def solution(mesh):
    in_specs = (
        P(("dp", "mp"), None),
        P("dp", None),
        P("dp"),
        P(("dp", "mp")),
        P(("dp", "mp")),
        P(("dp", "mp")),
        P(("dp", "mp"), None),
        P(),
        P(None, "dp", "mp"),
        P(None, None, "dp", "mp"),
        P(("mp", "dp"), None),
        P(None, ("mp", "dp"), None),
        P("dp", "mp"),
        P(None, "dp", "mp"),
        P(("mp", "dp"), None),
        P(None, ("mp", "dp"), None),
        P(),
        P(),
        P(),
        P(),
    )
    out_specs = (
        P(None, "dp", "mp"),
        P(None, None, "dp", "mp"),
        P(None, "dp", "mp"),
        P(("mp", "dp"), None),
        P(None, ("mp", "dp"), None),
        P(("mp", "dp"), None),
        P("dp", "mp"),
        P(None, "dp", "mp"),
        P("dp", "mp"),
        P(("mp", "dp"), None),
        P(None, ("mp", "dp"), None),
        P(("mp", "dp"), None),
        P(),
        P(),
        P(),
        P(),
        P(),
        P(),
        P(),
    )
    plan = Plan(mesh.shape["dp"], mesh.shape["mp"])
    return jax.shard_map(
        functools.partial(per_device, plan), mesh=mesh, in_specs=in_specs, out_specs=out_specs, check_vma=False
    )
```

time: 1820 us -> 791 us (0.43)
  waiting for transfers between devices: 1150 us -> 243 us
  matrix products: 314 us -> 18.3 us
  Pallas kernels: 0 us -> 234 us
  starting transfers between devices: 0.71 us -> 123 us
  blocking collectives: 121 us -> 0 us
  other arithmetic: 153 us -> 108 us
    reduce_scatter x7 -> x0, waiting for transfers between devices: 484 us -> none  [the longest x1 141 us: per_device(): lax.psum_scatter(d_up, 'dp', scatter_dimension=0, tiled=True)]
    all_gather x8 -> x1, waiting for transfers between devices: 353 us -> 0.02 us  [per_device(): up_gathered = lax.all_gather(shards['up'], AXES, axis=0)]
    ppermute x0 -> x101, waiting for transfers between devices: none -> 243 us  [send(): return lax.ppermute(value, AXES, pairs)]
    pallas_call x0 -> x16, Pallas kernels: none -> 234 us  [the longest x6 117 us: with_matrices(): pl.pallas_call(kernel, out_shape=[jax.ShapeDtypeStruct(shape, dtype) for...]
    dot_general x9 -> x0, matrix products: 185 us -> none  [the longest x1 48 us: attend_backward(): jnp.einsum('ihd,jhd->hij', d_context, values, preferred_element_type=jnp....]
    unnamed x18 -> x1, waiting for transfers between devices: 181 us -> 0.02 us
    psum x1 -> x0, waiting for transfers between devices: 131 us -> none  [per_device(): red_head, red_norms = lax.psum((d_head, d_norms), ('dp', 'mp'))]
    ppermute x0 -> x101, starting transfers between devices: none -> 123 us  [send(): return lax.ppermute(value, AXES, pairs)]
  transfers between devices with their start and end apart: 17 -> 102, of which waited for: 15 -> 34; matrix products, arithmetic and copies ran while one was open for 20% -> 16% of each run, Pallas kernels for 0% -> 24%
where the time goes in v1:
time: 791 us; the launch traced here: 785 us
  waiting for transfers between devices  243 us (31%)
  Pallas kernels  234 us (30%)
  starting transfers between devices  123 us (16%)
  other arithmetic  108 us (14%)
  local copies, waits for them, and re-layouts  33.6 us (4%)
  between operations  26 us (3%)
  matrix products  18.3 us (2%)
    ppermute x101, waiting for transfers between devices, send(): return lax.ppermute(value, AXES, pairs)  243 us
    ppermute x101, starting transfers between devices, send(): return lax.ppermute(value, AXES, pairs)  123 us
    pallas_call x6, Pallas kernels, with_matrices(): pl.pallas_call(kernel, out_shape=[jax.ShapeDtypeStruct(shape, dtype) for...  117 us
    pallas_call x4, Pallas kernels, weight_grad(): pl.pallas_call(kernel, out_shape=[jax.ShapeDtypeStruct((count, rows, widt...  54.8 us
    convert_element_type x15, other arithmetic, add_all(): return total.astype(dtype)  47.1 us
    pallas_call x2, Pallas kernels, attend_call(): pl.pallas_call(functools.partial(kernel, groups, pairs), out_shape=jax.Sh...  36.1 us
    unnamed x127, local copies, waits for them, and re-layouts  18.9 us
  transfers between devices with their start and end apart: 102, of which 34 were waited for; matrix products, arithmetic and copies ran while one was open for 16% of the time, Pallas kernels for 24%

profile of v1, /device:TPU:0, one launch (start us, length us, event | category | flops | bytes accessed | tf_op | source)
XLA Modules:
  0.0 785.4 jit_solution(11311178293205568029)
XLA Ops:
  26.1 9.1 %collective-permute-done = bf16[1,80,1920]{2,1,0:T(8,128)(2,1)} collective-permute-done((bf16[1,80,1920]{2,1,0:T(8,128)(2,1)}, bf16[1,80,1920]{2,1,0:T(8,128)(2,1)}, u32[]{:S(2)}, u32[]{:S(2)}) %collective-permute-start) | collective-permute-done | bytes 307232 | tf_op jit(solution)/shard_map/gather_entry/ppermute | solution.py:112
  36.1 11.7 %collective-permute-done.1 = bf16[1,80,1920]{2,1,0:T(8,128)(2,1)} collective-permute-done((bf16[1,80,1920]{2,1,0:T(8,128)(2,1)}, bf16[1,80,1920]{2,1,0:T(8,128)(2,1)}, u32[]{:S(2)}, u32[]{:S(2)}) %collective-permute-start.1) | collective-permute-done | bytes 307232 | tf_op jit(solution)/shard_map/gather_entry/ppermute | solution.py:112
  53.0 7.8 collective-permute-start.4
  63.3 7.2 collective-permute-done.4
  70.4 6.6 collective-permute-done.5
  77.1 11.6 %collective-permute-done.7.refs_3_ = bf16[4,80,1920]{2,1,0:T(8,128)(2,1)} collective-permute-done((bf16[4,80,1920]{2,1,0:T(8,128)(2,1)S(1)}, bf16[4,80,1920]{2,1,0:T(8,128)(2,1)}, u32[]{:S(2)}, u32[]{:S(2)}) %collective-permute-start.7) | collective-permute-done | bytes 1228832 | tf_op jit(solution)/shard_map/gather_entry/ppermute | solution.py:112
  93.4 44.2 %collective-permute-done.13.refs_2_ = bf16[4,40,1280]{2,1,0:T(8,128)(2,1)S(1)} collective-permute-done((bf16[4,40,1280]{2,1,0:T(8,128)(2,1)S(1)}, bf16[4,40,1280]{2,1,0:T(8,128)(2,1)S(1)}, u32[]{:S(2)}, u32[]{:S(2)}) %collective-permute-start.13) | collective-permute-done | bytes 409632 | tf_op jit(solution)/shard_map/gather_exit/ppermute | solution.py:112
  139.8 8.1 %collective-permute-start.16 = (bf16[1,160,640]{2,1,0:T(8,128)(2,1)}, bf16[1,160,640]{2,1,0:T(8,128)(2,1)}, u32[]{:S(2)}, u32[]{:S(2)}) collective-permute-start(bf16[1,160,640]{2,1,0:T(8,128)(2,1)} %get-tuple-element.195), channel_id=1, source_target_pairs={{0,8},{1,9},{2,10},{3,11},{4,12},{5,13},{6,14},{7,15},{8,0},{9,1},... | collective-permute-start | bytes 614408 | tf_op jit(solution)/shard_map/gather_down_a/ppermute | solution.py:112
  151.7 14.5 %collective-permute-done.16 = bf16[1,160,640]{2,1,0:T(8,128)(2,1)} collective-permute-done((bf16[1,160,640]{2,1,0:T(8,128)(2,1)}, bf16[1,160,640]{2,1,0:T(8,128)(2,1)}, u32[]{:S(2)}, u32[]{:S(2)}) %collective-permute-start.16) | collective-permute-done | bytes 204832 | tf_op jit(solution)/shard_map/gather_down_a/ppermute | solution.py:112
  170.1 14.8 %shard_map.348.qkv_ref = bf16[640,3840]{1,0:T(8,128)(2,1)} custom-call(s32[32]{0:T(128)} %dynamic-slice_bitcast_fusion.slots_ref, bf16[640,1280]{1,0:T(8,128)(2,1)} %add_convert_fusion.6.refs_0_.left_ref, bf16[4,80,1920]{2,1,0:T(8,128)(2,1)} %copy-done.47, bf16[4,80,1920]{2,1,0:T(8,128)(2,1)} %copy-done.56, ...), custom_call_target="tpu_custom_call" | custom-call | flops 6291456000 | bytes 16384000 | tf_op jit(solution)/shard_map/pallas_call | solution.py:551
  192.7 12.8 %collective-permute-done.26 = f32[41]{0:T(128)S(1)} collective-permute-done((f32[41]{0:T(128)S(1)}, f32[41]{0:T(128)S(1)}, u32[]{:S(2)}, u32[]{:S(2)}) %collective-permute-start.26) | collective-permute-done | bytes 196 | tf_op jit(solution)/shard_map/game_counts/ppermute | solution.py:112
  211.4 10.2 %shard_map.349 = bf16[640,1280]{1,0:T(8,128)(2,1)} custom-call(s32[4,160,1]{2,1,0:T(8,128)} %copy.53.column_ref, s32[4,1,160]{2,1,0:T(1,128)} %broadcast_in_dim.57.row_ref, bf16[640,3840]{1,0:T(8,128)(2,1)} %shard_map.348.qkv_ref), custom_call_target="tpu_custom_call" | custom-call | flops 524288000 | bytes 9830400 | tf_op jit(solution)/shard_map/pallas_call | solution.py:454
  241.4 8.9 %collective-permute-done.31.refs_5_ = bf16[4,160,640]{2,1,0:T(8,128)(2,1)S(1)} collective-permute-done((bf16[4,160,640]{2,1,0:T(8,128)(2,1)}, bf16[4,160,640]{2,1,0:T(8,128)(2,1)S(1)}, u32[]{:S(2)}, u32[]{:S(2)}) %collective-permute-start.31) | collective-permute-done | bytes 819232 | tf_op jit(solution)/shard_map/gather_down_a/ppermute | solution.py:112
  251.6 7.5 collective-permute-done.35.refs_12_
  264.4 10.1 %collective-permute-done.37.refs_13_ = bf16[4,160,640]{2,1,0:T(8,128)(2,1)} collective-permute-done((bf16[4,160,640]{2,1,0:T(8,128)(2,1)S(1)}, bf16[4,160,640]{2,1,0:T(8,128)(2,1)}, u32[]{:S(2)}, u32[]{:S(2)}) %collective-permute-start.37) | collective-permute-done | bytes 819232 | tf_op jit(solution)/shard_map/gather_down_b/ppermute | solution.py:112
  279.8 21.3 %shard_map.351 = (f32[640,5120]{1,0:T(8,128)}, bf16[640,5120]{1,0:T(8,128)(2,1)}) custom-call(s32[32]{0:T(128)} %iota.21.slots_ref, bf16[640,1280]{1,0:T(8,128)(2,1)} %add_convert_fusion.5.refs_0_.left_ref, bf16[32,80,2560]{2,1,0:T(8,128)(2,1)} %bitcast.60), custom_call_target="tpu_custom_call" | custom-call | flops 8388608000 | bytes 34406400 | tf_op jit(solution)/shard_map/pallas_call | solution.py:551
  301.1 19.5 %shard_map.352 = f32[640,1280]{1,0:T(8,128)} custom-call(s32[64]{0:T(128)} %pad_add_fusion.slots_ref, bf16[640,5120]{1,0:T(8,128)(2,1)} %get-tuple-element.211.refs_0_.left_ref, f32[640,1280]{1,0:T(8,128)} %copy-done.3, bf16[4,160,640]{2,1,0:T(8,128)(2,1)} %pad_maximum_fusion.refs_2_, bf16[4,160,640]{2,1,0:T(8,128)(2,1)} %collective-permute-done.22.refs_3_, ...), custom_call_target="tpu_custom_call" | custom-call | flops 8388608000 | bytes 26214400 | tf_op jit(solution)/shard_map/pallas_call | solution.py:551
  334.9 11.7 %shard_map.353 = (bf16[16,160,640]{2,1,0:T(8,128)(2,1)}, bf16[12,160,640]{2,1,0:T(8,128)(2,1)}, bf16[4,160,640]{2,1,0:T(8,128)(2,1)}) custom-call(s32[32]{0:T(128)} %dynamic-slice_bitcast_fusion.slots_ref, bf16[640,5120]{1,0:T(8,128)(2,1)} %get-tuple-element.211.refs_0_.left_ref, bf16[640,640]{1,0:T(8,128)(2,1)} %slice.575.right_ref), custom_call_target="tpu_custom_call" | custom-call | flops 4194304000 | bytes 13926400 | tf_op jit(solution)/shard_map/pallas_call | solution.py:764
  358.3 11.9 %shard_map.354 = (bf16[16,160,640]{2,1,0:T(8,128)(2,1)}, bf16[12,160,640]{2,1,0:T(8,128)(2,1)}, bf16[4,160,640]{2,1,0:T(8,128)(2,1)}) custom-call(s32[32]{0:T(128)} %dynamic-slice_bitcast_fusion.slots_ref, bf16[640,5120]{1,0:T(8,128)(2,1)} %get-tuple-element.211.refs_0_.left_ref, bf16[640,640]{1,0:T(8,128)(2,1)} %slice.463.right_ref), custom_call_target="tpu_custom_call" | custom-call | flops 4194304000 | bytes 13926400 | tf_op jit(solution)/shard_map/pallas_call | solution.py:764
  377.7 26.1 %shard_map.355.right_ref.refs_0_ = bf16[640,5120]{1,0:T(8,128)(2,1)} custom-call(s32[64]{0:T(128)} %pad_add_fusion.slots_ref, bf16[640,1280]{1,0:T(8,128)(2,1)} %copy-done.11, f32[640,5120]{1,0:T(8,128)} %get-tuple-element.245.refs_1_, bf16[4,160,640]{2,1,0:T(8,128)(2,1)} %pad_maximum_fusion.refs_2_, bf16[4,160,640]{2,1,0:T(8,128)(2,1)} %collective-permute-done.22.refs_3_, ...), custom_call_target="tpu_custom_call" | custom-call | flops 8388608000 | bytes 34406400 | tf_op jit(solution)/shard_map/pallas_call | solution.py:551
  412.3 17.1 %shard_map.356 = (bf16[16,80,2560]{2,1,0:T(8,128)(2,1)}, bf16[12,80,2560]{2,1,0:T(8,128)(2,1)}, bf16[4,80,2560]{2,1,0:T(8,128)(2,1)}) custom-call(s32[32]{0:T(128)} %dynamic-slice_bitcast_fusion.slots_ref, bf16[640,1280]{1,0:T(8,128)(2,1)} %add_convert_fusion.5.refs_0_.left_ref, bf16[640,5120]{1,0:T(8,128)(2,1)} %shard_map.355.right_ref.refs_0_), custom_call_target="tpu_custom_call" | custom-call | flops 8388608000 | bytes 21299200 | tf_op jit(solution)/shard_map/pallas_call | solution.py:764
  439.6 7.6 collective-permute-done.56
  452.6 19.5 %shard_map.357 = f32[640,1280]{1,0:T(8,128)} custom-call(s32[32]{0:T(128)} %iota.22.slots_ref, bf16[640,5120]{1,0:T(8,128)(2,1)} %shard_map.355.right_ref.refs_0_, bf16[32,80,2560]{2,1,0:T(8,128)(2,1)} %bitcast.61), custom_call_target="tpu_custom_call" | custom-call | flops 8388608000 | bytes 22937600 | tf_op jit(solution)/shard_map/pallas_call | solution.py:551
  513.8 6.2 add_convert_fusion.1
  526.0 25.9 %shard_map.359.right_ref.refs_0_ = bf16[640,3840]{1,0:T(8,128)(2,1)} custom-call(s32[4,160,1]{2,1,0:T(8,128)} %copy.53.column_ref, s32[4,1,160]{2,1,0:T(1,128)} %broadcast_in_dim.57.row_ref, bf16[640,3840]{1,0:T(8,128)(2,1)} %shard_map.348.qkv_ref, bf16[640,1280]{1,0:T(8,128)(2,1)} %convolution_convert_fusion.1.d_context_ref), custom_call_target="tpu_custom_call" | custom-call | flops 1310720000 | bytes 24576000 | tf_op jit(solution)/shard_map/pallas_call | solution.py:454
  562.1 14.2 %shard_map.360 = (bf16[16,80,1920]{2,1,0:T(8,128)(2,1)}, bf16[12,80,1920]{2,1,0:T(8,128)(2,1)}, bf16[4,80,1920]{2,1,0:T(8,128)(2,1)}) custom-call(s32[32]{0:T(128)} %dynamic-slice_bitcast_fusion.slots_ref, bf16[640,1280]{1,0:T(8,128)(2,1)} %add_convert_fusion.6.refs_0_.left_ref, bf16[640,3840]{1,0:T(8,128)(2,1)} %shard_map.359.right_ref.refs_0_), custom_call_target="tpu_custom_call" | custom-call | flops 6291456000 | bytes 16384000 | tf_op jit(solution)/shard_map/pallas_call | solution.py:764
  603.1 9.8 %collective-permute-done.78 = bf16[4,40,1280]{2,1,0:T(8,128)(2,1)} collective-permute-done((bf16[4,40,1280]{2,1,0:T(8,128)(2,1)}, bf16[4,40,1280]{2,1,0:T(8,128)(2,1)}, u32[]{:S(2)}, u32[]{:S(2)}) %collective-permute-start.78) | collective-permute-done | bytes 409632 | tf_op jit(solution)/shard_map/scatter_exit/ppermute | solution.py:112
  637.2 15.7 %shard_map.361 = f32[640,1280]{1,0:T(8,128)} custom-call(s32[32]{0:T(128)} %dynamic-slice_bitcast_fusion.slots_ref, bf16[640,3840]{1,0:T(8,128)(2,1)} %shard_map.359.right_ref.refs_0_, bf16[4,80,1920]{2,1,0:T(8,128)(2,1)} %copy-done.47, bf16[4,80,1920]{2,1,0:T(8,128)(2,1)} %copy-done.56, bf16[4,80,1920]{2,1,0:T(8,128)(2,1)} %collective-permute-done.7.refs_3_, ...), custom_call_target="tpu_custom_call" | custom-call | flops 6291456000 | bytes 18022400 | tf_op jit(solution)/shard_map/pallas_call | solution.py:551
  652.9 8.4 %collective-permute-start.84 = (bf16[1,40,1280]{2,1,0:T(8,128)(2,1)S(1)}, bf16[1,40,1280]{2,1,0:T(8,128)(2,1)S(1)}, u32[]{:S(2)}, u32[]{:S(2)}) collective-permute-start(bf16[1,40,1280]{2,1,0:T(8,128)(2,1)S(1)} %get-tuple-element.294), channel_id=1, source_target_pairs={{0,8},{1,9},{2,10},{3,11},{4,12},{5,13},{6,14},{7,15},{8,0},{9,1},... | collective-permute-start | bytes 307208 | tf_op jit(solution)/shard_map/scatter_exit/ppermute | solution.py:112
  680.0 6.4 collective-permute-done.87
  686.4 12.3 %collective-permute-done.88 = bf16[1,80,1920]{2,1,0:T(8,128)(2,1)S(1)} collective-permute-done((bf16[1,80,1920]{2,1,0:T(8,128)(2,1)S(1)}, bf16[1,80,1920]{2,1,0:T(8,128)(2,1)S(1)}, u32[]{:S(2)}, u32[]{:S(2)}) %collective-permute-start.88) | collective-permute-done | bytes 307232 | tf_op jit(solution)/shard_map/scatter_entry/ppermute | solution.py:112
  735.9 12.2 %shard_map.362 = (f32[2,3,80,640]{3,2,1,0:T(8,128)}, f32[2,40,1280]{2,1,0:T(8,128)}, f32[2,80,2560]{2,1,0:T(8,128)}, f32[2,160,1280]{2,1,0:T(8,128)}, f32[2,142,...) custom-call(f32[3]{0:T(128)} %pad_maximum_fusion.5.scalars_ref, ...), custom_call_target="tpu_custom_call" | custom-call | tf_op jit(solution)/shard_map/pallas_call | solution.py:854
  (457 shorter events, 328.7 us)
Async XLA Ops:
  7.2 272.0 %all-gather.3.cloned.1.call-start = ((), (), s32[]{:S(2)}) async-start(), calls=%async_computation | async-start | bytes 13516800 | tf_op jit(solution)/shard_map/all_gather | solution.py:940
  17.6 30.2 %collective-permute-start.1 = (bf16[1,80,1920]{2,1,0:T(8,128)(2,1)}, bf16[1,80,1920]{2,1,0:T(8,128)(2,1)}, u32[]{:S(2)}, u32[]{:S(2)}) collective-permute-start(bf16[1,80,1920]{2,1,0:T(8,128)(2,1)} %broadcast_in_dim_reshape.2), channel_id=1, source_target_pairs={{0,16},{1,17},{2,18},{3,19},{4,20},{5,21},{6,22},{7,23},{8,24},{9,... | collective-permute-start | bytes 921608 | tf_op jit(solution)/shard_map/gather_entry/ppermute | solution.py:112
  20.2 28.6 %collective-permute-start.2 = (bf16[1,80,1920]{2,1,0:T(8,128)(2,1)}, bf16[1,80,1920]{2,1,0:T(8,128)(2,1)}, u32[]{:S(2)}, u32[]{:S(2)}) collective-permute-start(bf16[1,80,1920]{2,1,0:T(8,128)(2,1)} %broadcast_in_dim_reshape.2), channel_id=1, source_target_pairs={{0,24},{1,25},{2,26},{3,27},{4,28},{5,29},{6,30},{7,31},{8,16},{9,... | collective-permute-start | bytes 921608 | tf_op jit(solution)/shard_map/gather_entry/ppermute | solution.py:112
  49.9 38.9 %collective-permute-start.7 = (bf16[4,80,1920]{2,1,0:T(8,128)(2,1)S(1)}, bf16[4,80,1920]{2,1,0:T(8,128)(2,1)}, u32[]{:S(2)}, u32[]{:S(2)}) collective-permute-start(bf16[4,80,1920]{2,1,0:T(8,128)(2,1)S(1)} %constant_dynamic-update-slice_fusion.refs_1_), channel_id=1, source_target_pairs={{0,1},{1,0},{2,6},{3,7},{4,5},{5,4},{6,2},{7,3},{8,9},{9,8},{10,14... | collective-permute-start | bytes 3686408 | tf_op jit(solution)/shard_map/gather_entry/ppermute | solution.py:112
  51.4 37.3 %collective-permute-start.3 = (bf16[4,80,1920]{2,1,0:T(8,128)(2,1)S(1)}, bf16[4,80,1920]{2,1,0:T(8,128)(2,1)S(1)}, u32[]{:S(2)}, u32[]{:S(2)}) collective-permute-start(bf16[4,80,1920]{2,1,0:T(8,128)(2,1)S(1)} %constant_dynamic-update-slice_fusion.refs_1_), channel_id=1, source_target_pairs={{0,4},{1,5},{2,3},{3,2},{4,0},{5,1},{6,7},{7,6},{8,12},{9,13},{10,... | collective-permute-start | bytes 3686408 | tf_op jit(solution)/shard_map/gather_entry/ppermute | solution.py:112
  88.8 49.6 %collective-permute-start.10 = (bf16[4,80,1920]{2,1,0:T(8,128)(2,1)S(1)}, bf16[4,80,1920]{2,1,0:T(8,128)(2,1)}, u32[]{:S(2)}, u32[]{:S(2)}) collective-permute-start(bf16[4,80,1920]{2,1,0:T(8,128)(2,1)S(1)} %collective-permute-done.3.refs_2_), channel_id=1, source_target_pairs={{0,1},{1,0},{2,6},{3,7},{4,5},{5,4},{6,2},{7,3},{8,9},{9,8},{10,14... | collective-permute-start | bytes 3686408 | tf_op jit(solution)/shard_map/gather_entry/ppermute | solution.py:112
  90.3 48.9 %collective-permute-start.11 = (bf16[4,80,1920]{2,1,0:T(8,128)(2,1)S(1)}, bf16[4,80,1920]{2,1,0:T(8,128)(2,1)S(1)}, u32[]{:S(2)}, u32[]{:S(2)}) collective-permute-start(bf16[4,80,1920]{2,1,0:T(8,128)(2,1)S(1)} %constant_dynamic-update-slice_fusion.refs_1_), channel_id=1, source_target_pairs={{0,2},{1,3},{2,0},{3,1},{4,6},{5,7},{6,4},{7,5},{8,10},{9,11},{10,... | collective-permute-start | bytes 3686408 | tf_op jit(solution)/shard_map/gather_entry/ppermute | solution.py:112
  90.3 48.9 %collective-permute-start.12 = (bf16[4,80,1920]{2,1,0:T(8,128)(2,1)S(1)}, bf16[4,80,1920]{2,1,0:T(8,128)(2,1)S(1)}, u32[]{:S(2)}, u32[]{:S(2)}) collective-permute-start(bf16[4,80,1920]{2,1,0:T(8,128)(2,1)S(1)} %collective-permute-done.3.refs_2_), channel_id=1, source_target_pairs={{0,2},{1,3},{2,0},{3,1},{4,6},{5,7},{6,4},{7,5},{8,10},{9,11},{10,... | collective-permute-start | bytes 3686408 | tf_op jit(solution)/shard_map/gather_entry/ppermute | solution.py:112
  90.8 46.9 %collective-permute-start.13 = (bf16[4,40,1280]{2,1,0:T(8,128)(2,1)S(1)}, bf16[4,40,1280]{2,1,0:T(8,128)(2,1)S(1)}, u32[]{:S(2)}, u32[]{:S(2)}) collective-permute-start(bf16[4,40,1280]{2,1,0:T(8,128)(2,1)S(1)} %pad_maximum_fusion.2.refs_0_), channel_id=1, source_target_pairs={{0,1},{1,0},{2,6},{3,7},{4,5},{5,4},{6,2},{7,3},{8,9},{9,8},{10,14... | collective-permute-start | bytes 1228808 | tf_op jit(solution)/shard_map/gather_exit/ppermute | solution.py:112
  91.3 46.3 %collective-permute-start.8 = (bf16[4,40,1280]{2,1,0:T(8,128)(2,1)S(1)}, bf16[4,40,1280]{2,1,0:T(8,128)(2,1)S(1)}, u32[]{:S(2)}, u32[]{:S(2)}) collective-permute-start(bf16[4,40,1280]{2,1,0:T(8,128)(2,1)S(1)} %pad_maximum_fusion.2.refs_0_), channel_id=1, source_target_pairs={{0,4},{1,5},{2,3},{3,2},{4,0},{5,1},{6,7},{7,6},{8,12},{9,13},{10,... | collective-permute-start | bytes 1228808 | tf_op jit(solution)/shard_map/gather_exit/ppermute | solution.py:112
  139.2 29.3 %collective-permute-start.14 = (bf16[4,80,1920]{2,1,0:T(8,128)(2,1)}, bf16[4,80,1920]{2,1,0:T(8,128)(2,1)}, u32[]{:S(2)}, u32[]{:S(2)}) collective-permute-start(bf16[4,80,1920]{2,1,0:T(8,128)(2,1)} %collective-permute-done.7.refs_3_), channel_id=1, source_target_pairs={{0,2},{1,3},{2,0},{3,1},{4,6},{5,7},{6,4},{7,5},{8,10},{9,11},{10,... | collective-permute-start | bytes 3686408 | tf_op jit(solution)/shard_map/gather_entry/ppermute | solution.py:112
  139.2 29.2 %collective-permute-start.15 = (bf16[4,80,1920]{2,1,0:T(8,128)(2,1)}, bf16[4,80,1920]{2,1,0:T(8,128)(2,1)}, u32[]{:S(2)}, u32[]{:S(2)}) collective-permute-start(bf16[4,80,1920]{2,1,0:T(8,128)(2,1)} %collective-permute-done.10.refs_4_), channel_id=1, source_target_pairs={{0,2},{1,3},{2,0},{3,1},{4,6},{5,7},{6,4},{7,5},{8,10},{9,11},{10,... | collective-permute-start | bytes 3686408 | tf_op jit(solution)/shard_map/gather_entry/ppermute | solution.py:112
  184.9 43.4 %collective-permute-start.22 = (bf16[4,160,640]{2,1,0:T(8,128)(2,1)}, bf16[4,160,640]{2,1,0:T(8,128)(2,1)}, u32[]{:S(2)}, u32[]{:S(2)}) collective-permute-start(bf16[4,160,640]{2,1,0:T(8,128)(2,1)} %pad_maximum_fusion.refs_2_), channel_id=1, source_target_pairs={{0,4},{1,5},{2,3},{3,2},{4,0},{5,1},{6,7},{7,6},{8,12},{9,13},{10,... | collective-permute-start | bytes 2457608 | tf_op jit(solution)/shard_map/gather_down_a/ppermute | solution.py:112
  185.9 42.3 %collective-permute-start.29 = (bf16[4,160,640]{2,1,0:T(8,128)(2,1)}, bf16[4,160,640]{2,1,0:T(8,128)(2,1)}, u32[]{:S(2)}, u32[]{:S(2)}) collective-permute-start(bf16[4,160,640]{2,1,0:T(8,128)(2,1)} %pad_maximum_fusion.refs_2_), channel_id=1, source_target_pairs={{0,1},{1,0},{2,6},{3,7},{4,5},{5,4},{6,2},{7,3},{8,9},{9,8},{10,14... | collective-permute-start | bytes 2457608 | tf_op jit(solution)/shard_map/gather_down_a/ppermute | solution.py:112
  375.2 35.1 %collective-permute-start.52 = (bf16[12,160,640]{2,1,0:T(8,128)(2,1)}, bf16[12,160,640]{2,1,0:T(8,128)(2,1)}, u32[]{:S(2)}, u32[]{:S(2)}) collective-permute-start(bf16[12,160,640]{2,1,0:T(8,128)(2,1)} %get-tuple-element.246), channel_id=1, source_target_pairs={{0,2},{1,3},{2,0},{3,1},{4,6},{5,7},{6,4},{7,5},{8,10},{9,11},{10,... | collective-permute-start | bytes 7372808 | tf_op jit(solution)/shard_map/scatter_down_b/ppermute | solution.py:112
  375.2 28.6 %collective-permute-start.51 = (f32[71,1280]{1,0:T(8,128)S(1)}, f32[71,1280]{1,0:T(8,128)}, u32[]{:S(2)}, u32[]{:S(2)}) collective-permute-start(f32[71,1280]{1,0:T(8,128)S(1)} %slice_select_fusion), channel_id=1, source_target_pairs={{0,2},{1,3},{2,0},{3,1},{4,6},{5,7},{6,4},{7,5},{8,10},{9,11},{10,... | collective-permute-start | bytes 1090568 | tf_op jit(solution)/shard_map/sum_head/ppermute | solution.py:112
  375.7 32.2 %collective-permute-start.50 = (bf16[4,160,640]{2,1,0:T(8,128)(2,1)}, bf16[4,160,640]{2,1,0:T(8,128)(2,1)}, u32[]{:S(2)}, u32[]{:S(2)}) collective-permute-start(bf16[4,160,640]{2,1,0:T(8,128)(2,1)} %get-tuple-element.242), channel_id=1, source_target_pairs={{0,2},{1,3},{2,0},{3,1},{4,6},{5,7},{6,4},{7,5},{8,10},{9,11},{10,... | collective-permute-start | bytes 2457608 | tf_op jit(solution)/shard_map/scatter_down_b/ppermute | solution.py:112
  375.7 29.4 %collective-permute-start.48 = (bf16[4,160,640]{2,1,0:T(8,128)(2,1)}, bf16[4,160,640]{2,1,0:T(8,128)(2,1)}, u32[]{:S(2)}, u32[]{:S(2)}) collective-permute-start(bf16[4,160,640]{2,1,0:T(8,128)(2,1)} %get-tuple-element.239), channel_id=1, source_target_pairs={{0,4},{1,5},{2,3},{3,2},{4,0},{5,1},{6,7},{7,6},{8,12},{9,13},{10,... | collective-permute-start | bytes 2457608 | tf_op jit(solution)/shard_map/scatter_down_a/ppermute | solution.py:112
  377.2 27.9 %collective-permute-start.49 = (bf16[4,160,640]{2,1,0:T(8,128)(2,1)}, bf16[4,160,640]{2,1,0:T(8,128)(2,1)}, u32[]{:S(2)}, u32[]{:S(2)}) collective-permute-start(bf16[4,160,640]{2,1,0:T(8,128)(2,1)} %get-tuple-element.240), channel_id=1, source_target_pairs={{0,1},{1,0},{2,6},{3,7},{4,5},{5,4},{6,2},{7,3},{8,9},{9,8},{10,14... | collective-permute-start | bytes 2457608 | tf_op jit(solution)/shard_map/scatter_down_a/ppermute | solution.py:112
  448.0 37.1 %collective-permute-start.58 = (bf16[12,80,2560]{2,1,0:T(8,128)(2,1)}, bf16[12,80,2560]{2,1,0:T(8,128)(2,1)}, u32[]{:S(2)}, u32[]{:S(2)}) collective-permute-start(bf16[12,80,2560]{2,1,0:T(8,128)(2,1)} %get-tuple-element.256), channel_id=1, source_target_pairs={{0,2},{1,3},{2,0},{3,1},{4,6},{5,7},{6,4},{7,5},{8,10},{9,11},{10,... | collective-permute-start | bytes 14745608 | tf_op jit(solution)/shard_map/scatter_up/ppermute | solution.py:112
  448.0 33.6 %collective-permute-start.61 = (bf16[4,80,2560]{2,1,0:T(8,128)(2,1)}, bf16[4,80,2560]{2,1,0:T(8,128)(2,1)}, u32[]{:S(2)}, u32[]{:S(2)}) collective-permute-start(bf16[4,80,2560]{2,1,0:T(8,128)(2,1)} %get-tuple-element.259), channel_id=1, source_target_pairs={{0,2},{1,3},{2,0},{3,1},{4,6},{5,7},{6,4},{7,5},{8,10},{9,11},{10,... | collective-permute-start | bytes 4915208 | tf_op jit(solution)/shard_map/scatter_up/ppermute | solution.py:112
  448.5 30.2 %collective-permute-start.59 = (bf16[4,160,640]{2,1,0:T(8,128)(2,1)}, bf16[4,160,640]{2,1,0:T(8,128)(2,1)}, u32[]{:S(2)}, u32[]{:S(2)}) collective-permute-start(bf16[4,160,640]{2,1,0:T(8,128)(2,1)} %get-tuple-element.257), channel_id=1, source_target_pairs={{0,4},{1,5},{2,3},{3,2},{4,0},{5,1},{6,7},{7,6},{8,12},{9,13},{10,... | collective-permute-start | bytes 2457608 | tf_op jit(solution)/shard_map/scatter_down_b/ppermute | solution.py:112
  449.9 28.9 %collective-permute-start.60 = (bf16[4,160,640]{2,1,0:T(8,128)(2,1)}, bf16[4,160,640]{2,1,0:T(8,128)(2,1)}, u32[]{:S(2)}, u32[]{:S(2)}) collective-permute-start(bf16[4,160,640]{2,1,0:T(8,128)(2,1)} %get-tuple-element.258), channel_id=1, source_target_pairs={{0,1},{1,0},{2,6},{3,7},{4,5},{5,4},{6,2},{7,3},{8,9},{9,8},{10,14... | collective-permute-start | bytes 2457608 | tf_op jit(solution)/shard_map/scatter_down_b/ppermute | solution.py:112
  520.0 37.4 %collective-permute-start.68 = (bf16[4,80,2560]{2,1,0:T(8,128)(2,1)}, bf16[4,80,2560]{2,1,0:T(8,128)(2,1)}, u32[]{:S(2)}, u32[]{:S(2)}) collective-permute-start(bf16[4,80,2560]{2,1,0:T(8,128)(2,1)} %get-tuple-element.270), channel_id=1, source_target_pairs={{0,4},{1,5},{2,3},{3,2},{4,0},{5,1},{6,7},{7,6},{8,12},{9,13},{10,... | collective-permute-start | bytes 4915208 | tf_op jit(solution)/shard_map/scatter_up/ppermute | solution.py:112
  520.9 36.5 %collective-permute-start.69 = (bf16[4,80,2560]{2,1,0:T(8,128)(2,1)}, bf16[4,80,2560]{2,1,0:T(8,128)(2,1)}, u32[]{:S(2)}, u32[]{:S(2)}) collective-permute-start(bf16[4,80,2560]{2,1,0:T(8,128)(2,1)} %get-tuple-element.271), channel_id=1, source_target_pairs={{0,1},{1,0},{2,6},{3,7},{4,5},{5,4},{6,2},{7,3},{8,9},{9,8},{10,14... | collective-permute-start | bytes 4915208 | tf_op jit(solution)/shard_map/scatter_up/ppermute | solution.py:112
  522.0 31.8 %collective-permute-start.70 = (bf16[4,40,1280]{2,1,0:T(8,128)(2,1)}, bf16[4,40,1280]{2,1,0:T(8,128)(2,1)S(1)}, u32[]{:S(2)}, u32[]{:S(2)}) collective-permute-start(bf16[4,40,1280]{2,1,0:T(8,128)(2,1)} %get-tuple-element.273), channel_id=1, source_target_pairs={{0,2},{1,3},{2,0},{3,1},{4,6},{5,7},{6,4},{7,5},{8,10},{9,11},{10,... | collective-permute-start | bytes 1228808 | tf_op jit(solution)/shard_map/scatter_exit/ppermute | solution.py:112
  522.0 29.9 %collective-permute-start.71 = (f32[71,1280]{1,0:T(8,128)}, f32[71,1280]{1,0:T(8,128)}, u32[]{:S(2)}, u32[]{:S(2)}) collective-permute-start(f32[71,1280]{1,0:T(8,128)} %add.518), channel_id=1, source_target_pairs={{0,16},{1,17},{2,18},{3,19},{4,20},{5,21},{6,22},{7,23},{8,24},{9,... | collective-permute-start | bytes 1090568 | tf_op jit(solution)/shard_map/sum_head/ppermute | solution.py:112
  525.8 35.4 %collective-permute-start.72 = (bf16[12,40,1280]{2,1,0:T(8,128)(2,1)}, bf16[12,40,1280]{2,1,0:T(8,128)(2,1)}, u32[]{:S(2)}, u32[]{:S(2)}) collective-permute-start(bf16[12,40,1280]{2,1,0:T(8,128)(2,1)} %get-tuple-element.276), channel_id=1, source_target_pairs={{0,2},{1,3},{2,0},{3,1},{4,6},{5,7},{6,4},{7,5},{8,10},{9,11},{10,... | collective-permute-start | bytes 3686408 | tf_op jit(solution)/shard_map/scatter_exit/ppermute | solution.py:112
  595.9 29.5 %collective-permute-start.80 = (bf16[1,80,2560]{2,1,0:T(8,128)(2,1)}, bf16[1,80,2560]{2,1,0:T(8,128)(2,1)S(1)}, u32[]{:S(2)}, u32[]{:S(2)}) collective-permute-start(bf16[1,80,2560]{2,1,0:T(8,128)(2,1)} %get-tuple-element.290), channel_id=1, source_target_pairs={{0,16},{1,17},{2,18},{3,19},{4,20},{5,21},{6,22},{7,23},{8,24},{9,... | collective-permute-start | bytes 1228808 | tf_op jit(solution)/shard_map/scatter_up/ppermute | solution.py:112
  625.4 36.0 %collective-permute-start.82 = (bf16[4,80,1920]{2,1,0:T(8,128)(2,1)}, bf16[4,80,1920]{2,1,0:T(8,128)(2,1)}, u32[]{:S(2)}, u32[]{:S(2)}) collective-permute-start(bf16[4,80,1920]{2,1,0:T(8,128)(2,1)} %get-tuple-element.292), channel_id=1, source_target_pairs={{0,4},{1,5},{2,3},{3,2},{4,0},{5,1},{6,7},{7,6},{8,12},{9,13},{10,... | collective-permute-start | bytes 3686408 | tf_op jit(solution)/shard_map/scatter_entry/ppermute | solution.py:112
  626.7 37.1 %collective-permute-start.83 = (bf16[4,80,1920]{2,1,0:T(8,128)(2,1)}, bf16[4,80,1920]{2,1,0:T(8,128)(2,1)}, u32[]{:S(2)}, u32[]{:S(2)}) collective-permute-start(bf16[4,80,1920]{2,1,0:T(8,128)(2,1)} %get-tuple-element.293), channel_id=1, source_target_pairs={{0,1},{1,0},{2,6},{3,7},{4,5},{5,4},{6,2},{7,3},{8,9},{9,8},{10,14... | collective-permute-start | bytes 3686408 | tf_op jit(solution)/shard_map/scatter_entry/ppermute | solution.py:112
  633.8 92.7 %collective-permute-start.95 = (f32[71,1280]{1,0:T(8,128)}, f32[71,1280]{1,0:T(8,128)}, u32[]{:S(2)}, u32[]{:S(2)}) collective-permute-start(f32[71,1280]{1,0:T(8,128)} %add.528), channel_id=1, source_target_pairs={{0,2},{1,3},{2,0},{3,1},{4,6},{5,7},{6,4},{7,5},{8,10},{9,11},{10,... | collective-permute-start | bytes 1090568 | tf_op jit(solution)/shard_map/sum_head/ppermute | solution.py:112
  (130 other events, 2078.5 us)
Sparse Core Ops, SparseCore 0:
  11.5 149.2 all-gather.2

commit v2 on v1

--- a/solution.py
+++ b/solution.py
@@ -100,6 +100,9 @@
     def z_moves(self):
         return [self.flip_z(bits) for bits in range(1, self.z)]
 
+    def z_groups(self, split):
+        return split if split and self.z == 4 else (tuple(range(self.z - 1)),)
+
 
 def moved(table, pairs):
     got = np.full_like(table, -1)
@@ -127,34 +130,34 @@
 
 
 class Clock:
-    def __init__(self):
-        self.gates = []
-
-    def hold(self, values):
+    def __init__(self, token):
+        self.token = token
+
+    def through(self, values):
         flat, tree = jax.tree.flatten(values)
-        passed = lax.optimization_barrier(tuple(flat) + tuple(self.gates))
-        return jax.tree.unflatten(tree, passed[: len(flat)])
+        passed = lax.optimization_barrier(tuple(flat) + (self.token,))
+        self.token = passed[-1]
+        return jax.tree.unflatten(tree, passed[:-1])
 
     def start(self, travels, more=()):
-        values, more = self.hold(([[v for v, _ in travel.wanted] for travel in travels], more))
-        self.gates = []
+        values, more = self.through(([[v for v, _ in travel.wanted] for travel in travels], more))
         for travel, ready in zip(travels, values):
             with jax.named_scope(travel.name):
                 travel.going = [send(v, pairs) for v, (_, pairs) in zip(ready, travel.wanted)]
         return more
 
-    def wait(self, travels):
+    def wait(self, travels, more=()):
+        loud = [travel for travel in travels if not travel.quiet]
+        arrived, more = self.through(([travel.going for travel in loud], more))
+        for travel, got in zip(loud, arrived):
+            travel.going = got
         for travel in travels:
-            if not travel.quiet:
-                self.gates = self.gates + travel.going
+            got, travel.going = travel.going, None
             try:
-                travel.wanted = travel.steps.send(travel.going)
+                travel.wanted = travel.steps.send(got)
             except StopIteration as end:
                 travel.wanted, travel.result = None, end.value
-            travel.going = None
-
-    def also(self, *values):
-        self.gates = self.gates + list(values)
+        return more
 
 
 def path_table(plan):
@@ -166,10 +169,13 @@
     return np.concatenate([table, moved(table, core)], 1)
 
 
-def gather_shards(plan, shard):
+def gather_shards(plan, shard, split=()):
     first, second, core = plan.flip_first(), plan.flip_second(), plan.flip_core()
-    got = yield [(shard[None], pairs) for pairs in plan.z_moves()]
-    line = jnp.concatenate([shard[None]] + got)
+    moves, got = plan.z_moves(), {}
+    for group in plan.z_groups(split):
+        arrived = yield [(shard[None], moves[k]) for k in group]
+        got.update(zip(group, arrived))
+    line = jnp.concatenate([shard[None]] + [got[k] for k in range(len(moves))])
     near, side = yield [(line, first), (line, second)]
     far, line_twin, near_twin = yield [(near, second), (line, core), (near, core)]
     side_twin, far_twin = yield [(side, core), (far, core)]
@@ -180,7 +186,7 @@
     return [4 * plan.z, 3 * plan.z, plan.z]
 
 
-def scatter_shards(plan, pieces):
+def scatter_shards(plan, pieces, split=()):
     first, second, core = plan.flip_first(), plan.flip_second(), plan.flip_core()
     own, rest_twin, far_twin = pieces
     size = plan.z
@@ -194,11 +200,12 @@
     side = add_all([quarter(own, 2), quarter(rest_got, 2)])
     near_got, side_got = yield [(near, first), (side, second)]
     terms = [quarter(own, 0), quarter(rest_got, 0), near_got, side_got]
-    got = yield [
-        (add_all([term[k + 1 : k + 2] for term in terms]), pairs)
-        for k, pairs in enumerate(plan.z_moves())
-    ]
-    return add_all([term[:1] for term in terms] + got, jnp.float32)[0]
+    moves, arrived = plan.z_moves(), []
+    for group in plan.z_groups(split):
+        arrived += yield [
+            (add_all([term[k + 1 : k + 2] for term in terms]), moves[k]) for k in group
+        ]
+    return add_all([term[:1] for term in terms] + arrived, jnp.float32)[0]
 
 
 def total_steps(plan, value, halves=False):
@@ -211,14 +218,12 @@
     else:
         (got,) = yield [(value, plan.flip_core())]
         value = value + got
-    moves = [
-        plan.pairs(lambda z, y, c, x: (z, y, c, 1 - x)),
-        plan.pairs(lambda z, y, c, x: (z, 1 - y, c, x)),
-    ]
+    moves = [plan.pairs(lambda z, y, c, x: (z, y, c, 1 - x))]
     bit = 1
     while bit < plan.z:
         moves.append(plan.flip_z(bit))
         bit *= 2
+    moves.append(plan.pairs(lambda z, y, c, x: (z, 1 - y, c, x)))
     for pairs in moves:
         (got,) = yield [(value, pairs)]
         value = value + got
@@ -229,10 +234,14 @@
 
 
 def total_over_devices(plan, value):
-    travel, clock = Travel("small_sum", total_steps(plan, value)), Clock()
+    travel = Travel("small_sum", total_steps(plan, value))
     while travel.wanted:
-        clock.start([travel])
-        clock.wait([travel])
+        with jax.named_scope(travel.name):
+            got = [send(v, pairs) for v, pairs in travel.wanted]
+        try:
+            travel.wanted = travel.steps.send(got)
+        except StopIteration as end:
+            travel.wanted, travel.result = None, end.value
     return travel.result
 
 
@@ -399,18 +408,19 @@
 
 
 def pair_probs(stacked_queries, keys, allowed):
-    scores = rows_by_rows(stacked_queries, keys) * HD ** (-0.5)
+    scores = rows_by_rows(keys, stacked_queries) * HD ** (-0.5)
     scores = jnp.where(allowed, scores, masked_score)
-    raised = jnp.exp(scores - jnp.max(scores, -1, keepdims=True))
-    return raised * (1.0 / jnp.sum(raised, -1, keepdims=True))
+    raised = jnp.exp(scores - jnp.max(scores, 0, keepdims=True))
+    return raised * (1.0 / jnp.sum(raised, 0, keepdims=True))
 
 
 def allowed_pairs(column_ref, row_ref):
     same = column_ref[0] == row_ref[0]
     shape = same.shape
-    causal = lax.broadcasted_iota(jnp.int32, shape, 1) <= lax.broadcasted_iota(jnp.int32, shape, 0)
-    one = (same & causal).astype(jnp.float32)
-    return jnp.concatenate([one, one]) > 0.5
+    causal = lax.broadcasted_iota(jnp.int32, shape, 0) <= (
+        lax.broadcasted_iota(jnp.int32, shape, 1) % LEN
+    )
+    return same & causal
 
 
 def attend_kernel(groups, pairs, column_ref, row_ref, qkv_ref, context_ref):
@@ -419,7 +429,7 @@
         for pair in range(pairs):
             queries, keys, values = pair_blocks(qkv_ref, 0, group, pair, pairs)
             probs = pair_probs(both_heads(queries), keys, allowed).astype(jnp.bfloat16)
-            context = own_columns(matmul(probs, values))
+            context = own_columns(rows_of_both(probs, values))
             start = (group * pairs + pair) * PAIR
             context_ref[:, start : start + PAIR] = context.astype(jnp.bfloat16)
 
@@ -434,12 +444,13 @@
             d_context = both_heads(d_context_ref[:, start : start + PAIR])
             queries = both_heads(queries)
             probs = pair_probs(queries, keys, allowed)
-            d_probs = rows_by_rows(d_context, values)
-            d_values = rows_of_both(probs.astype(jnp.bfloat16), d_context)
-            mean = jnp.sum(probs * d_probs, -1, keepdims=True)
-            d_scores = (probs * (d_probs - mean)).astype(jnp.bfloat16)
-            d_queries = own_columns(matmul(d_scores, keys)) * HD ** (-0.5)
-            d_keys = rows_of_both(d_scores, queries) * HD ** (-0.5)
+            d_probs = rows_by_rows(values, d_context)
+            d_values = matmul(probs.astype(jnp.bfloat16), d_context)
+            weighted = probs * d_probs
+            mean = jnp.sum(weighted, 0, keepdims=True)
+            d_scores = (weighted - probs * mean).astype(jnp.bfloat16)
+            d_queries = own_columns(rows_of_both(d_scores, keys)) * HD ** (-0.5)
+            d_keys = matmul(d_scores, queries) * HD ** (-0.5)
             start = group * 3 * span + pair * PAIR
             for part, value in enumerate((d_queries, d_keys, d_values)):
                 at = start + part * span
@@ -457,7 +468,7 @@
         grid=(count,),
         in_specs=[
             pl.BlockSpec((1, LEN, 1), lambda i: (i, 0, 0)),
-            pl.BlockSpec((1, 1, LEN), lambda i: (i, 0, 0)),
+            pl.BlockSpec((1, 1, 2 * LEN), lambda i: (i, 0, 0)),
             rows(columns),
         ]
         + [rows(other.shape[1]) for other in others],
@@ -468,7 +479,7 @@
             bytes_accessed=scale * qkv.size * 2,
             transcendentals=count * LEN * LEN * columns // (3 * HD),
         ),
-    )(segments[:, :, None], segments[:, None, :], qkv, *others)
+    )(segments[:, :, None], jnp.tile(segments, (1, 2))[:, None, :], qkv, *others)
 
 
 class Spread:
@@ -628,48 +639,55 @@
     )[0]
 
 
+def gelu_and_slope(value):
+    scale, cubic = (2.0 / np.pi) ** 0.5, 0.044715
+    square = value * value
+    bent = jnp.tanh(value * (scale + scale * cubic * square))
+    half = 0.5 * bent + 0.5
+    inner = value * (scale + 3.0 * scale * cubic * square)
+    return value * half, half + (0.5 - 0.5 * bent * bent) * inner
+
+
 def hidden_forward(rows, spread, block):
     count, deep = rows.shape
     wide = spread.shape[1]
     if not spread.aligned or wide % block:
-        up_pre = matmul(rows, spread.matrix())
-        return up_pre, jax.nn.gelu(up_pre).astype(jnp.bfloat16)
+        gelu, slope = gelu_and_slope(matmul(rows, spread.matrix()))
+        return gelu.astype(jnp.bfloat16), slope.astype(jnp.bfloat16)
 
     def body(inputs, matrices, results):
         up_pre = matmul(inputs[0][...], matrices[0][:, step_slice(block)])
-        results[0][...] = up_pre
-        results[1][...] = jax.nn.gelu(up_pre).astype(jnp.bfloat16)
+        gelu, slope = gelu_and_slope(up_pre)
+        results[0][...] = gelu.astype(jnp.bfloat16)
+        results[1][...] = slope.astype(jnp.bfloat16)
 
     return with_matrices(
         spread.plan,
         body,
         [spread],
         [(rows, (count, deep), fixed)],
-        [
-            ((count, wide), jnp.float32, (count, block), by_columns),
-            ((count, wide), jnp.bfloat16, (count, block), by_columns),
-        ],
+        [((count, wide), jnp.bfloat16, (count, block), by_columns)] * 2,
         wide // block,
         2 * count * deep * wide,
     )
 
 
-def hidden_back(d_out, up_pre, spread, block):
-    count, wide = up_pre.shape
+def hidden_back(d_out, slope, spread, block):
+    count, wide = slope.shape
     if not spread.aligned or wide % block:
         d_activated = matmul_t(d_out, spread.matrix())
-        return jax.vjp(jax.nn.gelu, up_pre)[1](d_activated)[0].astype(jnp.bfloat16)
+        return (d_activated * slope.astype(jnp.float32)).astype(jnp.bfloat16)
 
     def body(inputs, matrices, results):
         d_activated = rows_by_rows(inputs[0][...], matrices[0][step_slice(block), :])
-        slope = jax.vjp(jax.nn.gelu, inputs[1][...])[1](d_activated)[0]
-        results[0][...] = slope.astype(jnp.bfloat16)
+        d_up = d_activated * inputs[1][...].astype(jnp.float32)
+        results[0][...] = d_up.astype(jnp.bfloat16)
 
     return with_matrices(
         spread.plan,
         body,
         [spread],
-        [(d_out, d_out.shape, fixed), (up_pre, (count, block), by_columns)],
+        [(d_out, d_out.shape, fixed), (slope, (count, block), by_columns)],
         [((count, wide), jnp.bfloat16, (count, block), by_columns)],
         wide // block,
         2 * count * d_out.shape[1] * wide,
@@ -888,6 +906,7 @@
 
 
 BY_COLUMNS = ("entry", "up")
+SPLITS = {"up": ((0, 1), (2,)), "exit": ((0,), (1, 2))}
 
 
 def per_device(
@@ -920,34 +939,44 @@
     segments = lax.dynamic_slice_in_dim(segment_ids, lax.axis_index("mp") * own_seqs, own_seqs)
     row_games = lax.dynamic_slice_in_dim(jnp.repeat(game_ids, LEN), row_start, own_rows)
 
-    clock = Clock()
+    clock = Clock(step_count.astype(jnp.float32))
     masters = {"entry": entry_weight, "exit": exit_weight, "up": up_weight, "down": down_weight}
     rows_here, half_wide = entry_weight.shape[1:]
     halves = {name: value.astype(jnp.bfloat16) for name, value in masters.items()}
     down_half = down_weight.shape[1] // 2
-    shards = {
-        "entry": halves["entry"].transpose(1, 0, 2).reshape(rows_here, 3 * half_wide),
-        "exit": halves["exit"],
-        "up": halves["up"],
-        "down_a": halves["down"][:, :down_half],
-        "down_b": halves["down"][:, down_half:],
+    entry_shard = halves["entry"].transpose(1, 0, 2).reshape(rows_here, 3 * half_wide)
+    paths = {
+        name: Travel("gather_" + name, gather_shards(plan, shard, split))
+        for name, shard, split in (
+            ("entry", entry_shard, ()),
+            ("up", halves["up"], ((0, 1), (2,))),
+            ("down", halves["down"], ()),
+        )
     }
-    paths = {
-        name: Travel("gather_" + name, gather_shards(plan, shard))
-        for name, shard in shards.items()
-        if name != "up"
-    }
-    up_gathered = lax.all_gather(shards["up"], AXES, axis=0)
+    game_match = (row_games[:, None] == jnp.arange(GAMES)[None, :]).astype(jnp.float32)
+    flag_float = valid_flags.astype(jnp.float32)
+    local_counts = jnp.sum(game_match * jnp.sum(flag_float, -1, keepdims=True), 0)
+    exit_rows, wide = exit_weight.shape
+    tens = jnp.floor(local_counts / 64.0)
+    pair = jnp.concatenate([tens, local_counts - 64.0 * tens]).astype(jnp.bfloat16)
+    below = jnp.zeros((16 - exit_rows % 16, wide), jnp.bfloat16).at[0, : 2 * GAMES].set(pair)
+    gathered = lax.all_gather(jnp.concatenate([halves["exit"], below]), ("mp", "dp"), axis=0)
+    exit_all = gathered[:, :exit_rows].reshape(-1, wide)
+    pairs_all = jnp.sum(gathered[:, exit_rows, : 2 * GAMES].astype(jnp.float32), 0)
+    counts_all = 64.0 * pairs_all[:GAMES] + pairs_all[GAMES:]
+    inverse = 1.0 / (GAMES * jnp.maximum(counts_all, 1.0))
+    token_scale = jnp.sum(game_match * inverse[None, :], -1)
+
     slots = jnp.asarray(path_table(plan), jnp.int32)[here]
 
     def chosen(names):
         return [paths[name] for name in names.split() if paths[name].wanted]
 
-    def start(names, more=()):
+    def start(names, *more):
         return clock.start(chosen(names), more)
 
-    def wait(names):
-        clock.wait([path for path in chosen(names) if path.going])
+    def wait(names, *more):
+        return clock.wait([path for path in chosen(names) if path.going], more)
 
     def finish(name):
         while paths[name].wanted:
@@ -955,53 +984,41 @@
             wait(name)
         return paths[name].result
 
-    def whole(*names):
-        parts = [(finish(name), slots) for name in names]
-        return Spread(plan, parts, names[0] in BY_COLUMNS)
-
-    game_match = (row_games[:, None] == jnp.arange(GAMES)[None, :]).astype(jnp.float32)
-    flag_float = valid_flags.astype(jnp.float32)
-    local_counts = jnp.sum(game_match * jnp.sum(flag_float, -1, keepdims=True), 0)
-    paths["games"] = Travel("game_counts", total_steps(plan, local_counts), True)
-
-    start("games entry")
-    resid, gains = clock.hold((tokens.astype(jnp.float32), norm_params))
+    def whole(name):
+        return Spread(plan, [(finish(name), slots)], name in BY_COLUMNS)
+
+
+    resid, gains = start("entry", tokens.astype(jnp.float32), norm_params)
     normed_one = layer_norm(resid, gains[0], gains[3]).astype(jnp.bfloat16)
-    clock.also(normed_one)
-    wait("entry games")
-    start("entry exit")
-    wait("entry exit")
-    start("entry exit")
-    wait("entry exit")
-    (normed_one,) = start("entry down_a", (normed_one,))
+    (normed_one,) = wait("entry", normed_one)
+    start("entry up")
+    wait("entry up")
+    start("entry up")
+    wait("entry up")
+    start("entry up")
     wait("entry")
-    (normed_one,) = start("exit games", (normed_one,))
+    (normed_one,) = start("down", normed_one)
     entry_all = whole("entry")
     projected = project(normed_one, entry_all, 768)
-    clock.also(projected)
-    wait("down_a exit games")
-    (projected,) = start("down_a down_b exit", (projected,))
+    (projected,) = wait("up down", projected)
+    (projected,) = start("up", projected)
     context = attend_call(
         attend_kernel, segments, projected, [], tokens.shape[1], plan.mp, 2
     )
-    clock.also(context)
-    wait("exit down_a down_b")
-    (context,) = start("down_a down_b games", (context,))
-    exit_all = whole("exit").matrix()
     after_attn = resid + matmul(context, exit_all)
     normed_two = layer_norm(after_attn, norm_params[1], norm_params[4]).astype(jnp.bfloat16)
-    clock.also(normed_two)
-    wait("down_a down_b games")
-    start("down_a down_b games")
-    up_all = Spread(plan, [([up_gathered], jnp.arange(plan.n, dtype=jnp.int32))], True)
-    up_pre, activated = hidden_forward(normed_two, up_all, 512)
-    wait("down_a down_b games")
-    start("down_b games")
-    wait("down_b games")
-    counts_all = finish("games")
-    inverse = 1.0 / (GAMES * jnp.maximum(counts_all, 1.0))
-    token_scale = jnp.sum(game_match * inverse[None, :], -1)
-    down_all = whole("down_a", "down_b")
+    after_attn, normed_two = wait("up", after_attn, normed_two)
+    (normed_two,) = start("up down", normed_two)
+    wait("up")
+    (normed_two,) = start("", normed_two)
+    up_all = whole("up")
+    activated, slope = hidden_forward(normed_two, up_all, 512)
+    activated, slope = wait("down", activated, slope)
+    start("down")
+    wait("down")
+    start("down")
+    wait("down")
+    down_all = whole("down")
     after_mlp = hidden_out(activated, after_attn, down_all, 320)
     final_norm = layer_norm(after_mlp, norm_params[2], norm_params[5]).astype(jnp.bfloat16)
     head_half = head_weight.astype(jnp.bfloat16)
@@ -1018,82 +1035,82 @@
     d_mlp_out = d_mlp_in.astype(jnp.bfloat16)
 
     def leave(name, left, right, block):
-        rows, width = shards[name].shape
+        rows = {"entry": rows_here, "exit": exit_weight.shape[0], "up": rows_here}
+        by_columns = name in BY_COLUMNS
+        width = right.shape[1] // (plan.mp if by_columns else 1)
+        part = (width, scatter_counts(plan), slots)
         (pieces,) = weight_grad(
             plan,
             left,
             right,
-            rows,
-            [(width, scatter_counts(plan), slots)],
-            name in BY_COLUMNS,
+            rows.get(name, down_weight.shape[0]),
+            [part],
+            by_columns,
             block,
         )
-        paths[name] = Travel("scatter_" + name, scatter_shards(plan, pieces))
-
-    def waiting(name):
-        return [value for value, _ in paths[name].wanted]
-
+        paths[name] = Travel(
+            "scatter_" + name,
+            scatter_shards(plan, pieces, SPLITS.get(name, ())),
+        )
+
+    leave("down_a", activated, d_mlp_out[:, :down_half], 1280)
+    d_mlp_out, d_logits = start("down_a", d_mlp_out, d_logits)
+    d_mlp_out, d_logits = wait("down_a", d_mlp_out, d_logits)
+    d_mlp_out, d_logits = start("down_a", d_mlp_out, d_logits)
+    leave("down_b", activated, d_mlp_out[:, down_half:], 1280)
     head_rows = head_weight.shape[0]
-    leave("down_a", activated, d_mlp_out[:, :down_half], 1280)
-    d_mlp_out, d_logits = start("down_a", (d_mlp_out, d_logits))
-    wait("down_a")
-    d_mlp_out, d_logits = start("down_a", (d_mlp_out, d_logits))
-    leave("down_b", activated, d_mlp_out[:, down_half:], 1280)
     d_head = jnp.pad(contract(d_logits, final_norm), ((0, head_rows % 2), (0, 0)))
-    paths["head"] = Travel("sum_head", total_steps(plan, d_head, halves=True), True)
-    clock.also(*waiting("down_b"))
-    wait("down_a")
-    (d_mlp_out,) = start("down_a down_b head", (d_mlp_out,))
-    d_up_pre = hidden_back(d_mlp_out, up_pre, down_all, 512)
-    clock.also(d_up_pre)
-    wait("down_a down_b head")
-    (d_up_pre,) = start("down_a down_b head", (d_up_pre,))
+    d_mlp_out, d_head = wait("down_a", d_mlp_out, d_head)
+    paths["head"] = Travel("sum_head", total_steps(plan, d_head, halves=True))
+    d_mlp_out, *late = start("down_a down_b head", d_mlp_out, *masters.values())
+    d_up_pre = hidden_back(d_mlp_out, slope, down_all, 512)
+    weight_local = jnp.stack([jnp.sum(master * master) for master in late])
+    d_up_pre, weight_local = wait("down_a down_b head", d_up_pre, weight_local)
+    (d_up_pre,) = start("down_a down_b head", d_up_pre)
     leave("up", normed_two, d_up_pre, 2560)
-    clock.also(*waiting("up"))
-    wait("down_a down_b head")
-    (d_up_pre,) = start("down_b up head", (d_up_pre,))
+    (d_up_pre,) = wait("down_a down_b head", d_up_pre)
+    (d_up_pre,) = start("down_b up head", d_up_pre)
     d_normed_two = project_back(d_up_pre, up_all, 256)
-    clock.also(d_normed_two)
-    wait("down_b up head")
-    (d_normed_two,) = start("down_b up head", (d_normed_two,))
+    (d_normed_two,) = wait("down_b up head", d_normed_two)
+    (d_normed_two,) = start("down_b up", d_normed_two)
     d_ln_two, d_gain_two, d_shift_two = norm_back(
         after_attn, norm_params[1], norm_params[4], d_normed_two
     )
     d_attn_out = (d_mlp_in + d_ln_two).astype(jnp.bfloat16)
     leave("exit", context, d_attn_out, 1280)
     d_context = matmul_t(d_attn_out, exit_all).astype(jnp.bfloat16)
-    clock.also(d_context, *waiting("exit"))
-    wait("down_b up head")
-    (d_context,) = start("up exit head", (d_context,))
+    (d_context,) = wait("down_b up", d_context)
+    (d_context,) = start("up exit", d_context)
+    (d_context,) = wait("exit", d_context)
+    (d_context,) = start("exit head", d_context)
     d_projected = attend_call(
         attend_back_kernel, segments, projected, [d_context], projected.shape[1], plan.mp, 5
     )
-    clock.also(d_projected)
-    wait("up exit head")
-    (d_projected,) = start("up exit head", (d_projected,))
+    (d_projected,) = wait("up exit head", d_projected)
+    (d_projected,) = start("exit head", d_projected)
     leave("entry", normed_one, d_projected, 1920)
-    clock.also(*waiting("entry"))
-    wait("exit head")
-    (d_projected,) = start("entry", (d_projected,))
-    wait("entry")
-    (d_projected,) = start("entry exit", (d_projected,))
+    (d_projected,) = wait("exit head", d_projected)
+    (d_projected,) = start("entry", d_projected)
+    (d_projected,) = wait("entry", d_projected)
+    (d_projected,) = start("entry up exit", d_projected)
     d_normed_one = project_back(d_projected, entry_all, 256)
+    (d_normed_one,) = wait("entry up exit", d_normed_one)
+    (d_normed_one,) = start("entry up exit", d_normed_one)
     _, d_gain_one, d_shift_one = norm_back(resid, norm_params[0], norm_params[3], d_normed_one)
-    clock.also(d_gain_one, d_shift_one)
-    wait("entry exit up")
-    start("entry exit")
-    wait("entry exit")
-    start("entry")
-    wait("entry")
-    reds = {name: finish(name) for name in shards}
+    d_gain_one, d_shift_one = wait("entry up exit", d_gain_one, d_shift_one)
+    start("entry head")
+    wait("entry head")
     red_head = finish("head")[:head_rows]
+    names = ("entry", "exit", "up", "down_a", "down_b")
+    reds = {name: finish(name) for name in names}
 
     masters = [entry_weight, exit_weight, up_weight, down_weight, head_weight]
     states = [entry_state, exit_state, up_state, down_state, head_state]
-    local_square = sum(jnp.sum(reds[name] * reds[name]) for name in shards)
-    weight_local = jnp.stack([jnp.sum(master * master) for master in masters[:4]])
+    local_square = sum(jnp.sum(reds[name] * reds[name]) for name in names)
     wide = norm_params.shape[1]
-    scalars = jnp.concatenate([jnp.stack([loss_local, local_square]), weight_local])
+    scalars = jnp.concatenate(
+        [jnp.stack([loss_local, local_square]), weight_local, clock.token]
+    )
     small = total_over_devices(
         plan,
         jnp.stack(

time: 791 us -> 699 us (0.88)
  waiting for transfers between devices: 243 us -> 193 us
  starting transfers between devices: 123 us -> 103 us
  Pallas kernels: 234 us -> 220 us
    ppermute x101 -> x86, waiting for transfers between devices: 243 us -> 193 us  [send(): return lax.ppermute(value, AXES, pairs)]
    ppermute x101 -> x86, starting transfers between devices: 123 us -> 103 us  [send(): return lax.ppermute(value, AXES, pairs)]
    unnamed x127 -> x173, local copies, waits for them, and re-layouts: 18.9 us -> 23.2 us
    reduce_sum x9 -> x10, other arithmetic: 21.1 us -> 18.9 us  [the longest x5 14.9 us: per_device(): local_square = sum((jnp.sum(reds[name] * reds[name]) for name in names))]
  transfers between devices with their start and end apart: 102 -> 87, of which waited for: 34 -> 34; matrix products, arithmetic and copies ran while one was open for 16% -> 11% of each run, Pallas kernels for 24% -> 25%
where the time goes in v2:
time: 699 us; the launch traced here: 693 us
  Pallas kernels  220 us (31%)
  waiting for transfers between devices  193 us (28%)
  starting transfers between devices  103 us (15%)
  other arithmetic  101 us (14%)
  local copies, waits for them, and re-layouts  35.4 us (5%)
  between operations  26.3 us (4%)
  matrix products  14 us (2%)
    ppermute x86, waiting for transfers between devices, send(): return lax.ppermute(value, AXES, pairs)  193 us
    pallas_call x6, Pallas kernels, with_matrices(): pl.pallas_call(kernel, out_shape=[jax.ShapeDtypeStruct(shape, dtype) for...  113 us
    ppermute x86, starting transfers between devices, send(): return lax.ppermute(value, AXES, pairs)  103 us
    pallas_call x4, Pallas kernels, weight_grad(): pl.pallas_call(kernel, out_shape=[jax.ShapeDtypeStruct((count, rows, widt...  55 us
    convert_element_type x15, other arithmetic, add_all(): return total.astype(dtype)  45.6 us
    pallas_call x2, Pallas kernels, attend_call(): pl.pallas_call(functools.partial(kernel, groups, pairs), out_shape=jax.Sh...  30.6 us
    unnamed x173, local copies, waits for them, and re-layouts  23.2 us
    reduce_sum x5, other arithmetic, per_device(): local_square = sum((jnp.sum(reds[name] * reds[name]) for name in names))  14.9 us
  transfers between devices with their start and end apart: 87, of which 34 were waited for; matrix products, arithmetic and copies ran while one was open for 11% of the time, Pallas kernels for 25%

profile of v2, /device:TPU:0, one launch (start us, length us, event | category | flops | bytes accessed | tf_op | source)
XLA Modules:
  0.0 693.4 jit_solution(16145792990659354584)
XLA Ops:
  23.0 5.4 collective-permute-done
  28.4 12.8 %collective-permute-done.1 = bf16[1,80,1920]{2,1,0:T(8,128)(2,1)} collective-permute-done((bf16[1,80,1920]{2,1,0:T(8,128)(2,1)}, bf16[1,80,1920]{2,1,0:T(8,128)(2,1)}, u32[]{:S(2)}, u32[]{:S(2)}) %collective-permute-start.1) | collective-permute-done | bytes 307232 | tf_op jit(solution)/shard_map/gather_entry/ppermute | solution.py:115
  47.4 6.7 collective-permute-start.5
  55.1 20.7 %collective-permute-done.5 = bf16[1,80,2560]{2,1,0:T(8,128)(2,1)S(1)} collective-permute-done((bf16[1,80,2560]{2,1,0:T(8,128)(2,1)S(1)}, bf16[1,80,2560]{2,1,0:T(8,128)(2,1)S(1)}, u32[]{:S(2)}, u32[]{:S(2)}) %collective-permute-start.5) | collective-permute-done | bytes 409632 | tf_op jit(solution)/shard_map/gather_up/ppermute | solution.py:115
  80.9 18.4 %collective-permute-done.10 = bf16[1,80,2560]{2,1,0:T(8,128)(2,1)S(1)} collective-permute-done((bf16[1,80,2560]{2,1,0:T(8,128)(2,1)S(1)}, bf16[1,80,2560]{2,1,0:T(8,128)(2,1)S(1)}, u32[]{:S(2)}, u32[]{:S(2)}) %collective-permute-start.10) | collective-permute-done | bytes 409632 | tf_op jit(solution)/shard_map/gather_up/ppermute | solution.py:115
  108.6 11.3 %collective-permute-start.15 = (bf16[1,160,1280]{2,1,0:T(8,128)(2,1)S(1)}, bf16[1,160,1280]{2,1,0:T(8,128)(2,1)S(1)}, u32[]{:S(2)}, u32[]{:S(2)}) collective-permute-start(bf16[1,160,1280]{2,1,0:T(8,128)(2,1)S(1)} %convert_bitcast_fusion.1), channel_id=1, source_target_pairs={{0,8},{1,9},{2,10},{3,11},{4,12},{5,13},{6,14},{7,15},{8,0},{9,1},... | collective-permute-start | bytes 1228808 | tf_op jit(solution)/shard_map/gather_down/ppermute | solution.py:115
  122.3 15.0 %shard_map.348.qkv_ref = bf16[640,3840]{1,0:T(8,128)(2,1)} custom-call(s32[32]{0:T(128)} %dynamic-slice_bitcast_fusion.slots_ref, bf16[640,1280]{1,0:T(8,128)(2,1)} %add_convert_fusion.6.refs_0_.left_ref, bf16[4,80,1920]{2,1,0:T(8,128)(2,1)} %copy-done.54, bf16[4,80,1920]{2,1,0:T(8,128)(2,1)} %copy-done.78, ...), custom_call_target="tpu_custom_call" | custom-call | flops 6291456000 | bytes 16384000 | tf_op jit(solution)/shard_map/pallas_call | solution.py:562
  140.7 10.0 %collective-permute-done.16 = bf16[1,160,1280]{2,1,0:T(8,128)(2,1)S(1)} collective-permute-done((bf16[1,160,1280]{2,1,0:T(8,128)(2,1)S(1)}, bf16[1,160,1280]{2,1,0:T(8,128)(2,1)S(1)}, u32[]{:S(2)}, u32[]{:S(2)}) %collective-permute-start.16) | collective-permute-done | bytes 409632 | tf_op jit(solution)/shard_map/gather_down/ppermute | solution.py:115
  151.8 11.3 %shard_map.349 = bf16[640,1280]{1,0:T(8,128)(2,1)} custom-call(s32[4,160,1]{2,1,0:T(8,128)} %copy.53.column_ref, s32[4,1,320]{2,1,0:T(1,128)} %tile.5.row_ref, bf16[640,3840]{1,0:T(8,128)(2,1)} %shard_map.348.qkv_ref), custom_call_target="tpu_custom_call" | custom-call | flops 524288000 | bytes 9830400 | tf_op jit(solution)/shard_map/pallas_call | solution.py:465
  180.4 23.9 %shard_map.350 = (bf16[640,5120]{1,0:T(8,128)(2,1)}, bf16[640,5120]{1,0:T(8,128)(2,1)}) custom-call(s32[32]{0:T(128)} %dynamic-slice_bitcast_fusion.slots_ref, bf16[640,1280]{1,0:T(8,128)(2,1)} %add_convert_fusion.5.refs_0_.left_ref, bf16[4,80,2560]{2,1,0:T(8,128)(2,1)} %copy-done.26, bf16[4,80,2560]{2,1,0:T(8,128)(2,1)} %collective-permute-done.13.refs_2_, ...), custom_call_target="tpu_custom_call" | custom-call | flops 8388608000 | bytes 27852800 | tf_op jit(solution)/shard_map/pallas_call | solution.py:562
  204.3 8.0 %collective-permute-done.21.refs_3_ = bf16[4,160,1280]{2,1,0:T(8,128)(2,1)} collective-permute-done((bf16[4,160,1280]{2,1,0:T(8,128)(2,1)}, bf16[4,160,1280]{2,1,0:T(8,128)(2,1)}, u32[]{:S(2)}, u32[]{:S(2)}) %collective-permute-start.21) | collective-permute-done | bytes 1638432 | tf_op jit(solution)/shard_map/gather_down/ppermute | solution.py:115
  214.0 19.7 %collective-permute-done.25.refs_5_ = bf16[4,160,1280]{2,1,0:T(8,128)(2,1)S(1)} collective-permute-done((bf16[4,160,1280]{2,1,0:T(8,128)(2,1)}, bf16[4,160,1280]{2,1,0:T(8,128)(2,1)S(1)}, u32[]{:S(2)}, u32[]{:S(2)}) %collective-permute-start.25) | collective-permute-done | bytes 1638432 | tf_op jit(solution)/shard_map/gather_down/ppermute | solution.py:115
  239.7 19.1 %shard_map.351 = f32[640,1280]{1,0:T(8,128)} custom-call(s32[32]{0:T(128)} %dynamic-slice_bitcast_fusion.slots_ref, bf16[640,5120]{1,0:T(8,128)(2,1)} %get-tuple-element.388.refs_0_.left_ref, f32[640,1280]{1,0:T(8,128)} %copy-done.2, bf16[4,160,1280]{2,1,0:T(8,128)(2,1)} %pad_maximum_fusion.1.refs_2_, bf16[4,160,1280]{2,1,0:T(8,128)(2,1)} %collective-permute-done.21.refs_3_, ...), custom_call_target="tpu_custom_call" | custom-call | flops 8388608000 | bytes 26214400 | tf_op jit(solution)/shard_map/pallas_call | solution.py:562
  270.9 11.6 %shard_map.352 = (bf16[16,160,640]{2,1,0:T(8,128)(2,1)}, bf16[12,160,640]{2,1,0:T(8,128)(2,1)}, bf16[4,160,640]{2,1,0:T(8,128)(2,1)}) custom-call(s32[32]{0:T(128)} %dynamic-slice_bitcast_fusion.slots_ref, bf16[640,5120]{1,0:T(8,128)(2,1)} %get-tuple-element.388.refs_0_.left_ref, bf16[640,640]{1,0:T(8,128)(2,1)} %slice.599.right_ref), custom_call_target="tpu_custom_call" | custom-call | flops 4194304000 | bytes 13926400 | tf_op jit(solution)/shard_map/pallas_call | solution.py:782
  283.1 5.3 collective-permute-done.30
  294.5 12.1 %shard_map.353 = (bf16[16,160,640]{2,1,0:T(8,128)(2,1)}, bf16[12,160,640]{2,1,0:T(8,128)(2,1)}, bf16[4,160,640]{2,1,0:T(8,128)(2,1)}) custom-call(s32[32]{0:T(128)} %dynamic-slice_bitcast_fusion.slots_ref, bf16[640,5120]{1,0:T(8,128)(2,1)} %get-tuple-element.388.refs_0_.left_ref, bf16[640,640]{1,0:T(8,128)(2,1)} %slice.481.right_ref), custom_call_target="tpu_custom_call" | custom-call | flops 4194304000 | bytes 13926400 | tf_op jit(solution)/shard_map/pallas_call | solution.py:782
  313.6 20.1 %shard_map.354.right_ref.refs_0_ = bf16[640,5120]{1,0:T(8,128)(2,1)} custom-call(s32[32]{0:T(128)} %dynamic-slice_bitcast_fusion.slots_ref, bf16[640,1280]{1,0:T(8,128)(2,1)} %copy-done.20, bf16[640,5120]{1,0:T(8,128)(2,1)} %get-tuple-element.437.refs_1_, bf16[4,160,1280]{2,1,0:T(8,128)(2,1)} %pad_maximum_fusion.1.refs_2_, ...), custom_call_target="tpu_custom_call" | custom-call | flops 8388608000 | bytes 27852800 | tf_op jit(solution)/shard_map/pallas_call | solution.py:562
  346.3 7.6 %collective-permute-start.38 = (bf16[1,160,640]{2,1,0:T(8,128)(2,1)S(1)}, bf16[1,160,640]{2,1,0:T(8,128)(2,1)S(1)}, u32[]{:S(2)}, u32[]{:S(2)}) collective-permute-start(bf16[1,160,640]{2,1,0:T(8,128)(2,1)S(1)} %get-tuple-element.450), channel_id=1, source_target_pairs={{0,8},{1,9},{2,10},{3,11},{4,12},{5,13},{6,14},{7,15},{8,0},{9,1},... | collective-permute-start | bytes 614408 | tf_op jit(solution)/shard_map/scatter_down_a/ppermute | solution.py:115
  357.5 17.1 %shard_map.355 = (bf16[16,80,2560]{2,1,0:T(8,128)(2,1)}, bf16[12,80,2560]{2,1,0:T(8,128)(2,1)}, bf16[4,80,2560]{2,1,0:T(8,128)(2,1)}) custom-call(s32[32]{0:T(128)} %dynamic-slice_bitcast_fusion.slots_ref, bf16[640,1280]{1,0:T(8,128)(2,1)} %add_convert_fusion.5.refs_0_.left_ref, bf16[640,5120]{1,0:T(8,128)(2,1)} %shard_map.354.right_ref.refs_0_), custom_call_target="tpu_custom_call" | custom-call | flops 8388608000 | bytes 21299200 | tf_op jit(solution)/shard_map/pallas_call | solution.py:782
  385.9 19.2 %shard_map.356 = f32[640,1280]{1,0:T(8,128)} custom-call(s32[32]{0:T(128)} %dynamic-slice_bitcast_fusion.slots_ref, bf16[640,5120]{1,0:T(8,128)(2,1)} %shard_map.354.right_ref.refs_0_, bf16[4,80,2560]{2,1,0:T(8,128)(2,1)} %copy-done.26, bf16[4,80,2560]{2,1,0:T(8,128)(2,1)} %collective-permute-done.13.refs_2_, ...), custom_call_target="tpu_custom_call" | custom-call | flops 8388608000 | bytes 22937600 | tf_op jit(solution)/shard_map/pallas_call | solution.py:562
  425.1 4.1 convolution_convert_fusion
  429.2 4.3 shard_map.357
  437.4 6.1 add_convert_fusion
  449.8 19.3 %shard_map.358.right_ref.refs_0_ = bf16[640,3840]{1,0:T(8,128)(2,1)} custom-call(s32[4,160,1]{2,1,0:T(8,128)} %copy.53.column_ref, s32[4,1,320]{2,1,0:T(1,128)} %tile.5.row_ref, bf16[640,3840]{1,0:T(8,128)(2,1)} %shard_map.348.qkv_ref, bf16[640,1280]{1,0:T(8,128)(2,1)} %convolution_convert_fusion.1.d_context_ref), custom_call_target="tpu_custom_call" | custom-call | flops 1310720000 | bytes 24576000 | tf_op jit(solution)/shard_map/pallas_call | solution.py:465
  469.1 13.4 %collective-permute-done.54 = bf16[4,80,2560]{2,1,0:T(8,128)(2,1)S(1)} collective-permute-done((bf16[4,80,2560]{2,1,0:T(8,128)(2,1)}, bf16[4,80,2560]{2,1,0:T(8,128)(2,1)S(1)}, u32[]{:S(2)}, u32[]{:S(2)}) %collective-permute-start.54) | collective-permute-done | bytes 1638432 | tf_op jit(solution)/shard_map/scatter_up/ppermute | solution.py:115
  492.6 14.2 %shard_map.359 = (bf16[16,80,1920]{2,1,0:T(8,128)(2,1)}, bf16[12,80,1920]{2,1,0:T(8,128)(2,1)}, bf16[4,80,1920]{2,1,0:T(8,128)(2,1)}) custom-call(s32[32]{0:T(128)} %dynamic-slice_bitcast_fusion.slots_ref, bf16[640,1280]{1,0:T(8,128)(2,1)} %add_convert_fusion.6.refs_0_.left_ref, bf16[640,3840]{1,0:T(8,128)(2,1)} %shard_map.358.right_ref.refs_0_), custom_call_target="tpu_custom_call" | custom-call | flops 6291456000 | bytes 16384000 | tf_op jit(solution)/shard_map/pallas_call | solution.py:782
  526.6 15.8 %shard_map.360 = f32[640,1280]{1,0:T(8,128)} custom-call(s32[32]{0:T(128)} %dynamic-slice_bitcast_fusion.slots_ref, bf16[640,3840]{1,0:T(8,128)(2,1)} %shard_map.358.right_ref.refs_0_, bf16[4,80,1920]{2,1,0:T(8,128)(2,1)} %copy-done.54, bf16[4,80,1920]{2,1,0:T(8,128)(2,1)} %copy-done.78, bf16[4,80,1920]{2,1,0:T(8,128)(2,1)} %collective-permute-done.4.refs_3_, ...), custom_call_target="tpu_custom_call" | custom-call | flops 6291456000 | bytes 18022400 | tf_op jit(solution)/shard_map/pallas_call | solution.py:562
  546.3 4.4 add_convert_fusion.8
  568.4 15.9 %collective-permute-done.70 = bf16[1,40,1280]{2,1,0:T(8,128)(2,1)S(1)} collective-permute-done((bf16[1,40,1280]{2,1,0:T(8,128)(2,1)S(1)}, bf16[1,40,1280]{2,1,0:T(8,128)(2,1)S(1)}, u32[]{:S(2)}, u32[]{:S(2)}) %collective-permute-start.70) | collective-permute-done | bytes 102432 | tf_op jit(solution)/shard_map/scatter_exit/ppermute | solution.py:115
  598.5 14.1 %collective-permute-done.73 = bf16[1,80,1920]{2,1,0:T(8,128)(2,1)S(1)} collective-permute-done((bf16[1,80,1920]{2,1,0:T(8,128)(2,1)S(1)}, bf16[1,80,1920]{2,1,0:T(8,128)(2,1)S(1)}, u32[]{:S(2)}, u32[]{:S(2)}) %collective-permute-start.73) | collective-permute-done | bytes 307232 | tf_op jit(solution)/shard_map/scatter_entry/ppermute | solution.py:115
  645.1 12.2 %shard_map.361 = (f32[2,3,80,640]{3,2,1,0:T(8,128)}, f32[2,40,1280]{2,1,0:T(8,128)}, f32[2,80,2560]{2,1,0:T(8,128)}, f32[2,160,1280]{2,1,0:T(8,128)}, f32[2,142,...) custom-call(f32[3]{0:T(128)} %pad_maximum_fusion.6.scalars_ref, ...), custom_call_target="tpu_custom_call" | custom-call | tf_op jit(solution)/shard_map/pallas_call | solution.py:872
  680.0 5.0 shard_map.362
  (477 shorter events, 262.9 us)
Async XLA Ops:
  7.2 157.4 %all-gather.3.cloned.1.call-start = ((), (), s32[]{:S(2)}) async-start(), calls=%async_computation | async-start | bytes 4055040 | tf_op jit(solution)/shard_map/all_gather | solution.py:963
  15.0 26.2 %collective-permute-start.1 = (bf16[1,80,1920]{2,1,0:T(8,128)(2,1)}, bf16[1,80,1920]{2,1,0:T(8,128)(2,1)}, u32[]{:S(2)}, u32[]{:S(2)}) collective-permute-start(bf16[1,80,1920]{2,1,0:T(8,128)(2,1)} %broadcast_in_dim_reshape.2), channel_id=1, source_target_pairs={{0,16},{1,17},{2,18},{3,19},{4,20},{5,21},{6,22},{7,23},{8,24},{9,... | collective-permute-start | bytes 921608 | tf_op jit(solution)/shard_map/gather_entry/ppermute | solution.py:115
  17.6 23.6 %collective-permute-start.2 = (bf16[1,80,1920]{2,1,0:T(8,128)(2,1)}, bf16[1,80,1920]{2,1,0:T(8,128)(2,1)}, u32[]{:S(2)}, u32[]{:S(2)}) collective-permute-start(bf16[1,80,1920]{2,1,0:T(8,128)(2,1)} %broadcast_in_dim_reshape.2), channel_id=1, source_target_pairs={{0,24},{1,25},{2,26},{3,27},{4,28},{5,29},{6,30},{7,31},{8,16},{9,... | collective-permute-start | bytes 921608 | tf_op jit(solution)/shard_map/gather_entry/ppermute | solution.py:115
  44.3 31.5 %collective-permute-start.3 = (bf16[4,80,1920]{2,1,0:T(8,128)(2,1)S(1)}, bf16[4,80,1920]{2,1,0:T(8,128)(2,1)S(1)}, u32[]{:S(2)}, u32[]{:S(2)}) collective-permute-start(bf16[4,80,1920]{2,1,0:T(8,128)(2,1)S(1)} %constant_dynamic-update-slice_fusion.refs_1_), channel_id=1, source_target_pairs={{0,4},{1,5},{2,3},{3,2},{4,0},{5,1},{6,7},{7,6},{8,12},{9,13},{10,... | collective-permute-start | bytes 3686408 | tf_op jit(solution)/shard_map/gather_entry/ppermute | solution.py:115
  45.9 29.9 %collective-permute-start.4 = (bf16[4,80,1920]{2,1,0:T(8,128)(2,1)S(1)}, bf16[4,80,1920]{2,1,0:T(8,128)(2,1)}, u32[]{:S(2)}, u32[]{:S(2)}) collective-permute-start(bf16[4,80,1920]{2,1,0:T(8,128)(2,1)S(1)} %constant_dynamic-update-slice_fusion.refs_1_), channel_id=1, source_target_pairs={{0,1},{1,0},{2,6},{3,7},{4,5},{5,4},{6,2},{7,3},{8,9},{9,8},{10,14... | collective-permute-start | bytes 3686408 | tf_op jit(solution)/shard_map/gather_entry/ppermute | solution.py:115
  47.4 28.4 %collective-permute-start.5 = (bf16[1,80,2560]{2,1,0:T(8,128)(2,1)S(1)}, bf16[1,80,2560]{2,1,0:T(8,128)(2,1)S(1)}, u32[]{:S(2)}, u32[]{:S(2)}) collective-permute-start(bf16[1,80,2560]{2,1,0:T(8,128)(2,1)S(1)} %convert_bitcast_fusion), channel_id=1, source_target_pairs={{0,8},{1,9},{2,10},{3,11},{4,12},{5,13},{6,14},{7,15},{8,0},{9,1},... | collective-permute-start | bytes 1228808 | tf_op jit(solution)/shard_map/gather_up/ppermute | solution.py:115
  75.8 24.8 %collective-permute-start.7 = (bf16[4,80,1920]{2,1,0:T(8,128)(2,1)S(1)}, bf16[4,80,1920]{2,1,0:T(8,128)(2,1)}, u32[]{:S(2)}, u32[]{:S(2)}) collective-permute-start(bf16[4,80,1920]{2,1,0:T(8,128)(2,1)S(1)} %collective-permute-done.3.refs_2_), channel_id=1, source_target_pairs={{0,1},{1,0},{2,6},{3,7},{4,5},{5,4},{6,2},{7,3},{8,9},{9,8},{10,14... | collective-permute-start | bytes 3686408 | tf_op jit(solution)/shard_map/gather_entry/ppermute | solution.py:115
  102.6 38.0 %collective-permute-start.13 = (bf16[4,80,2560]{2,1,0:T(8,128)(2,1)S(1)}, bf16[4,80,2560]{2,1,0:T(8,128)(2,1)}, u32[]{:S(2)}, u32[]{:S(2)}) collective-permute-start(bf16[4,80,2560]{2,1,0:T(8,128)(2,1)S(1)} %pad_maximum_fusion.refs_1_), channel_id=1, source_target_pairs={{0,4},{1,5},{2,3},{3,2},{4,0},{5,1},{6,7},{7,6},{8,12},{9,13},{10,... | collective-permute-start | bytes 4915208 | tf_op jit(solution)/shard_map/gather_up/ppermute | solution.py:115
  104.5 36.2 %collective-permute-start.14 = (bf16[4,80,2560]{2,1,0:T(8,128)(2,1)S(1)}, bf16[4,80,2560]{2,1,0:T(8,128)(2,1)}, u32[]{:S(2)}, u32[]{:S(2)}) collective-permute-start(bf16[4,80,2560]{2,1,0:T(8,128)(2,1)S(1)} %pad_maximum_fusion.refs_1_), channel_id=1, source_target_pairs={{0,1},{1,0},{2,6},{3,7},{4,5},{5,4},{6,2},{7,3},{8,9},{9,8},{10,14... | collective-permute-start | bytes 4915208 | tf_op jit(solution)/shard_map/gather_up/ppermute | solution.py:115
  108.6 32.1 %collective-permute-start.15 = (bf16[1,160,1280]{2,1,0:T(8,128)(2,1)S(1)}, bf16[1,160,1280]{2,1,0:T(8,128)(2,1)S(1)}, u32[]{:S(2)}, u32[]{:S(2)}) collective-permute-start(bf16[1,160,1280]{2,1,0:T(8,128)(2,1)S(1)} %convert_bitcast_fusion.1), channel_id=1, source_target_pairs={{0,8},{1,9},{2,10},{3,11},{4,12},{5,13},{6,14},{7,15},{8,0},{9,1},... | collective-permute-start | bytes 1228808 | tf_op jit(solution)/shard_map/gather_down/ppermute | solution.py:115
  119.9 30.9 %collective-permute-start.16 = (bf16[1,160,1280]{2,1,0:T(8,128)(2,1)S(1)}, bf16[1,160,1280]{2,1,0:T(8,128)(2,1)S(1)}, u32[]{:S(2)}, u32[]{:S(2)}) collective-permute-start(bf16[1,160,1280]{2,1,0:T(8,128)(2,1)S(1)} %convert_bitcast_fusion.1), channel_id=1, source_target_pairs={{0,16},{1,17},{2,18},{3,19},{4,20},{5,21},{6,22},{7,23},{8,24},{9,... | collective-permute-start | bytes 1228808 | tf_op jit(solution)/shard_map/gather_down/ppermute | solution.py:115
  120.1 30.7 %collective-permute-start.17 = (bf16[1,160,1280]{2,1,0:T(8,128)(2,1)S(1)}, bf16[1,160,1280]{2,1,0:T(8,128)(2,1)S(1)}, u32[]{:S(2)}, u32[]{:S(2)}) collective-permute-start(bf16[1,160,1280]{2,1,0:T(8,128)(2,1)S(1)} %convert_bitcast_fusion.1), channel_id=1, source_target_pairs={{0,24},{1,25},{2,26},{3,27},{4,28},{5,29},{6,30},{7,31},{8,16},{9,... | collective-permute-start | bytes 1228808 | tf_op jit(solution)/shard_map/gather_down/ppermute | solution.py:115
  173.6 38.7 %collective-permute-start.21 = (bf16[4,160,1280]{2,1,0:T(8,128)(2,1)}, bf16[4,160,1280]{2,1,0:T(8,128)(2,1)}, u32[]{:S(2)}, u32[]{:S(2)}) collective-permute-start(bf16[4,160,1280]{2,1,0:T(8,128)(2,1)} %pad_maximum_fusion.1.refs_2_), channel_id=1, source_target_pairs={{0,4},{1,5},{2,3},{3,2},{4,0},{5,1},{6,7},{7,6},{8,12},{9,13},{10,... | collective-permute-start | bytes 4915208 | tf_op jit(solution)/shard_map/gather_down/ppermute | solution.py:115
  175.2 37.2 %collective-permute-start.22 = (bf16[4,160,1280]{2,1,0:T(8,128)(2,1)}, bf16[4,160,1280]{2,1,0:T(8,128)(2,1)}, u32[]{:S(2)}, u32[]{:S(2)}) collective-permute-start(bf16[4,160,1280]{2,1,0:T(8,128)(2,1)} %pad_maximum_fusion.1.refs_2_), channel_id=1, source_target_pairs={{0,1},{1,0},{2,6},{3,7},{4,5},{5,4},{6,2},{7,3},{8,9},{9,8},{10,14... | collective-permute-start | bytes 4915208 | tf_op jit(solution)/shard_map/gather_down/ppermute | solution.py:115
  311.3 29.5 %collective-permute-start.36 = (bf16[12,160,640]{2,1,0:T(8,128)(2,1)}, bf16[12,160,640]{2,1,0:T(8,128)(2,1)}, u32[]{:S(2)}, u32[]{:S(2)}) collective-permute-start(bf16[12,160,640]{2,1,0:T(8,128)(2,1)} %get-tuple-element.434), channel_id=1, source_target_pairs={{0,2},{1,3},{2,0},{3,1},{4,6},{5,7},{6,4},{7,5},{8,10},{9,11},{10,... | collective-permute-start | bytes 7372808 | tf_op jit(solution)/shard_map/scatter_down_b/ppermute | solution.py:115
  311.3 28.7 %collective-permute-start.33 = (bf16[4,160,640]{2,1,0:T(8,128)(2,1)}, bf16[4,160,640]{2,1,0:T(8,128)(2,1)}, u32[]{:S(2)}, u32[]{:S(2)}) collective-permute-start(bf16[4,160,640]{2,1,0:T(8,128)(2,1)} %get-tuple-element.431), channel_id=1, source_target_pairs={{0,4},{1,5},{2,3},{3,2},{4,0},{5,1},{6,7},{7,6},{8,12},{9,13},{10,... | collective-permute-start | bytes 2457608 | tf_op jit(solution)/shard_map/scatter_down_a/ppermute | solution.py:115
  311.9 28.1 %collective-permute-start.34 = (bf16[4,160,640]{2,1,0:T(8,128)(2,1)}, bf16[4,160,640]{2,1,0:T(8,128)(2,1)}, u32[]{:S(2)}, u32[]{:S(2)}) collective-permute-start(bf16[4,160,640]{2,1,0:T(8,128)(2,1)} %get-tuple-element.432), channel_id=1, source_target_pairs={{0,1},{1,0},{2,6},{3,7},{4,5},{5,4},{6,2},{7,3},{8,9},{9,8},{10,14... | collective-permute-start | bytes 2457608 | tf_op jit(solution)/shard_map/scatter_down_a/ppermute | solution.py:115
  313.1 26.9 %collective-permute-start.35 = (bf16[4,160,640]{2,1,0:T(8,128)(2,1)}, bf16[4,160,640]{2,1,0:T(8,128)(2,1)}, u32[]{:S(2)}, u32[]{:S(2)}) collective-permute-start(bf16[4,160,640]{2,1,0:T(8,128)(2,1)} %get-tuple-element.433), channel_id=1, source_target_pairs={{0,2},{1,3},{2,0},{3,1},{4,6},{5,7},{6,4},{7,5},{8,10},{9,11},{10,... | collective-permute-start | bytes 2457608 | tf_op jit(solution)/shard_map/scatter_down_b/ppermute | solution.py:115
  313.1 26.9 %collective-permute-start.37 = (f32[71,1280]{1,0:T(8,128)}, f32[71,1280]{1,0:T(8,128)S(1)}, u32[]{:S(2)}, u32[]{:S(2)}) collective-permute-start(f32[71,1280]{1,0:T(8,128)} %slice_select_fusion), channel_id=1, source_target_pairs={{0,2},{1,3},{2,0},{3,1},{4,6},{5,7},{6,4},{7,5},{8,10},{9,11},{10,... | collective-permute-start | bytes 1090568 | tf_op jit(solution)/shard_map/sum_head/ppermute | solution.py:115
  345.4 29.3 %collective-permute-start.41 = (bf16[4,160,640]{2,1,0:T(8,128)(2,1)S(1)}, bf16[4,160,640]{2,1,0:T(8,128)(2,1)S(1)}, u32[]{:S(2)}, u32[]{:S(2)}) collective-permute-start(bf16[4,160,640]{2,1,0:T(8,128)(2,1)S(1)} %add_convert_fusion.13), channel_id=1, source_target_pairs={{0,1},{1,0},{2,6},{3,7},{4,5},{5,4},{6,2},{7,3},{8,9},{9,8},{10,14... | collective-permute-start | bytes 2457608 | tf_op jit(solution)/shard_map/scatter_down_b/ppermute | solution.py:115
  346.3 28.3 %collective-permute-start.38 = (bf16[1,160,640]{2,1,0:T(8,128)(2,1)S(1)}, bf16[1,160,640]{2,1,0:T(8,128)(2,1)S(1)}, u32[]{:S(2)}, u32[]{:S(2)}) collective-permute-start(bf16[1,160,640]{2,1,0:T(8,128)(2,1)S(1)} %get-tuple-element.450), channel_id=1, source_target_pairs={{0,8},{1,9},{2,10},{3,11},{4,12},{5,13},{6,14},{7,15},{8,0},{9,1},... | collective-permute-start | bytes 614408 | tf_op jit(solution)/shard_map/scatter_down_a/ppermute | solution.py:115
  381.0 24.1 %collective-permute-start.46 = (bf16[12,80,2560]{2,1,0:T(8,128)(2,1)}, bf16[12,80,2560]{2,1,0:T(8,128)(2,1)}, u32[]{:S(2)}, u32[]{:S(2)}) collective-permute-start(bf16[12,80,2560]{2,1,0:T(8,128)(2,1)} %get-tuple-element.466), channel_id=1, source_target_pairs={{0,2},{1,3},{2,0},{3,1},{4,6},{5,7},{6,4},{7,5},{8,10},{9,11},{10,... | collective-permute-start | bytes 14745608 | tf_op jit(solution)/shard_map/scatter_up/ppermute | solution.py:115
  381.0 24.1 %collective-permute-start.45 = (bf16[4,80,2560]{2,1,0:T(8,128)(2,1)}, bf16[4,80,2560]{2,1,0:T(8,128)(2,1)}, u32[]{:S(2)}, u32[]{:S(2)}) collective-permute-start(bf16[4,80,2560]{2,1,0:T(8,128)(2,1)} %get-tuple-element.465), channel_id=1, source_target_pairs={{0,2},{1,3},{2,0},{3,1},{4,6},{5,7},{6,4},{7,5},{8,10},{9,11},{10,... | collective-permute-start | bytes 4915208 | tf_op jit(solution)/shard_map/scatter_up/ppermute | solution.py:115
  443.5 38.9 %collective-permute-start.54 = (bf16[4,80,2560]{2,1,0:T(8,128)(2,1)}, bf16[4,80,2560]{2,1,0:T(8,128)(2,1)S(1)}, u32[]{:S(2)}, u32[]{:S(2)}) collective-permute-start(bf16[4,80,2560]{2,1,0:T(8,128)(2,1)} %get-tuple-element.494), channel_id=1, source_target_pairs={{0,4},{1,5},{2,3},{3,2},{4,0},{5,1},{6,7},{7,6},{8,12},{9,13},{10,... | collective-permute-start | bytes 4915208 | tf_op jit(solution)/shard_map/scatter_up/ppermute | solution.py:115
  444.1 38.4 %collective-permute-start.55 = (bf16[4,80,2560]{2,1,0:T(8,128)(2,1)}, bf16[4,80,2560]{2,1,0:T(8,128)(2,1)}, u32[]{:S(2)}, u32[]{:S(2)}) collective-permute-start(bf16[4,80,2560]{2,1,0:T(8,128)(2,1)} %get-tuple-element.495), channel_id=1, source_target_pairs={{0,1},{1,0},{2,6},{3,7},{4,5},{5,4},{6,2},{7,3},{8,9},{9,8},{10,14... | collective-permute-start | bytes 4915208 | tf_op jit(solution)/shard_map/scatter_up/ppermute | solution.py:115
  447.9 38.6 %collective-permute-start.56 = (bf16[4,40,1280]{2,1,0:T(8,128)(2,1)}, bf16[4,40,1280]{2,1,0:T(8,128)(2,1)}, u32[]{:S(2)}, u32[]{:S(2)}) collective-permute-start(bf16[4,40,1280]{2,1,0:T(8,128)(2,1)} %add_convert_fusion.22), channel_id=1, source_target_pairs={{0,1},{1,0},{2,6},{3,7},{4,5},{5,4},{6,2},{7,3},{8,9},{9,8},{10,14... | collective-permute-start | bytes 1228808 | tf_op jit(solution)/shard_map/scatter_exit/ppermute | solution.py:115
  522.8 23.5 %collective-permute-start.63 = (bf16[4,80,1920]{2,1,0:T(8,128)(2,1)}, bf16[4,80,1920]{2,1,0:T(8,128)(2,1)}, u32[]{:S(2)}, u32[]{:S(2)}) collective-permute-start(bf16[4,80,1920]{2,1,0:T(8,128)(2,1)} %add_convert_fusion.10), channel_id=1, source_target_pairs={{0,1},{1,0},{2,6},{3,7},{4,5},{5,4},{6,2},{7,3},{8,9},{9,8},{10,14... | collective-permute-start | bytes 3686408 | tf_op jit(solution)/shard_map/scatter_entry/ppermute | solution.py:115
  550.8 33.6 %collective-permute-start.67 = (bf16[4,80,1920]{2,1,0:T(8,128)(2,1)}, bf16[4,80,1920]{2,1,0:T(8,128)(2,1)}, u32[]{:S(2)}, u32[]{:S(2)}) collective-permute-start(bf16[4,80,1920]{2,1,0:T(8,128)(2,1)} %get-tuple-element.539), channel_id=1, source_target_pairs={{0,4},{1,5},{2,3},{3,2},{4,0},{5,1},{6,7},{7,6},{8,12},{9,13},{10,... | collective-permute-start | bytes 3686408 | tf_op jit(solution)/shard_map/scatter_entry/ppermute | solution.py:115
  551.8 32.6 %collective-permute-start.68 = (bf16[4,80,1920]{2,1,0:T(8,128)(2,1)}, bf16[4,80,1920]{2,1,0:T(8,128)(2,1)}, u32[]{:S(2)}, u32[]{:S(2)}) collective-permute-start(bf16[4,80,1920]{2,1,0:T(8,128)(2,1)} %get-tuple-element.540), channel_id=1, source_target_pairs={{0,1},{1,0},{2,6},{3,7},{4,5},{5,4},{6,2},{7,3},{8,9},{9,8},{10,14... | collective-permute-start | bytes 3686408 | tf_op jit(solution)/shard_map/scatter_entry/ppermute | solution.py:115
  557.7 26.6 %collective-permute-start.69 = (bf16[1,80,2560]{2,1,0:T(8,128)(2,1)}, bf16[1,80,2560]{2,1,0:T(8,128)(2,1)S(1)}, u32[]{:S(2)}, u32[]{:S(2)}) collective-permute-start(bf16[1,80,2560]{2,1,0:T(8,128)(2,1)} %get-tuple-element.541), channel_id=1, source_target_pairs={{0,24},{1,25},{2,26},{3,27},{4,28},{5,29},{6,30},{7,31},{8,16},{9,... | collective-permute-start | bytes 1228808 | tf_op jit(solution)/shard_map/scatter_up/ppermute | solution.py:115
  588.6 24.1 %collective-permute-start.73 = (bf16[1,80,1920]{2,1,0:T(8,128)(2,1)S(1)}, bf16[1,80,1920]{2,1,0:T(8,128)(2,1)S(1)}, u32[]{:S(2)}, u32[]{:S(2)}) collective-permute-start(bf16[1,80,1920]{2,1,0:T(8,128)(2,1)S(1)} %get-tuple-element.553), channel_id=1, source_target_pairs={{0,16},{1,17},{2,18},{3,19},{4,20},{5,21},{6,22},{7,23},{8,24},{9,... | collective-permute-start | bytes 921608 | tf_op jit(solution)/shard_map/scatter_entry/ppermute | solution.py:115
  589.7 22.9 %collective-permute-start.74 = (bf16[1,80,1920]{2,1,0:T(8,128)(2,1)S(1)}, bf16[1,80,1920]{2,1,0:T(8,128)(2,1)S(1)}, u32[]{:S(2)}, u32[]{:S(2)}) collective-permute-start(bf16[1,80,1920]{2,1,0:T(8,128)(2,1)S(1)} %get-tuple-element.554), channel_id=1, source_target_pairs={{0,24},{1,25},{2,26},{3,27},{4,28},{5,29},{6,30},{7,31},{8,16},{9,... | collective-permute-start | bytes 921608 | tf_op jit(solution)/shard_map/scatter_entry/ppermute | solution.py:115
  (138 other events, 1819.1 us)
Sparse Core Ops, SparseCore 0:
  18.9 91.1 all-gather.2

commit v3 on v2

--- a/solution.py
+++ b/solution.py
@@ -67,6 +67,12 @@
 ANY = pl.BlockSpec(memory_space=pl.ANY)
 
 
+def room_for(*buffers):
+    need = sum(int(np.prod(shape)) * size * copies for shape, size, copies in buffers)
+    room = min(60 * 2**20, need + need // 8 + 8 * 2**20)
+    return pltpu.CompilerParams(vmem_limit_bytes=int(room))
+
+
 class Plan:
     def __init__(self, dp, mp):
         self.dp, self.mp = dp, mp
@@ -122,6 +128,57 @@
     return total.astype(dtype)
 
 
+class Sum:
+    def __init__(self, terms, count):
+        self.terms, self.count = terms, count
+        self.shape = terms[0][0].shape[1:]
+
+
+def make_sums(sums):
+    if not sums:
+        return []
+    arrays = [array for job in sums for array, _ in job.terms]
+    parts = [job.count // 2 if job.count % 2 == 0 else job.count for job in sums]
+    in_specs, out_specs = [], []
+    for job, part in zip(sums, parts):
+        moves = int(part < job.count)
+
+        def spec(offset, part=part, moves=moves, shape=job.shape):
+            return pl.BlockSpec(
+                (part,) + shape, lambda i, at=offset // part: (at + moves * i, 0, 0)
+            )
+
+        in_specs = in_specs + [spec(offset) for _, offset in job.terms]
+        out_specs.append(spec(0))
+
+    def kernel(*refs):
+        outs, first = refs[len(arrays) :], 0
+        for job, part, out in zip(sums, parts, outs):
+            mine = refs[first : first + len(job.terms)]
+            first = first + len(job.terms)
+
+            def add(mine=mine, out=out):
+                out[...] = add_all([ref[...] for ref in mine])
+
+            if part < job.count:
+                add()
+            else:
+                pl.when(pl.program_id(0) == 0)(add)
+
+    size = sum(job.count * np.prod(job.shape) * (len(job.terms) + 1) for job in sums)
+    return pl.pallas_call(
+        kernel,
+        out_shape=[jax.ShapeDtypeStruct((job.count,) + job.shape, jnp.bfloat16) for job in sums],
+        grid=(2,),
+        in_specs=in_specs,
+        out_specs=out_specs,
+        compiler_params=pltpu.CompilerParams(vmem_limit_bytes=VMEM_LIMIT),
+        cost_estimate=pl.CostEstimate(
+            flops=int(size), bytes_accessed=int(2 * size), transcendentals=0
+        ),
+    )(*arrays)
+
+
 class Travel:
     def __init__(self, name, steps, quiet=False):
         self.name, self.steps, self.quiet = name, steps, quiet
@@ -140,7 +197,10 @@
         return jax.tree.unflatten(tree, passed[:-1])
 
     def start(self, travels, more=()):
-        values, more = self.through(([[v for v, _ in travel.wanted] for travel in travels], more))
+        wanted = [[v for v, _ in travel.wanted] for travel in travels]
+        made = list(make_sums([v for want in wanted for v in want if isinstance(v, Sum)]))
+        wanted = [[made.pop(0) if isinstance(v, Sum) else v for v in want] for want in wanted]
+        values, more = self.through((wanted, more))
         for travel, ready in zip(travels, values):
             with jax.named_scope(travel.name):
                 travel.going = [send(v, pairs) for v, (_, pairs) in zip(ready, travel.wanted)]
@@ -186,25 +246,23 @@
     return [4 * plan.z, 3 * plan.z, plan.z]
 
 
-def scatter_shards(plan, pieces, split=()):
+def scatter_shards(plan, pieces, split=(), apart=False):
     first, second, core = plan.flip_first(), plan.flip_second(), plan.flip_core()
     own, rest_twin, far_twin = pieces
     size = plan.z
-
-    def quarter(value, k):
-        return value[k * size : (k + 1) * size]
-
     far_got, rest_got = yield [(far_twin, core), (rest_twin, core)]
-    (far_got,) = yield [(add_all([quarter(own, 3), far_got]), second)]
-    near = add_all([quarter(own, 1), quarter(rest_got, 1), far_got])
-    side = add_all([quarter(own, 2), quarter(rest_got, 2)])
-    near_got, side_got = yield [(near, first), (side, second)]
-    terms = [quarter(own, 0), quarter(rest_got, 0), near_got, side_got]
+    (far_got,) = yield [(Sum([(own, 3 * size), (far_got, 0)], size), second)]
+    near_sum = Sum([(own, size), (rest_got, size), (far_got, 0)], size)
+    side_sum = Sum([(own, 2 * size), (rest_got, 2 * size)], size)
+    if apart:
+        (near_got,) = yield [(near_sum, first)]
+        (side_got,) = yield [(side_sum, second)]
+    else:
+        near_got, side_got = yield [(near_sum, first), (side_sum, second)]
+    terms = [own, rest_got, near_got, side_got]
     moves, arrived = plan.z_moves(), []
     for group in plan.z_groups(split):
-        arrived += yield [
-            (add_all([term[k + 1 : k + 2] for term in terms]), moves[k]) for k in group
-        ]
+        arrived += yield [(Sum([(term, k + 1) for term in terms], 1), moves[k]) for k in group]
     return add_all([term[:1] for term in terms] + arrived, jnp.float32)[0]
 
 
@@ -218,11 +276,11 @@
     else:
         (got,) = yield [(value, plan.flip_core())]
         value = value + got
-    moves = [plan.pairs(lambda z, y, c, x: (z, y, c, 1 - x))]
-    bit = 1
+    moves, bit = [], 1
     while bit < plan.z:
         moves.append(plan.flip_z(bit))
         bit *= 2
+    moves.append(plan.pairs(lambda z, y, c, x: (z, y, c, 1 - x)))
     moves.append(plan.pairs(lambda z, y, c, x: (z, 1 - y, c, x)))
     for pairs in moves:
         (got,) = yield [(value, pairs)]
@@ -233,16 +291,20 @@
     return value
 
 
-def total_over_devices(plan, value):
-    travel = Travel("small_sum", total_steps(plan, value))
+def total_over_devices(plan, value, more=()):
+    travel, clock = Travel("small_sum", total_steps(plan, value)), None
     while travel.wanted:
         with jax.named_scope(travel.name):
             got = [send(v, pairs) for v, pairs in travel.wanted]
+        if clock is None:
+            clock = Clock(got[0])
+            more = clock.through(more)
+            got = [clock.token]
         try:
             travel.wanted = travel.steps.send(got)
         except StopIteration as end:
             travel.wanted, travel.result = None, end.value
-    return travel.result
+    return travel.result, more
 
 
 def slot_counts(pieces):
@@ -529,7 +591,12 @@
         inputs, refs = refs[: len(operands)], refs[len(operands) :]
         sources, refs = refs[: sum(sizes)], refs[sum(sizes) :]
         results, refs = refs[: len(outs)], refs[len(outs) :]
-        matrices, sems = refs[: len(spreads)], refs[len(spreads)]
+        kept, refs = refs[: len(spreads)], refs[len(spreads) :]
+        matrices, sems, kept_sems = refs[: len(spreads)], refs[len(spreads)], refs[len(spreads) + 1]
+        keeps = [
+            pltpu.make_async_copy(matrix, out, kept_sems.at[k])
+            for k, (matrix, out) in enumerate(zip(matrices, kept))
+        ]
 
         @pl.when(pl.program_id(0) == 0)
         def _():
@@ -553,23 +620,35 @@
                 first = first + len(spread.pieces)
             for copy in copies:
                 copy.wait()
+            for keep in keeps:
+                keep.start()
 
         body(inputs, matrices, results)
+
+        @pl.when(pl.program_id(0) == pl.num_programs(0) - 1)
+        def _():
+            for keep in keeps:
+                keep.wait()
 
     moved_bytes = sum(2 * spread.shape[0] * spread.shape[1] for spread in spreads)
     moved_bytes += sum(array.size * array.dtype.itemsize for array, _, _ in operands)
     moved_bytes += sum(np.prod(shape) * np.dtype(dtype).itemsize for shape, dtype, _, _ in outs)
     return pl.pallas_call(
         kernel,
-        out_shape=[jax.ShapeDtypeStruct(shape, dtype) for shape, dtype, _, _ in outs],
+        out_shape=[jax.ShapeDtypeStruct(shape, dtype) for shape, dtype, _, _ in outs]
+        + [jax.ShapeDtypeStruct(spread.shape, jnp.bfloat16) for spread in spreads],
         grid_spec=pltpu.PrefetchScalarGridSpec(
             num_scalar_prefetch=1,
             grid=(steps,),
             in_specs=[pl.BlockSpec(block, index) for _, block, index in operands]
             + [ANY] * sum(sizes),
-            out_specs=[pl.BlockSpec(block, index) for _, _, block, index in outs],
+            out_specs=[pl.BlockSpec(block, index) for _, _, block, index in outs]
+            + [ANY] * len(spreads),
             scratch_shapes=[pltpu.VMEM(spread.shape, jnp.bfloat16) for spread in spreads]
-            + [pltpu.SemaphoreType.DMA((total,))],
+            + [
+                pltpu.SemaphoreType.DMA((total,)),
+                pltpu.SemaphoreType.DMA((len(spreads),)),
+            ],
         ),
         compiler_params=pltpu.CompilerParams(vmem_limit_bytes=VMEM_LIMIT),
         cost_estimate=pl.CostEstimate(
@@ -582,15 +661,15 @@
     )
 
 
-def fixed(step, slots):
+def fixed(step, *scalars):
     return (0, 0)
 
 
-def by_columns(step, slots):
+def by_columns(step, *scalars):
     return (0, step)
 
 
-def by_rows(step, slots):
+def by_rows(step, *scalars):
     return (step, 0)
 
 
@@ -602,7 +681,8 @@
     count, deep = rows.shape
     wide = spread.shape[1]
     if not spread.aligned or wide % block:
-        return matmul(rows, spread.matrix()).astype(jnp.bfloat16)
+        whole = spread.matrix()
+        return matmul(rows, whole).astype(jnp.bfloat16), whole
 
     def body(inputs, matrices, results):
         product = matmul(inputs[0][...], matrices[0][:, step_slice(block)])
@@ -616,23 +696,37 @@
         [((count, wide), jnp.bfloat16, (count, block), by_columns)],
         wide // block,
         2 * count * deep * wide,
-    )[0]
-
-
-def project_back(rows, spread, block):
+    )
+
+
+def by_blocks(body, operands, outs, steps, flops):
+    moved_bytes = sum(array.size * array.dtype.itemsize for array, _, _ in operands)
+    moved_bytes += sum(np.prod(shape) * np.dtype(dtype).itemsize for shape, dtype, _, _ in outs)
+    return pl.pallas_call(
+        body,
+        out_shape=[jax.ShapeDtypeStruct(shape, dtype) for shape, dtype, _, _ in outs],
+        grid=(steps,),
+        in_specs=[pl.BlockSpec(block, index) for _, block, index in operands],
+        out_specs=[pl.BlockSpec(block, index) for _, _, block, index in outs],
+        compiler_params=pltpu.CompilerParams(vmem_limit_bytes=VMEM_LIMIT),
+        cost_estimate=pl.CostEstimate(
+            flops=flops, bytes_accessed=int(moved_bytes), transcendentals=0
+        ),
+    )(*[array for array, _, _ in operands])
+
+
+def project_back(rows, matrix, block):
     count, deep = rows.shape
-    wide = spread.shape[0]
-    if not spread.aligned or wide % block:
-        return matmul_t(rows, spread.matrix())
-
-    def body(inputs, matrices, results):
-        results[0][...] = rows_by_rows(inputs[0][...], matrices[0][step_slice(block), :])
-
-    return with_matrices(
-        spread.plan,
+    wide = matrix.shape[0]
+    if wide % block:
+        return matmul_t(rows, matrix)
+
+    def body(rows_ref, matrix_ref, out_ref):
+        out_ref[...] = rows_by_rows(rows_ref[...], matrix_ref[...])
+
+    return by_blocks(
         body,
-        [spread],
-        [(rows, (count, deep), fixed)],
+        [(rows, (count, deep), fixed), (matrix, (block, deep), by_rows)],
         [((count, wide), jnp.float32, (count, block), by_columns)],
         wide // block,
         2 * count * deep * wide,
@@ -652,8 +746,9 @@
     count, deep = rows.shape
     wide = spread.shape[1]
     if not spread.aligned or wide % block:
-        gelu, slope = gelu_and_slope(matmul(rows, spread.matrix()))
-        return gelu.astype(jnp.bfloat16), slope.astype(jnp.bfloat16)
+        whole = spread.matrix()
+        gelu, slope = gelu_and_slope(matmul(rows, whole))
+        return gelu.astype(jnp.bfloat16), slope.astype(jnp.bfloat16), whole
 
     def body(inputs, matrices, results):
         up_pre = matmul(inputs[0][...], matrices[0][:, step_slice(block)])
@@ -672,22 +767,23 @@
     )
 
 
-def hidden_back(d_out, slope, spread, block):
+def hidden_back(d_out, slope, matrix, block):
     count, wide = slope.shape
-    if not spread.aligned or wide % block:
-        d_activated = matmul_t(d_out, spread.matrix())
+    if wide % block:
+        d_activated = matmul_t(d_out, matrix)
         return (d_activated * slope.astype(jnp.float32)).astype(jnp.bfloat16)
 
-    def body(inputs, matrices, results):
-        d_activated = rows_by_rows(inputs[0][...], matrices[0][step_slice(block), :])
-        d_up = d_activated * inputs[1][...].astype(jnp.float32)
-        results[0][...] = d_up.astype(jnp.bfloat16)
-
-    return with_matrices(
-        spread.plan,
+    def body(d_out_ref, matrix_ref, slope_ref, out_ref):
+        d_activated = rows_by_rows(d_out_ref[...], matrix_ref[...])
+        out_ref[...] = (d_activated * slope_ref[...].astype(jnp.float32)).astype(jnp.bfloat16)
+
+    return by_blocks(
         body,
-        [spread],
-        [(d_out, d_out.shape, fixed), (slope, (count, block), by_columns)],
+        [
+            (d_out, d_out.shape, fixed),
+            (matrix, (block, d_out.shape[1]), by_rows),
+            (slope, (count, block), by_columns),
+        ],
         [((count, wide), jnp.bfloat16, (count, block), by_columns)],
         wide // block,
         2 * count * d_out.shape[1] * wide,
@@ -698,7 +794,8 @@
     count, deep = activated.shape
     wide = base.shape[1]
     if not spread.aligned or count % block:
-        return base + matmul(activated, spread.matrix())
+        whole = spread.matrix()
+        return base + matmul(activated, whole), whole
 
     def body(inputs, matrices, results):
         results[0][...] = inputs[1][...] + matmul(inputs[0][...], matrices[0][...])
@@ -711,7 +808,7 @@
         [((count, wide), jnp.float32, (block, wide), by_rows)],
         count // block,
         2 * count * deep * wide,
-    )[0]
+    )
 
 
 def weight_grad(plan, left, right, rows, parts, split_columns, block):
@@ -878,7 +975,7 @@
         out_specs=[vmem] * (2 * count + 2) + [smem],
         compiler_params=pltpu.CompilerParams(vmem_limit_bytes=VMEM_LIMIT),
     )(scalars, *flat, *states, *masters, *norms)
-    return found[:count], found[count : 2 * count], *found[2 * count :]
+    return list(found[:count]), found[count : 2 * count], *found[2 * count :]
 
 
 def new_weights(steps, masters, directions):
@@ -900,13 +997,13 @@
         + [jax.ShapeDtypeStruct(master.shape, jnp.bfloat16) for master in masters[:-1]],
         in_specs=[smem] + [vmem] * (2 * count),
         out_specs=[vmem] * (2 * count - 1),
-        compiler_params=pltpu.CompilerParams(vmem_limit_bytes=VMEM_LIMIT),
+        compiler_params=room_for(*[(master.shape, 4, 4) for master in masters]),
     )(steps, *masters, *directions)
     return found[:count], found[count:]
 
 
 BY_COLUMNS = ("entry", "up")
-SPLITS = {"up": ((0, 1), (2,)), "exit": ((0,), (1, 2))}
+SPLITS = {"up": ((0, 1), (2,)), "down": ((0, 1), (2,))}
 
 
 def per_device(
@@ -943,7 +1040,6 @@
     masters = {"entry": entry_weight, "exit": exit_weight, "up": up_weight, "down": down_weight}
     rows_here, half_wide = entry_weight.shape[1:]
     halves = {name: value.astype(jnp.bfloat16) for name, value in masters.items()}
-    down_half = down_weight.shape[1] // 2
     entry_shard = halves["entry"].transpose(1, 0, 2).reshape(rows_here, 3 * half_wide)
     paths = {
         name: Travel("gather_" + name, gather_shards(plan, shard, split))
@@ -998,8 +1094,7 @@
     start("entry up")
     wait("entry")
     (normed_one,) = start("down", normed_one)
-    entry_all = whole("entry")
-    projected = project(normed_one, entry_all, 768)
+    projected, entry_all = project(normed_one, whole("entry"), 768)
     (projected,) = wait("up down", projected)
     (projected,) = start("up", projected)
     context = attend_call(
@@ -1011,15 +1106,14 @@
     (normed_two,) = start("up down", normed_two)
     wait("up")
     (normed_two,) = start("", normed_two)
-    up_all = whole("up")
-    activated, slope = hidden_forward(normed_two, up_all, 512)
+    activated, slope, up_all = hidden_forward(normed_two, whole("up"), 512)
     activated, slope = wait("down", activated, slope)
+    late = start("down", *masters.values())
+    weight_local = jnp.stack([jnp.sum(master * master) for master in late])
+    (weight_local,) = wait("down", weight_local)
     start("down")
     wait("down")
-    start("down")
-    wait("down")
-    down_all = whole("down")
-    after_mlp = hidden_out(activated, after_attn, down_all, 320)
+    after_mlp, down_all = hidden_out(activated, after_attn, whole("down"), 320)
     final_norm = layer_norm(after_mlp, norm_params[2], norm_params[5]).astype(jnp.bfloat16)
     head_half = head_weight.astype(jnp.bfloat16)
     logits = matmul_t(final_norm, head_half)
@@ -1029,89 +1123,79 @@
     )
     d_logits = loss_pull(jnp.ones_like(loss_local))[0].astype(jnp.bfloat16)
     d_final = matmul(d_logits, head_half)
-    d_mlp_in, d_gain_three, d_shift_three = norm_back(
-        after_mlp, norm_params[2], norm_params[5], d_final
-    )
+    d_mlp_in, _, _ = norm_back(after_mlp, norm_params[2], norm_params[5], d_final)
     d_mlp_out = d_mlp_in.astype(jnp.bfloat16)
 
-    def leave(name, left, right, block):
-        rows = {"entry": rows_here, "exit": exit_weight.shape[0], "up": rows_here}
-        by_columns = name in BY_COLUMNS
-        width = right.shape[1] // (plan.mp if by_columns else 1)
-        part = (width, scatter_counts(plan), slots)
-        (pieces,) = weight_grad(
-            plan,
-            left,
-            right,
-            rows.get(name, down_weight.shape[0]),
-            [part],
-            by_columns,
-            block,
-        )
-        paths[name] = Travel(
-            "scatter_" + name,
-            scatter_shards(plan, pieces, SPLITS.get(name, ())),
-        )
-
-    leave("down_a", activated, d_mlp_out[:, :down_half], 1280)
-    d_mlp_out, d_logits = start("down_a", d_mlp_out, d_logits)
-    d_mlp_out, d_logits = wait("down_a", d_mlp_out, d_logits)
-    d_mlp_out, d_logits = start("down_a", d_mlp_out, d_logits)
-    leave("down_b", activated, d_mlp_out[:, down_half:], 1280)
+    def leave(names, left, right, rows, widths, block):
+        by_columns = names.split()[0] in ("entry_a", "up")
+        parts = [(width, scatter_counts(plan), slots) for width in widths]
+        found = weight_grad(plan, left, right, rows, parts, by_columns, block)
+        for name, pieces in zip(names.split(), found):
+            steps = scatter_shards(plan, pieces, SPLITS.get(name, ()), name == "up")
+            paths[name] = Travel("scatter_" + name, steps)
+
+    down_rows = down_weight.shape[0]
+    entry_widths = (3 * half_wide * 8 // 15, 3 * half_wide - 3 * half_wide * 8 // 15)
+    leave("down", activated, d_mlp_out, down_rows, [wide], 1280)
     head_rows = head_weight.shape[0]
     d_head = jnp.pad(contract(d_logits, final_norm), ((0, head_rows % 2), (0, 0)))
-    d_mlp_out, d_head = wait("down_a", d_mlp_out, d_head)
     paths["head"] = Travel("sum_head", total_steps(plan, d_head, halves=True))
-    d_mlp_out, *late = start("down_a down_b head", d_mlp_out, *masters.values())
+    (d_mlp_out,) = start("down head", d_mlp_out)
     d_up_pre = hidden_back(d_mlp_out, slope, down_all, 512)
-    weight_local = jnp.stack([jnp.sum(master * master) for master in late])
-    d_up_pre, weight_local = wait("down_a down_b head", d_up_pre, weight_local)
-    (d_up_pre,) = start("down_a down_b head", d_up_pre)
-    leave("up", normed_two, d_up_pre, 2560)
-    (d_up_pre,) = wait("down_a down_b head", d_up_pre)
-    (d_up_pre,) = start("down_b up head", d_up_pre)
+    (d_up_pre,) = wait("down head", d_up_pre)
+    (d_up_pre,) = start("down head", d_up_pre)
+    leave("up", normed_two, d_up_pre, rows_here, [up_weight.shape[1]], 2560)
+    (d_up_pre,) = wait("down head", d_up_pre)
+    (d_up_pre,) = start("down up head", d_up_pre)
     d_normed_two = project_back(d_up_pre, up_all, 256)
-    (d_normed_two,) = wait("down_b up head", d_normed_two)
-    (d_normed_two,) = start("down_b up", d_normed_two)
-    d_ln_two, d_gain_two, d_shift_two = norm_back(
-        after_attn, norm_params[1], norm_params[4], d_normed_two
-    )
+    d_ln_two, _, _ = norm_back(after_attn, norm_params[1], norm_params[4], d_normed_two)
     d_attn_out = (d_mlp_in + d_ln_two).astype(jnp.bfloat16)
-    leave("exit", context, d_attn_out, 1280)
+    leave("exit", context, d_attn_out, exit_rows, [wide], 1280)
     d_context = matmul_t(d_attn_out, exit_all).astype(jnp.bfloat16)
-    (d_context,) = wait("down_b up", d_context)
-    (d_context,) = start("up exit", d_context)
-    (d_context,) = wait("exit", d_context)
-    (d_context,) = start("exit head", d_context)
+    (d_context,) = wait("down up head", d_context)
+    (d_context,) = start("down up exit", d_context)
     d_projected = attend_call(
         attend_back_kernel, segments, projected, [d_context], projected.shape[1], plan.mp, 5
     )
-    (d_projected,) = wait("up exit head", d_projected)
-    (d_projected,) = start("exit head", d_projected)
-    leave("entry", normed_one, d_projected, 1920)
-    (d_projected,) = wait("exit head", d_projected)
-    (d_projected,) = start("entry", d_projected)
-    (d_projected,) = wait("entry", d_projected)
-    (d_projected,) = start("entry up exit", d_projected)
+    (d_projected,) = wait("down up exit", d_projected)
+    (d_projected,) = start("up down exit", d_projected)
+    leave("entry_a entry_b", normed_one, d_projected, rows_here, entry_widths, 1920)
+    (d_projected,) = wait("up down exit", d_projected)
+    (d_projected,) = start("up entry_a entry_b", d_projected)
     d_normed_one = project_back(d_projected, entry_all, 256)
-    (d_normed_one,) = wait("entry up exit", d_normed_one)
-    (d_normed_one,) = start("entry up exit", d_normed_one)
+    reds = {"down": finish("down")}
+    (d_normed_one,) = wait("up entry_a entry_b", d_normed_one)
+    d_normed_one, reds = start("entry_a entry_b up head", d_normed_one, reds)
+    down_square = jnp.sum(reds["down"] * reds["down"])
     _, d_gain_one, d_shift_one = norm_back(resid, norm_params[0], norm_params[3], d_normed_one)
-    d_gain_one, d_shift_one = wait("entry up exit", d_gain_one, d_shift_one)
-    start("entry head")
-    wait("entry head")
+    d_gain_one, d_shift_one, reds, down_square = wait(
+        "entry_a entry_b up head", d_gain_one, d_shift_one, reds, down_square
+    )
+    late = start("entry_a up exit", after_mlp, d_final, after_attn, d_normed_two)
+    _, d_gain_three, d_shift_three = norm_back(late[0], norm_params[2], norm_params[5], late[1])
+    _, d_gain_two, d_shift_two = norm_back(late[2], norm_params[1], norm_params[4], late[3])
+    late = wait("entry_a up exit", d_gain_two, d_shift_two, d_gain_three, d_shift_three)
+    d_gain_two, d_shift_two, d_gain_three, d_shift_three = late
+    start("entry_b entry_a head")
+    reds["up"] = finish("up")
+    up_square = jnp.sum(reds["up"] * reds["up"])
+    reds, up_square = wait("entry_b entry_a head", reds, up_square)
+    start("entry_b exit head")
+    wait("entry_b exit head")
+    reds["exit"] = finish("exit")
+    exit_square = jnp.sum(reds["exit"] * reds["exit"])
     red_head = finish("head")[:head_rows]
-    names = ("entry", "exit", "up", "down_a", "down_b")
-    reds = {name: finish(name) for name in names}
-
+    reds["entry_a"], reds["entry_b"] = finish("entry_a"), finish("entry_b")
+    local_square = down_square + up_square + exit_square
+    for name in ("entry_a", "entry_b"):
+        local_square = local_square + jnp.sum(reds[name] * reds[name])
     masters = [entry_weight, exit_weight, up_weight, down_weight, head_weight]
     states = [entry_state, exit_state, up_state, down_state, head_state]
-    local_square = sum(jnp.sum(reds[name] * reds[name]) for name in names)
     wide = norm_params.shape[1]
     scalars = jnp.concatenate(
         [jnp.stack([loss_local, local_square]), weight_local, clock.token]
     )
-    small = total_over_devices(
+    small, _ = total_over_devices(
         plan,
         jnp.stack(
             [
@@ -1134,10 +1218,10 @@
     corr_first = 1.0 - jnp.power(beta_first, step_float)
     corr_second = 1.0 - jnp.power(beta_second, step_float)
     gradients = [
-        [reds["entry"]],
+        [jnp.concatenate([reds["entry_a"], reds["entry_b"]], 1)],
         [reds["exit"]],
         [reds["up"]],
-        [reds["down_a"], reds["down_b"]],
+        [reds["down"]],
         [red_head],
     ]
     moments, directions, norm_moments, norm_new, squares = moments_and_directions(
@@ -1147,7 +1231,8 @@
         masters,
         (red_norms, norm_state, norm_params),
     )
-    update_sums = total_over_devices(plan, squares[:4])
+    update_sums, late = total_over_devices(plan, squares[:4], (moments[4], norm_moments))
+    moments[4], norm_moments = late
     weight_norms = jnp.sqrt(weight_sums)
     update_norms = jnp.sqrt(update_sums)
     head_wnorm = jnp.sqrt(jnp.sum(head_weight * head_weight))

time: 699 us -> 674 us (0.964)
  other arithmetic: 101 us -> 75.6 us
  waiting for transfers between devices: 193 us -> 169 us
  Pallas kernels: 220 us -> 240 us
    pallas_call x0 -> x12, Pallas kernels: none -> 79.9 us  [the longest x3 43.6 us: by_blocks(): pl.pallas_call(body, out_shape=[jax.ShapeDtypeStruct(shape, dtype) for sh...]
    pallas_call x6 -> x3, Pallas kernels: 113 us -> 61.4 us  [with_matrices(): pl.pallas_call(kernel, out_shape=[jax.ShapeDtypeStruct(shape, dtype) for...]
    convert_element_type x16 -> x0, other arithmetic: 45.6 us -> none  [the longest x15 45.6 us: add_all(): return total.astype(dtype)]
    ppermute x86, waiting for transfers between devices: 193 us -> 169 us  [send(): return lax.ppermute(value, AXES, pairs)]
    reduce_sum x4 -> x6, other arithmetic: 1.81 us -> 9.35 us  [layer_norm(): spread = jnp.mean(centred * centred, -1, keepdims=True)]
    pallas_call x4 -> x3, Pallas kernels: 55 us -> 49.2 us  [weight_grad(): pl.pallas_call(kernel, out_shape=[jax.ShapeDtypeStruct((count, rows, widt...]
    unnamed x173 -> x159, local copies, waits for them, and re-layouts: 23.2 us -> 26.7 us
  transfers between devices with their start and end apart: 87 -> 87, of which waited for: 34 -> 34; matrix products, arithmetic and copies ran while one was open for 11% -> 12% of each run, Pallas kernels for 25% -> 23%
where the time goes in v3:
time: 674 us; the launch traced here: 669 us
  Pallas kernels  240 us (36%)
  waiting for transfers between devices  169 us (25%)
  starting transfers between devices  108 us (16%)
  other arithmetic  75.6 us (11%)
  local copies, waits for them, and re-layouts  34.8 us (5%)
  between operations  26 us (4%)
  matrix products  15.6 us (2%)
    ppermute x86, waiting for transfers between devices, send(): return lax.ppermute(value, AXES, pairs)  169 us
    ppermute x86, starting transfers between devices, send(): return lax.ppermute(value, AXES, pairs)  108 us
    pallas_call x3, Pallas kernels, with_matrices(): pl.pallas_call(kernel, out_shape=[jax.ShapeDtypeStruct(shape, dtype) for...  61.4 us
    pallas_call x3, Pallas kernels, weight_grad(): pl.pallas_call(kernel, out_shape=[jax.ShapeDtypeStruct((count, rows, widt...  49.2 us
    pallas_call x3, Pallas kernels, by_blocks(): pl.pallas_call(body, out_shape=[jax.ShapeDtypeStruct(shape, dtype) for sh...  43.6 us
    pallas_call x9, Pallas kernels, make_sums(): pl.pallas_call(kernel, out_shape=[jax.ShapeDtypeStruct((job.count,) + job...  36.3 us
    pallas_call x2, Pallas kernels, attend_call(): pl.pallas_call(functools.partial(kernel, groups, pairs), out_shape=jax.Sh...  30.4 us
    unnamed x159, local copies, waits for them, and re-layouts  26.7 us
  transfers between devices with their start and end apart: 87, of which 34 were waited for; matrix products, arithmetic and copies ran while one was open for 12% of the time, Pallas kernels for 23%

profile of v3, /device:TPU:0, one launch (start us, length us, event | category | flops | bytes accessed | tf_op | source)
XLA Modules:
  0.0 668.6 jit_solution(1772197491620893668)
XLA Ops:
  27.7 12.8 %collective-permute-done.1 = bf16[1,80,1920]{2,1,0:T(8,128)(2,1)S(1)} collective-permute-done((bf16[1,80,1920]{2,1,0:T(8,128)(2,1)S(1)}, bf16[1,80,1920]{2,1,0:T(8,128)(2,1)S(1)}, u32[]{:S(2)}, u32[]{:S(2)}) %collective-permute-start.1) | collective-permute-done | bytes 307232 | tf_op jit(solution)/shard_map/gather_entry/ppermute | solution.py:121
  43.8 6.7 %collective-permute-start.5 = (bf16[1,80,2560]{2,1,0:T(8,128)(2,1)S(1)}, bf16[1,80,2560]{2,1,0:T(8,128)(2,1)S(1)}, u32[]{:S(2)}, u32[]{:S(2)}) collective-permute-start(bf16[1,80,2560]{2,1,0:T(8,128)(2,1)S(1)} %convert_bitcast_fusion), channel_id=1, source_target_pairs={{0,8},{1,9},{2,10},{3,11},{4,12},{5,13},{6,14},{7,15},{8,0},{9,1},... | collective-permute-start | bytes 1228808 | tf_op jit(solution)/shard_map/gather_up/ppermute | solution.py:121
  51.4 20.6 %collective-permute-done.5 = bf16[1,80,2560]{2,1,0:T(8,128)(2,1)S(1)} collective-permute-done((bf16[1,80,2560]{2,1,0:T(8,128)(2,1)S(1)}, bf16[1,80,2560]{2,1,0:T(8,128)(2,1)S(1)}, u32[]{:S(2)}, u32[]{:S(2)}) %collective-permute-start.5) | collective-permute-done | bytes 409632 | tf_op jit(solution)/shard_map/gather_up/ppermute | solution.py:121
  78.2 17.5 %collective-permute-done.10 = bf16[1,80,2560]{2,1,0:T(8,128)(2,1)S(1)} collective-permute-done((bf16[1,80,2560]{2,1,0:T(8,128)(2,1)S(1)}, bf16[1,80,2560]{2,1,0:T(8,128)(2,1)S(1)}, u32[]{:S(2)}, u32[]{:S(2)}) %collective-permute-start.10) | collective-permute-done | bytes 409632 | tf_op jit(solution)/shard_map/gather_up/ppermute | solution.py:121
  105.4 10.4 %collective-permute-start.15 = (bf16[1,160,1280]{2,1,0:T(8,128)(2,1)S(1)}, bf16[1,160,1280]{2,1,0:T(8,128)(2,1)S(1)}, u32[]{:S(2)}, u32[]{:S(2)}) collective-permute-start(bf16[1,160,1280]{2,1,0:T(8,128)(2,1)S(1)} %convert_bitcast_fusion.1), channel_id=1, source_target_pairs={{0,8},{1,9},{2,10},{3,11},{4,12},{5,13},{6,14},{7,15},{8,0},{9,1},... | collective-permute-start | bytes 1228808 | tf_op jit(solution)/shard_map/gather_down/ppermute | solution.py:121
  118.4 15.9 %shard_map.348 = (bf16[640,3840]{1,0:T(8,128)(2,1)}, bf16[1280,3840]{1,0:T(8,128)(2,1)}) custom-call(s32[32]{0:T(128)} %dynamic-slice_bitcast_fusion.slots_ref, bf16[640,1280]{1,0:T(8,128)(2,1)} %add_convert_fusion.3.refs_0_.left_ref, bf16[4,80,1920]{2,1,0:T(8,128)(2,1)} %copy-done.48, bf16[4,80,1920]{2,1,0:T(8,128)(2,1)} %copy-done.73, ...), custom_call_target="tpu_custom_call" | custom-call | flops 6291456000 | bytes 16384000 | tf_op jit(solution)/shard_map/pallas_call | solution.py:636
  134.3 12.4 %collective-permute-done.16 = bf16[1,160,1280]{2,1,0:T(8,128)(2,1)S(1)} collective-permute-done((bf16[1,160,1280]{2,1,0:T(8,128)(2,1)S(1)}, bf16[1,160,1280]{2,1,0:T(8,128)(2,1)S(1)}, u32[]{:S(2)}, u32[]{:S(2)}) %collective-permute-start.16) | collective-permute-done | bytes 409632 | tf_op jit(solution)/shard_map/gather_down/ppermute | solution.py:121
  148.2 11.3 %shard_map.349 = bf16[640,1280]{1,0:T(8,128)(2,1)} custom-call(s32[4,160,1]{2,1,0:T(8,128)} %copy.53.column_ref, s32[4,1,320]{2,1,0:T(1,128)} %tile.5.row_ref, bf16[640,3840]{1,0:T(8,128)(2,1)} %get-tuple-element.396.qkv_ref), custom_call_target="tpu_custom_call" | custom-call | flops 524288000 | bytes 9830400 | tf_op jit(solution)/shard_map/pallas_call | solution.py:527
  175.7 26.1 %shard_map.350 = (bf16[640,5120]{1,0:T(8,128)(2,1)}, bf16[640,5120]{1,0:T(8,128)(2,1)}, bf16[1280,5120]{1,0:T(8,128)(2,1)}) custom-call(s32[32]{0:T(128)} %dynamic-slice_bitcast_fusion.slots_ref, bf16[640,1280]{1,0:T(8,128)(2,1)} %add_convert_fusion.2.refs_0_.left_ref, bf16[4,80,2560]{2,1,0:T(8,128)(2,1)} %pad_maximum_fusion.refs_1_, ...), custom_call_target="tpu_custom_call" | custom-call | flops 8388608000 | bytes 27852800 | tf_op jit(solution)/shard_map/pallas_call | solution.py:636
  201.8 7.1 %collective-permute-done.23.refs_3_ = bf16[4,160,1280]{2,1,0:T(8,128)(2,1)} collective-permute-done((bf16[4,160,1280]{2,1,0:T(8,128)(2,1)}, bf16[4,160,1280]{2,1,0:T(8,128)(2,1)}, u32[]{:S(2)}, u32[]{:S(2)}) %collective-permute-start.23) | collective-permute-done | bytes 1638432 | tf_op jit(solution)/shard_map/gather_down/ppermute | solution.py:121
  216.6 13.7 %collective-permute-done.25.refs_5_ = bf16[4,160,1280]{2,1,0:T(8,128)(2,1)} collective-permute-done((bf16[4,160,1280]{2,1,0:T(8,128)(2,1)}, bf16[4,160,1280]{2,1,0:T(8,128)(2,1)}, u32[]{:S(2)}, u32[]{:S(2)}) %collective-permute-start.25) | collective-permute-done | bytes 1638432 | tf_op jit(solution)/shard_map/gather_down/ppermute | solution.py:121
  236.9 19.4 %shard_map.351 = (f32[640,1280]{1,0:T(8,128)}, bf16[5120,1280]{1,0:T(8,128)(2,1)}) custom-call(s32[32]{0:T(128)} %dynamic-slice_bitcast_fusion.slots_ref, bf16[640,5120]{1,0:T(8,128)(2,1)} %get-tuple-element.419.refs_0_.left_ref, f32[640,1280]{1,0:T(8,128)} %copy-done.18, bf16[4,160,1280]{2,1,0:T(8,128)(2,1)} %pad_maximum_fusion.1.refs_2_, ...), custom_call_target="tpu_custom_call" | custom-call | flops 8388608000 | bytes 26214400 | tf_op jit(solution)/shard_map/pallas_call | solution.py:636
  271.3 17.0 %shard_map.352 = (bf16[16,160,1280]{2,1,0:T(8,128)(2,1)}, bf16[12,160,1280]{2,1,0:T(8,128)(2,1)}, bf16[4,160,1280]{2,1,0:T(8,128)(2,1)}) custom-call(s32[32]{0:T(128)} %dynamic-slice_bitcast_fusion.slots_ref, bf16[640,5120]{1,0:T(8,128)(2,1)} %get-tuple-element.419.refs_0_.left_ref, bf16[640,1280]{1,0:T(8,128)(2,1)} %add_convert_fusion.4.right_ref.d_out_ref), custom_call_target="tpu_custom_call" | custom-call | flops 8388608000 | bytes 21299200 | tf_op jit(solution)/shard_map/pallas_call | solution.py:879
  289.1 17.1 %shard_map.353.right_ref.rows_ref = bf16[640,5120]{1,0:T(8,128)(2,1)} custom-call(bf16[640,1280]{1,0:T(8,128)(2,1)} %add_convert_fusion.4.right_ref.d_out_ref, bf16[5120,1280]{1,0:T(8,128)(2,1)} %get-tuple-element.450.matrix_ref, bf16[640,5120]{1,0:T(8,128)(2,1)} %get-tuple-element.451.slope_ref), custom_call_target="tpu_custom_call" | custom-call | flops 8388608000 | bytes 27852800 | tf_op jit(solution)/shard_map/pallas_call | solution.py:705
  311.3 7.5 %collective-permute-start.34 = (f32[71,1280]{1,0:T(8,128)S(1)}, f32[71,1280]{1,0:T(8,128)S(1)}, u32[]{:S(2)}, u32[]{:S(2)}) collective-permute-start(f32[71,1280]{1,0:T(8,128)S(1)} %select_add_fusion.1), channel_id=1, source_target_pairs={{0,8},{1,9},{2,10},{3,11},{4,12},{5,13},{6,14},{7,15},{8,0},{9,1},... | collective-permute-start | bytes 1090568 | tf_op jit(solution)/shard_map/sum_head/ppermute | solution.py:121
  318.8 17.2 %shard_map.355 = (bf16[16,80,2560]{2,1,0:T(8,128)(2,1)}, bf16[12,80,2560]{2,1,0:T(8,128)(2,1)}, bf16[4,80,2560]{2,1,0:T(8,128)(2,1)}) custom-call(s32[32]{0:T(128)} %dynamic-slice_bitcast_fusion.slots_ref, bf16[640,1280]{1,0:T(8,128)(2,1)} %add_convert_fusion.2.refs_0_.left_ref, bf16[640,5120]{1,0:T(8,128)(2,1)} %shard_map.353.right_ref.rows_ref), custom_call_target="tpu_custom_call" | custom-call | flops 8388608000 | bytes 21299200 | tf_op jit(solution)/shard_map/pallas_call | solution.py:879
  338.0 5.0 shard_map.356
  345.8 14.2 %shard_map.357 = f32[640,1280]{1,0:T(8,128)} custom-call(bf16[640,5120]{1,0:T(8,128)(2,1)} %shard_map.353.right_ref.rows_ref, bf16[1280,5120]{1,0:T(8,128)(2,1)} %get-tuple-element.477.matrix_ref), custom_call_target="tpu_custom_call" | custom-call | flops 8388608000 | bytes 22937600 | tf_op jit(solution)/shard_map/pallas_call | solution.py:705
  370.5 4.5 shard_map.359
  379.0 5.9 convolution_convert_fusion.1.d_context_ref
  384.9 11.2 %collective-permute-done.39 = f32[71,1280]{1,0:T(8,128)S(1)} collective-permute-done((f32[71,1280]{1,0:T(8,128)S(1)}, f32[71,1280]{1,0:T(8,128)S(1)}, u32[]{:S(2)}, u32[]{:S(2)}) %collective-permute-start.39) | collective-permute-done | bytes 363552 | tf_op jit(solution)/shard_map/sum_head/ppermute | solution.py:121
  396.9 4.6 shard_map.358
  404.6 19.1 %shard_map.360.right_ref.rows_ref = bf16[640,3840]{1,0:T(8,128)(2,1)} custom-call(s32[4,160,1]{2,1,0:T(8,128)} %copy.53.column_ref, s32[4,1,320]{2,1,0:T(1,128)} %tile.5.row_ref, bf16[640,3840]{1,0:T(8,128)(2,1)} %get-tuple-element.396.qkv_ref, bf16[640,1280]{1,0:T(8,128)(2,1)} %convolution_convert_fusion.1.d_context_ref), custom_call_target="tpu_custom_call" | custom-call | flops 1310720000 | bytes 24576000 | tf_op jit(solution)/shard_map/pallas_call | solution.py:527
  424.6 4.6 shard_map.361
  436.3 15.0 %shard_map.362 = (bf16[16,80,1024]{2,1,0:T(8,128)(2,1)}, bf16[12,80,1024]{2,1,0:T(8,128)(2,1)}, bf16[4,80,1024]{2,1,0:T(8,128)(2,1)}, bf16[16,80,896]{2,1,0:T(8,...) custom-call(s32[64]{0:T(128)} %pad_add_fusion.slots_ref, ...), custom_call_target="tpu_custom_call" | custom-call | flops 6291456000 | bytes 16384000 | tf_op jit(solution)/shard_map/pallas_call | solution.py:879
  461.7 12.3 %shard_map.364 = f32[640,1280]{1,0:T(8,128)} custom-call(bf16[640,3840]{1,0:T(8,128)(2,1)} %shard_map.360.right_ref.rows_ref, bf16[1280,3840]{1,0:T(8,128)(2,1)} %get-tuple-element.523.matrix_ref), custom_call_target="tpu_custom_call" | custom-call | flops 6291456000 | bytes 18022400 | tf_op jit(solution)/shard_map/pallas_call | solution.py:705
  492.0 14.2 %collective-permute-done.57 = f32[71,1280]{1,0:T(8,128)S(1)} collective-permute-done((f32[71,1280]{1,0:T(8,128)S(1)}, f32[71,1280]{1,0:T(8,128)S(1)}, u32[]{:S(2)}, u32[]{:S(2)}) %collective-permute-start.57) | collective-permute-done | bytes 363552 | tf_op jit(solution)/shard_map/sum_head/ppermute | solution.py:121
  507.0 4.5 shard_map.366
  529.1 7.8 %collective-permute-done.61.refs_14_.refs_18_.refs_22_ = bf16[4,40,1280]{2,1,0:T(8,128)(2,1)S(1)} collective-permute-done((bf16[4,40,1280]{2,1,0:T(8,128)(2,1)}, bf16[4,40,1280]{2,1,0:T(8,128)(2,1)S(1)}, u32[]{:S(2)}, u32[]{:S(2)}) %collective-permute-start.61) | collective-permute-done | bytes 409632 | tf_op jit(solution)/shard_map/scatter_exit/ppermute | solution.py:121
  578.0 5.2 collective-permute-done.74
  593.3 4.5 collective-permute-start.77
  619.4 12.1 %shard_map.369 = (f32[2,3,80,640]{3,2,1,0:T(8,128)}, f32[2,40,1280]{2,1,0:T(8,128)}, f32[2,80,2560]{2,1,0:T(8,128)}, f32[2,160,1280]{2,1,0:T(8,128)}, f32[2,142,...) custom-call(f32[3]{0:T(128)} %pad_maximum_fusion.7.scalars_ref, ...), custom_call_target="tpu_custom_call" | custom-call | tf_op jit(solution)/shard_map/pallas_call | solution.py:969
  (464 shorter events, 265.1 us)
Async XLA Ops:
  7.2 153.7 %all-gather.3.cloned.1.call-start = ((), (), s32[]{:S(2)}) async-start(), calls=%async_computation | async-start | bytes 4055040 | tf_op jit(solution)/shard_map/all_gather | solution.py:1059
  14.6 25.9 %collective-permute-start.1 = (bf16[1,80,1920]{2,1,0:T(8,128)(2,1)S(1)}, bf16[1,80,1920]{2,1,0:T(8,128)(2,1)S(1)}, u32[]{:S(2)}, u32[]{:S(2)}) collective-permute-start(bf16[1,80,1920]{2,1,0:T(8,128)(2,1)S(1)} %broadcast_in_dim_reshape.2), channel_id=1, source_target_pairs={{0,16},{1,17},{2,18},{3,19},{4,20},{5,21},{6,22},{7,23},{8,24},{9,... | collective-permute-start | bytes 921608 | tf_op jit(solution)/shard_map/gather_entry/ppermute | solution.py:121
  17.2 23.3 %collective-permute-start.2 = (bf16[1,80,1920]{2,1,0:T(8,128)(2,1)S(1)}, bf16[1,80,1920]{2,1,0:T(8,128)(2,1)S(1)}, u32[]{:S(2)}, u32[]{:S(2)}) collective-permute-start(bf16[1,80,1920]{2,1,0:T(8,128)(2,1)S(1)} %broadcast_in_dim_reshape.2), channel_id=1, source_target_pairs={{0,24},{1,25},{2,26},{3,27},{4,28},{5,29},{6,30},{7,31},{8,16},{9,... | collective-permute-start | bytes 921608 | tf_op jit(solution)/shard_map/gather_entry/ppermute | solution.py:121
  40.6 33.9 %collective-permute-start.3 = (bf16[4,80,1920]{2,1,0:T(8,128)(2,1)S(1)}, bf16[4,80,1920]{2,1,0:T(8,128)(2,1)S(1)}, u32[]{:S(2)}, u32[]{:S(2)}) collective-permute-start(bf16[4,80,1920]{2,1,0:T(8,128)(2,1)S(1)} %constant_dynamic-update-slice_fusion.refs_1_), channel_id=1, source_target_pairs={{0,4},{1,5},{2,3},{3,2},{4,0},{5,1},{6,7},{7,6},{8,12},{9,13},{10,... | collective-permute-start | bytes 3686408 | tf_op jit(solution)/shard_map/gather_entry/ppermute | solution.py:121
  42.3 32.3 %collective-permute-start.4 = (bf16[4,80,1920]{2,1,0:T(8,128)(2,1)S(1)}, bf16[4,80,1920]{2,1,0:T(8,128)(2,1)}, u32[]{:S(2)}, u32[]{:S(2)}) collective-permute-start(bf16[4,80,1920]{2,1,0:T(8,128)(2,1)S(1)} %constant_dynamic-update-slice_fusion.refs_1_), channel_id=1, source_target_pairs={{0,1},{1,0},{2,6},{3,7},{4,5},{5,4},{6,2},{7,3},{8,9},{9,8},{10,14... | collective-permute-start | bytes 3686408 | tf_op jit(solution)/shard_map/gather_entry/ppermute | solution.py:121
  43.8 28.3 %collective-permute-start.5 = (bf16[1,80,2560]{2,1,0:T(8,128)(2,1)S(1)}, bf16[1,80,2560]{2,1,0:T(8,128)(2,1)S(1)}, u32[]{:S(2)}, u32[]{:S(2)}) collective-permute-start(bf16[1,80,2560]{2,1,0:T(8,128)(2,1)S(1)} %convert_bitcast_fusion), channel_id=1, source_target_pairs={{0,8},{1,9},{2,10},{3,11},{4,12},{5,13},{6,14},{7,15},{8,0},{9,1},... | collective-permute-start | bytes 1228808 | tf_op jit(solution)/shard_map/gather_up/ppermute | solution.py:121
  50.5 24.1 %collective-permute-start.6 = (bf16[1,80,2560]{2,1,0:T(8,128)(2,1)S(1)}, bf16[1,80,2560]{2,1,0:T(8,128)(2,1)S(1)}, u32[]{:S(2)}, u32[]{:S(2)}) collective-permute-start(bf16[1,80,2560]{2,1,0:T(8,128)(2,1)S(1)} %convert_bitcast_fusion), channel_id=1, source_target_pairs={{0,16},{1,17},{2,18},{3,19},{4,20},{5,21},{6,22},{7,23},{8,24},{9,... | collective-permute-start | bytes 1228808 | tf_op jit(solution)/shard_map/gather_up/ppermute | solution.py:121
  74.6 23.9 %collective-permute-start.7 = (bf16[4,80,1920]{2,1,0:T(8,128)(2,1)S(1)}, bf16[4,80,1920]{2,1,0:T(8,128)(2,1)}, u32[]{:S(2)}, u32[]{:S(2)}) collective-permute-start(bf16[4,80,1920]{2,1,0:T(8,128)(2,1)S(1)} %collective-permute-done.3.refs_2_), channel_id=1, source_target_pairs={{0,1},{1,0},{2,6},{3,7},{4,5},{5,4},{6,2},{7,3},{8,9},{9,8},{10,14... | collective-permute-start | bytes 3686408 | tf_op jit(solution)/shard_map/gather_entry/ppermute | solution.py:121
  75.2 23.3 %collective-permute-start.8 = (bf16[4,80,1920]{2,1,0:T(8,128)(2,1)S(1)}, bf16[4,80,1920]{2,1,0:T(8,128)(2,1)S(1)}, u32[]{:S(2)}, u32[]{:S(2)}) collective-permute-start(bf16[4,80,1920]{2,1,0:T(8,128)(2,1)S(1)} %constant_dynamic-update-slice_fusion.refs_1_), channel_id=1, source_target_pairs={{0,2},{1,3},{2,0},{3,1},{4,6},{5,7},{6,4},{7,5},{8,10},{9,11},{10,... | collective-permute-start | bytes 3686408 | tf_op jit(solution)/shard_map/gather_entry/ppermute | solution.py:121
  75.2 23.3 %collective-permute-start.9 = (bf16[4,80,1920]{2,1,0:T(8,128)(2,1)S(1)}, bf16[4,80,1920]{2,1,0:T(8,128)(2,1)S(1)}, u32[]{:S(2)}, u32[]{:S(2)}) collective-permute-start(bf16[4,80,1920]{2,1,0:T(8,128)(2,1)S(1)} %collective-permute-done.3.refs_2_), channel_id=1, source_target_pairs={{0,2},{1,3},{2,0},{3,1},{4,6},{5,7},{6,4},{7,5},{8,10},{9,11},{10,... | collective-permute-start | bytes 3686408 | tf_op jit(solution)/shard_map/gather_entry/ppermute | solution.py:121
  100.6 46.1 %collective-permute-start.13 = (bf16[4,80,2560]{2,1,0:T(8,128)(2,1)}, bf16[4,80,2560]{2,1,0:T(8,128)(2,1)}, u32[]{:S(2)}, u32[]{:S(2)}) collective-permute-start(bf16[4,80,2560]{2,1,0:T(8,128)(2,1)} %pad_maximum_fusion.refs_1_), channel_id=1, source_target_pairs={{0,4},{1,5},{2,3},{3,2},{4,0},{5,1},{6,7},{7,6},{8,12},{9,13},{10,... | collective-permute-start | bytes 4915208 | tf_op jit(solution)/shard_map/gather_up/ppermute | solution.py:121
  101.0 45.7 %collective-permute-start.14 = (bf16[4,80,2560]{2,1,0:T(8,128)(2,1)}, bf16[4,80,2560]{2,1,0:T(8,128)(2,1)}, u32[]{:S(2)}, u32[]{:S(2)}) collective-permute-start(bf16[4,80,2560]{2,1,0:T(8,128)(2,1)} %pad_maximum_fusion.refs_1_), channel_id=1, source_target_pairs={{0,1},{1,0},{2,6},{3,7},{4,5},{5,4},{6,2},{7,3},{8,9},{9,8},{10,14... | collective-permute-start | bytes 4915208 | tf_op jit(solution)/shard_map/gather_up/ppermute | solution.py:121
  105.4 28.9 %collective-permute-start.15 = (bf16[1,160,1280]{2,1,0:T(8,128)(2,1)S(1)}, bf16[1,160,1280]{2,1,0:T(8,128)(2,1)S(1)}, u32[]{:S(2)}, u32[]{:S(2)}) collective-permute-start(bf16[1,160,1280]{2,1,0:T(8,128)(2,1)S(1)} %convert_bitcast_fusion.1), channel_id=1, source_target_pairs={{0,8},{1,9},{2,10},{3,11},{4,12},{5,13},{6,14},{7,15},{8,0},{9,1},... | collective-permute-start | bytes 1228808 | tf_op jit(solution)/shard_map/gather_down/ppermute | solution.py:121
  115.8 30.9 %collective-permute-start.16 = (bf16[1,160,1280]{2,1,0:T(8,128)(2,1)S(1)}, bf16[1,160,1280]{2,1,0:T(8,128)(2,1)S(1)}, u32[]{:S(2)}, u32[]{:S(2)}) collective-permute-start(bf16[1,160,1280]{2,1,0:T(8,128)(2,1)S(1)} %convert_bitcast_fusion.1), channel_id=1, source_target_pairs={{0,16},{1,17},{2,18},{3,19},{4,20},{5,21},{6,22},{7,23},{8,24},{9,... | collective-permute-start | bytes 1228808 | tf_op jit(solution)/shard_map/gather_down/ppermute | solution.py:121
  117.0 29.7 %collective-permute-start.17 = (bf16[1,160,1280]{2,1,0:T(8,128)(2,1)S(1)}, bf16[1,160,1280]{2,1,0:T(8,128)(2,1)S(1)}, u32[]{:S(2)}, u32[]{:S(2)}) collective-permute-start(bf16[1,160,1280]{2,1,0:T(8,128)(2,1)S(1)} %convert_bitcast_fusion.1), channel_id=1, source_target_pairs={{0,24},{1,25},{2,26},{3,27},{4,28},{5,29},{6,30},{7,31},{8,16},{9,... | collective-permute-start | bytes 1228808 | tf_op jit(solution)/shard_map/gather_down/ppermute | solution.py:121
  146.7 22.7 %collective-permute-start.18 = (bf16[4,80,2560]{2,1,0:T(8,128)(2,1)}, bf16[4,80,2560]{2,1,0:T(8,128)(2,1)}, u32[]{:S(2)}, u32[]{:S(2)}) collective-permute-start(bf16[4,80,2560]{2,1,0:T(8,128)(2,1)} %collective-permute-done.13.refs_2_), channel_id=1, source_target_pairs={{0,1},{1,0},{2,6},{3,7},{4,5},{5,4},{6,2},{7,3},{8,9},{9,8},{10,14... | collective-permute-start | bytes 4915208 | tf_op jit(solution)/shard_map/gather_up/ppermute | solution.py:121
  170.0 38.9 %collective-permute-start.23 = (bf16[4,160,1280]{2,1,0:T(8,128)(2,1)}, bf16[4,160,1280]{2,1,0:T(8,128)(2,1)}, u32[]{:S(2)}, u32[]{:S(2)}) collective-permute-start(bf16[4,160,1280]{2,1,0:T(8,128)(2,1)} %pad_maximum_fusion.1.refs_2_), channel_id=1, source_target_pairs={{0,4},{1,5},{2,3},{3,2},{4,0},{5,1},{6,7},{7,6},{8,12},{9,13},{10,... | collective-permute-start | bytes 4915208 | tf_op jit(solution)/shard_map/gather_down/ppermute | solution.py:121
  171.2 37.8 %collective-permute-start.24 = (bf16[4,160,1280]{2,1,0:T(8,128)(2,1)}, bf16[4,160,1280]{2,1,0:T(8,128)(2,1)}, u32[]{:S(2)}, u32[]{:S(2)}) collective-permute-start(bf16[4,160,1280]{2,1,0:T(8,128)(2,1)} %pad_maximum_fusion.1.refs_2_), channel_id=1, source_target_pairs={{0,1},{1,0},{2,6},{3,7},{4,5},{5,4},{6,2},{7,3},{8,9},{9,8},{10,14... | collective-permute-start | bytes 4915208 | tf_op jit(solution)/shard_map/gather_down/ppermute | solution.py:121
  310.4 25.7 %collective-permute-start.33 = (bf16[4,160,1280]{2,1,0:T(8,128)(2,1)}, bf16[4,160,1280]{2,1,0:T(8,128)(2,1)S(1)}, u32[]{:S(2)}, u32[]{:S(2)}) collective-permute-start(bf16[4,160,1280]{2,1,0:T(8,128)(2,1)} %shard_map.354), channel_id=1, source_target_pairs={{0,1},{1,0},{2,6},{3,7},{4,5},{5,4},{6,2},{7,3},{8,9},{9,8},{10,14... | collective-permute-start | bytes 4915208 | tf_op jit(solution)/shard_map/scatter_down/ppermute | solution.py:121
  311.3 24.8 %collective-permute-start.34 = (f32[71,1280]{1,0:T(8,128)S(1)}, f32[71,1280]{1,0:T(8,128)S(1)}, u32[]{:S(2)}, u32[]{:S(2)}) collective-permute-start(f32[71,1280]{1,0:T(8,128)S(1)} %select_add_fusion.1), channel_id=1, source_target_pairs={{0,8},{1,9},{2,10},{3,11},{4,12},{5,13},{6,14},{7,15},{8,0},{9,1},... | collective-permute-start | bytes 1090568 | tf_op jit(solution)/shard_map/sum_head/ppermute | solution.py:121
  343.0 53.9 %collective-permute-start.38 = (bf16[12,80,2560]{2,1,0:T(8,128)(2,1)}, bf16[12,80,2560]{2,1,0:T(8,128)(2,1)}, u32[]{:S(2)}, u32[]{:S(2)}) collective-permute-start(bf16[12,80,2560]{2,1,0:T(8,128)(2,1)} %get-tuple-element.474), channel_id=1, source_target_pairs={{0,2},{1,3},{2,0},{3,1},{4,6},{5,7},{6,4},{7,5},{8,10},{9,11},{10,... | collective-permute-start | bytes 14745608 | tf_op jit(solution)/shard_map/scatter_up/ppermute | solution.py:121
  343.7 53.2 %collective-permute-start.35 = (bf16[4,160,1280]{2,1,0:T(8,128)(2,1)}, bf16[4,160,1280]{2,1,0:T(8,128)(2,1)}, u32[]{:S(2)}, u32[]{:S(2)}) collective-permute-start(bf16[4,160,1280]{2,1,0:T(8,128)(2,1)} %get-tuple-element.471), channel_id=1, source_target_pairs={{0,4},{1,5},{2,3},{3,2},{4,0},{5,1},{6,7},{7,6},{8,12},{9,13},{10,... | collective-permute-start | bytes 4915208 | tf_op jit(solution)/shard_map/scatter_down/ppermute | solution.py:121
  344.9 52.0 %collective-permute-start.36 = (bf16[4,160,1280]{2,1,0:T(8,128)(2,1)}, bf16[4,160,1280]{2,1,0:T(8,128)(2,1)}, u32[]{:S(2)}, u32[]{:S(2)}) collective-permute-start(bf16[4,160,1280]{2,1,0:T(8,128)(2,1)} %get-tuple-element.472), channel_id=1, source_target_pairs={{0,1},{1,0},{2,6},{3,7},{4,5},{5,4},{6,2},{7,3},{8,9},{9,8},{10,14... | collective-permute-start | bytes 4915208 | tf_op jit(solution)/shard_map/scatter_down/ppermute | solution.py:121
  345.8 51.1 %collective-permute-start.37 = (bf16[4,80,2560]{2,1,0:T(8,128)(2,1)}, bf16[4,80,2560]{2,1,0:T(8,128)(2,1)}, u32[]{:S(2)}, u32[]{:S(2)}) collective-permute-start(bf16[4,80,2560]{2,1,0:T(8,128)(2,1)} %get-tuple-element.473), channel_id=1, source_target_pairs={{0,2},{1,3},{2,0},{3,1},{4,6},{5,7},{6,4},{7,5},{8,10},{9,11},{10,... | collective-permute-start | bytes 4915208 | tf_op jit(solution)/shard_map/scatter_up/ppermute | solution.py:121
  401.5 23.0 %collective-permute-start.42 = (bf16[4,80,2560]{2,1,0:T(8,128)(2,1)}, bf16[4,80,2560]{2,1,0:T(8,128)(2,1)}, u32[]{:S(2)}, u32[]{:S(2)}) collective-permute-start(bf16[4,80,2560]{2,1,0:T(8,128)(2,1)} %get-tuple-element.492), channel_id=1, source_target_pairs={{0,1},{1,0},{2,6},{3,7},{4,5},{5,4},{6,2},{7,3},{8,9},{9,8},{10,14... | collective-permute-start | bytes 4915208 | tf_op jit(solution)/shard_map/scatter_up/ppermute | solution.py:121
  429.2 25.9 %collective-permute-start.45 = (bf16[4,80,2560]{2,1,0:T(8,128)(2,1)}, bf16[4,80,2560]{2,1,0:T(8,128)(2,1)}, u32[]{:S(2)}, u32[]{:S(2)}) collective-permute-start(bf16[4,80,2560]{2,1,0:T(8,128)(2,1)} %get-tuple-element.511), channel_id=1, source_target_pairs={{0,4},{1,5},{2,3},{3,2},{4,0},{5,1},{6,7},{7,6},{8,12},{9,13},{10,... | collective-permute-start | bytes 4915208 | tf_op jit(solution)/shard_map/scatter_up/ppermute | solution.py:121
  455.0 22.0 %collective-permute-start.50 = (bf16[12,80,1024]{2,1,0:T(8,128)(2,1)}, bf16[12,80,1024]{2,1,0:T(8,128)(2,1)}, u32[]{:S(2)}, u32[]{:S(2)}) collective-permute-start(bf16[12,80,1024]{2,1,0:T(8,128)(2,1)} %get-tuple-element.519), channel_id=1, source_target_pairs={{0,2},{1,3},{2,0},{3,1},{4,6},{5,7},{6,4},{7,5},{8,10},{9,11},{10,... | collective-permute-start | bytes 5898248 | tf_op jit(solution)/shard_map/scatter_entry_a/ppermute | solution.py:121
  481.3 25.7 %collective-permute-start.53 = (bf16[4,80,1024]{2,1,0:T(8,128)(2,1)}, bf16[4,80,1024]{2,1,0:T(8,128)(2,1)}, u32[]{:S(2)}, u32[]{:S(2)}) collective-permute-start(bf16[4,80,1024]{2,1,0:T(8,128)(2,1)} %get-tuple-element.540), channel_id=1, source_target_pairs={{0,1},{1,0},{2,6},{3,7},{4,5},{5,4},{6,2},{7,3},{8,9},{9,8},{10,14... | collective-permute-start | bytes 1966088 | tf_op jit(solution)/shard_map/scatter_entry_a/ppermute | solution.py:121
  482.3 24.7 %collective-permute-start.54 = (bf16[4,80,896]{2,1,0:T(8,128)(2,1)}, bf16[4,80,896]{2,1,0:T(8,128)(2,1)}, u32[]{:S(2)}, u32[]{:S(2)}) collective-permute-start(bf16[4,80,896]{2,1,0:T(8,128)(2,1)} %get-tuple-element.541), channel_id=1, source_target_pairs={{0,1},{1,0},{2,6},{3,7},{4,5},{5,4},{6,2},{7,3},{8,9},{9,8},{10,14... | collective-permute-start | bytes 1720328 | tf_op jit(solution)/shard_map/scatter_entry_b/ppermute | solution.py:121
  483.4 23.6 %collective-permute-start.55 = (bf16[1,80,2560]{2,1,0:T(8,128)(2,1)}, bf16[1,80,2560]{2,1,0:T(8,128)(2,1)}, u32[]{:S(2)}, u32[]{:S(2)}) collective-permute-start(bf16[1,80,2560]{2,1,0:T(8,128)(2,1)} %get-tuple-element.542), channel_id=1, source_target_pairs={{0,8},{1,9},{2,10},{3,11},{4,12},{5,13},{6,14},{7,15},{8,0},{9,1},... | collective-permute-start | bytes 1228808 | tf_op jit(solution)/shard_map/scatter_up/ppermute | solution.py:121
  483.4 23.6 %collective-permute-start.56 = (bf16[1,80,2560]{2,1,0:T(8,128)(2,1)}, bf16[1,80,2560]{2,1,0:T(8,128)(2,1)}, u32[]{:S(2)}, u32[]{:S(2)}) collective-permute-start(bf16[1,80,2560]{2,1,0:T(8,128)(2,1)} %get-tuple-element.543), channel_id=1, source_target_pairs={{0,16},{1,17},{2,18},{3,19},{4,20},{5,21},{6,22},{7,23},{8,24},{9,... | collective-permute-start | bytes 1228808 | tf_op jit(solution)/shard_map/scatter_up/ppermute | solution.py:121
  562.6 23.0 %collective-permute-start.75 = (f32[71,1280]{1,0:T(8,128)S(1)}, f32[71,1280]{1,0:T(8,128)S(1)}, u32[]{:S(2)}, u32[]{:S(2)}) collective-permute-start(f32[71,1280]{1,0:T(8,128)S(1)} %add.325), channel_id=1, source_target_pairs={{0,2},{1,3},{2,0},{3,1},{4,6},{5,7},{6,4},{7,5},{8,10},{9,11},{10,... | collective-permute-start | bytes 1090568 | tf_op jit(solution)/shard_map/sum_head/ppermute | solution.py:121
  (131 other events, 1556.1 us)
Sparse Core Ops, SparseCore 0:
  18.5 87.7 all-gather.2

commit v4 on v3

--- a/solution.py
+++ b/solution.py
@@ -47,19 +47,6 @@
 
 def contract(left, right):
     return jnp.einsum("ti,tj->ij", left, right, preferred_element_type=jnp.float32)
-
-
-def part_loss(logits, targets, flags, token_scale):
-    summed = jnp.zeros((), jnp.float32)
-    offset = 0
-    for column, span_cols in enumerate((RB, AB, WB)):
-        section = logits[:, offset : offset + span_cols]
-        log_probs = jax.nn.log_softmax(section, axis=-1)
-        picked = (targets[column][:, None] == jnp.arange(span_cols)[None, :]).astype(jnp.float32)
-        cross = -jnp.sum(log_probs * picked, -1)
-        summed = summed + jnp.sum(flags[:, column].astype(jnp.float32) * token_scale * cross)
-        offset = offset + span_cols
-    return summed
 
 
 AXES = ("dp", "mp")
@@ -706,7 +693,10 @@
         body,
         out_shape=[jax.ShapeDtypeStruct(shape, dtype) for shape, dtype, _, _ in outs],
         grid=(steps,),
-        in_specs=[pl.BlockSpec(block, index) for _, block, index in operands],
+        in_specs=[
+            pl.BlockSpec(block, index, pipeline_mode=pl.Buffered(1 if index is fixed else 2))
+            for _, block, index in operands
+        ],
         out_specs=[pl.BlockSpec(block, index) for _, _, block, index in outs],
         compiler_params=pltpu.CompilerParams(vmem_limit_bytes=VMEM_LIMIT),
         cost_estimate=pl.CostEstimate(
@@ -790,22 +780,130 @@
     )[0]
 
 
-def hidden_out(activated, base, spread, block):
+def heads_and_back(after, head, gain, shift, scales, targets):
+    centred = after - jnp.mean(after, -1, keepdims=True)
+    inverse = lax.rsqrt(jnp.mean(centred * centred, -1, keepdims=True) + norm_eps)
+    unit = centred * inverse
+    final = (unit * gain + shift).astype(jnp.bfloat16)
+    logits = rows_by_rows(final, head)
+    lane = lax.broadcasted_iota(jnp.int32, logits.shape, 1)
+    edges = (0, RB, RB + AB, RB + AB + WB)
+    inside = [(lane >= edges[k]) & (lane < edges[k + 1]) for k in range(3)]
+    tops = [
+        jnp.max(jnp.where(mask, logits, masked_score), -1, keepdims=True) for mask in inside
+    ]
+
+    def spread_over(columns, other):
+        value = jnp.where(inside[2], columns[2], other)
+        return jnp.where(inside[0], columns[0], jnp.where(inside[1], columns[1], value))
+
+    lowered = spread_over([logits - top for top in tops], masked_score)
+    raised = jnp.exp(lowered)
+    totals = [jnp.sum(jnp.where(mask, raised, 0.0), -1, keepdims=True) for mask in inside]
+    picked = [lane == targets[:, k : k + 1] for k in range(3)]
+    loss = jnp.float32(0.0)
+    for k in range(3):
+        found = jnp.sum(jnp.where(picked[k], lowered, 0.0), -1, keepdims=True)
+        loss = loss + jnp.sum(scales[:, k : k + 1] * (jnp.log(totals[k]) - found))
+    hot = jnp.where(picked[0] | picked[1] | picked[2], 1.0, 0.0)
+    shares = raised * spread_over([1.0 / total for total in totals], 0.0) - hot
+    d_logits = (shares * spread_over([scales[:, k : k + 1] for k in range(3)], 0.0)).astype(
+        jnp.bfloat16
+    )
+    d_unit = matmul(d_logits, head) * gain
+    leaning = jnp.mean(d_unit * unit, -1, keepdims=True)
+    d_after = inverse * (d_unit - jnp.mean(d_unit, -1, keepdims=True) - unit * leaning)
+    return final, d_logits, loss, d_after
+
+
+def context_back(d_up_pre, up, after, gain, d_later, exit_all, block):
+    count, deep = d_up_pre.shape
+    wide = up.shape[0]
+    rows = (block, wide)
+
+    def body(d_up_ref, up_ref, after_ref, gain_ref, later_ref, exit_ref, *outs):
+        d_normed = rows_by_rows(d_up_ref[...], up_ref[...])
+        outs[0][...] = d_normed
+        after_rows = after_ref[...]
+        centred = after_rows - jnp.mean(after_rows, -1, keepdims=True)
+        inverse = lax.rsqrt(jnp.mean(centred * centred, -1, keepdims=True) + norm_eps)
+        unit = centred * inverse
+        d_unit = d_normed * gain_ref[...]
+        leaning = jnp.mean(d_unit * unit, -1, keepdims=True)
+        d_norm = inverse * (d_unit - jnp.mean(d_unit, -1, keepdims=True) - unit * leaning)
+        d_out = (later_ref[...] + d_norm).astype(jnp.bfloat16)
+        outs[1][...] = d_out
+        outs[2][...] = rows_by_rows(d_out, exit_ref[...]).astype(jnp.bfloat16)
+
+    return by_blocks(
+        body,
+        [
+            (d_up_pre, (block, deep), by_rows),
+            (up, up.shape, fixed),
+            (after, rows, by_rows),
+            (gain, gain.shape, fixed),
+            (d_later, rows, by_rows),
+            (exit_all, exit_all.shape, fixed),
+        ],
+        [
+            ((count, wide), jnp.float32, rows, by_rows),
+            ((count, wide), jnp.bfloat16, rows, by_rows),
+            ((count, wide), jnp.bfloat16, rows, by_rows),
+        ],
+        count // block,
+        2 * count * wide * (deep + wide),
+    )
+
+
+def hidden_out(activated, base, spread, head, gain, shift, scales, targets, block):
     count, deep = activated.shape
     wide = base.shape[1]
+    lanes = head.shape[0]
     if not spread.aligned or count % block:
         whole = spread.matrix()
-        return base + matmul(activated, whole), whole
+        after = base + matmul(activated, whole)
+        final, d_logits, loss, d_after = heads_and_back(after, head, gain, shift, scales, targets)
+        return after, final, d_logits, d_after, d_after.astype(jnp.bfloat16), loss[None], whole
 
     def body(inputs, matrices, results):
-        results[0][...] = inputs[1][...] + matmul(inputs[0][...], matrices[0][...])
-
+        after = inputs[1][...] + matmul(inputs[0][...], matrices[0][...])
+        results[0][...] = after
+        final, d_logits, loss, d_after = heads_and_back(
+            after,
+            inputs[2][...],
+            inputs[3][...],
+            inputs[4][...],
+            inputs[5][...],
+            inputs[6][...],
+        )
+        results[1][...] = final
+        results[2][...] = d_logits
+        results[3][...] = d_after
+        results[4][...] = d_after.astype(jnp.bfloat16)
+        results[5][...] = jnp.full(results[5].shape, loss)
+
+    rows = (block, wide)
     return with_matrices(
         spread.plan,
         body,
         [spread],
-        [(activated, (block, deep), by_rows), (base, (block, wide), by_rows)],
-        [((count, wide), jnp.float32, (block, wide), by_rows)],
+        [
+            (activated, (block, deep), by_rows),
+            (base, rows, by_rows),
+            (head, head.shape, fixed),
+            (gain, gain.shape, fixed),
+            (shift, shift.shape, fixed),
+            (scales, (block, 3), by_rows),
+            (targets, (block, 3), by_rows),
+        ],
+        [
+            ((count, wide), jnp.float32, rows, by_rows),
+            ((count, wide), jnp.bfloat16, rows, by_rows),
+            ((count, lanes), jnp.bfloat16, (block, lanes), by_rows),
+            ((count, wide), jnp.float32, rows, by_rows),
+            ((count, wide), jnp.bfloat16, rows, by_rows),
+            ((8 * (count // block), 128), jnp.float32, (8, 128), by_rows),
+        ],
         count // block,
         2 * count * deep * wide,
     )
@@ -920,22 +1018,44 @@
     return [((), start, size) for start, size in zip(starts, columns)]
 
 
-def moments_and_directions(scalars, gradients, states, masters, norms):
+LOSS, SQUARE, WEIGHTS, GRAD_NORM = 0, 1, 2, 5
+
+
+def number_at(row, place):
+    lane = lax.broadcasted_iota(jnp.int32, row.shape, 1)
+    return jnp.sum(jnp.where(lane == place, row, 0.0), keepdims=True)
+
+
+def row_of(numbers):
+    lane = lax.broadcasted_iota(jnp.int32, (1, 128), 1)
+    row = jnp.zeros((1, 128), jnp.float32)
+    for place, number in numbers.items():
+        row = jnp.where(lane == place, number, row)
+    return row
+
+
+def moments_and_directions(corrections, small, gradients, states, masters, norms):
     count = len(masters)
     flat = [part for parts in gradients for part in parts]
     smem = pl.BlockSpec(memory_space=pltpu.SMEM)
     vmem = pl.BlockSpec(memory_space=pltpu.VMEM)
 
-    def kernel(scalars_ref, *refs):
+    def kernel(corrections_ref, small_ref, *refs):
         parts, refs = list(refs[: len(flat)]), refs[len(flat) :]
         old, weights, refs = refs[:count], refs[count : 2 * count], refs[2 * count :]
-        (norm_grad, norm_old, norm_weight), refs = refs[:3], refs[3:]
+        (norm_old, norm_weight), refs = refs[:2], refs[2:]
         fresh, ways, refs = refs[:count], refs[count : 2 * count], refs[2 * count :]
-        norm_fresh, norm_out, squares = refs
-        clip, corr_first, corr_second = scalars_ref[0], scalars_ref[1], scalars_ref[2]
+        norm_fresh, norm_out, row_ref = refs
+        corr_first, corr_second = corrections_ref[0], corrections_ref[1]
+        head_grad, norm_grad = parts[-1][...], small_ref[:6]
+        square = number_at(small_ref[6:7], SQUARE)
+        square = square + jnp.sum(head_grad * head_grad, keepdims=True)
+        grad_norm = jnp.sqrt(square + jnp.sum(norm_grad * norm_grad, keepdims=True))
+        clip = jnp.minimum(1.0, clip_limit / grad_norm)
+        numbers = {GRAD_NORM: grad_norm}
         for k in range(count):
             mine = [parts.pop(0) for _ in gradients[k]]
-            total = jnp.float32(0.0)
+            total = jnp.zeros((1, 1), jnp.float32)
             for which, (lead, start, width) in enumerate(
                 views(masters[k], [part.shape[1] for part in gradients[k]])
             ):
@@ -956,50 +1076,62 @@
                 fresh[k][(1,) + spot] = root
                 direction = direction + weight_decay * weights[k][spot]
                 ways[k][spot] = direction
-                total = total + jnp.sum(direction * direction)
-            squares[k] = total
+                total = total + jnp.sum(direction * direction, keepdims=True)
+            numbers[k] = total
         first, root, direction = adam_step(
-            norm_old[0], norm_old[1], clip * norm_grad[...], corr_first, corr_second
+            norm_old[0], norm_old[1], clip * norm_grad, corr_first, corr_second
         )
         norm_fresh[0] = first
         norm_fresh[1] = root
         norm_out[...] = norm_weight[...] - learn_rate * direction
+        row_ref[...] = row_of(numbers)
 
     like = lambda value: jax.ShapeDtypeStruct(value.shape, jnp.float32)
     found = pl.pallas_call(
         kernel,
         out_shape=[like(state) for state in states]
         + [like(master) for master in masters]
-        + [like(norms[1]), like(norms[2]), jax.ShapeDtypeStruct((count,), jnp.float32)],
+        + [like(norms[0]), like(norms[1]), jax.ShapeDtypeStruct((1, 128), jnp.float32)],
         in_specs=[smem] + [vmem] * (len(flat) + 2 * count + 3),
-        out_specs=[vmem] * (2 * count + 2) + [smem],
+        out_specs=[vmem] * (2 * count + 3),
         compiler_params=pltpu.CompilerParams(vmem_limit_bytes=VMEM_LIMIT),
-    )(scalars, *flat, *states, *masters, *norms)
+    )(corrections, small, *flat, *states, *masters, *norms)
     return list(found[:count]), found[count : 2 * count], *found[2 * count :]
 
 
-def new_weights(steps, masters, directions):
+def new_weights(head_square, small, row, summed, masters, directions):
     count = len(masters)
     smem = pl.BlockSpec(memory_space=pltpu.SMEM)
     vmem = pl.BlockSpec(memory_space=pltpu.VMEM)
 
-    def kernel(steps_ref, *refs):
+    def kernel(head_ref, small_ref, row_ref, summed_ref, *refs):
         weights, ways, refs = refs[:count], refs[count : 2 * count], refs[2 * count :]
+        weight_norms, update_norms = {}, {}
         for k in range(count):
-            value = weights[k][...] - steps_ref[k] * ways[k][...]
+            if k < count - 1:
+                weight_norms[k] = jnp.sqrt(number_at(small_ref[6:7], WEIGHTS + k))
+                update_norms[k] = jnp.sqrt(number_at(summed_ref[...], k))
+            else:
+                weight_norms[k] = jnp.sqrt(jnp.full((1, 1), head_ref[0]))
+                update_norms[k] = jnp.sqrt(number_at(row_ref[...], k))
+            step = learn_rate * (weight_norms[k] / update_norms[k])
+            value = weights[k][...] - step * ways[k][...]
             refs[k][...] = value
             if k < count - 1:
                 refs[count + k][...] = value.astype(jnp.bfloat16)
+        refs[-1][0:1] = row_of(weight_norms)
+        refs[-1][1:2] = row_of(update_norms)
 
     found = pl.pallas_call(
         kernel,
         out_shape=[jax.ShapeDtypeStruct(master.shape, jnp.float32) for master in masters]
-        + [jax.ShapeDtypeStruct(master.shape, jnp.bfloat16) for master in masters[:-1]],
-        in_specs=[smem] + [vmem] * (2 * count),
-        out_specs=[vmem] * (2 * count - 1),
-        compiler_params=room_for(*[(master.shape, 4, 4) for master in masters]),
-    )(steps, *masters, *directions)
-    return found[:count], found[count:]
+        + [jax.ShapeDtypeStruct(master.shape, jnp.bfloat16) for master in masters[:-1]]
+        + [jax.ShapeDtypeStruct((2, 128), jnp.float32)],
+        in_specs=[smem] + [vmem] * (3 + 2 * count),
+        out_specs=[vmem] * (2 * count),
+        compiler_params=pltpu.CompilerParams(vmem_limit_bytes=VMEM_LIMIT),
+    )(head_square, small, row, summed, *masters, *directions)
+    return found[:count], found[count:-1], found[-1]
 
 
 BY_COLUMNS = ("entry", "up")
@@ -1108,23 +1240,29 @@
     (normed_two,) = start("", normed_two)
     activated, slope, up_all = hidden_forward(normed_two, whole("up"), 512)
     activated, slope = wait("down", activated, slope)
+    head_rows = head_weight.shape[0]
+    head_half = jnp.pad(head_weight.astype(jnp.bfloat16), ((0, -head_rows % 128), (0, 0)))
+    targets = jnp.stack([return_bins, action_bins + RB, reward_bins + (RB + AB)], 1)
+    scales = flag_float * token_scale[:, None]
     late = start("down", *masters.values())
     weight_local = jnp.stack([jnp.sum(master * master) for master in late])
-    (weight_local,) = wait("down", weight_local)
+    weight_local, head_half, targets, scales = wait(
+        "down", weight_local, head_half, targets, scales
+    )
     start("down")
     wait("down")
-    after_mlp, down_all = hidden_out(activated, after_attn, whole("down"), 320)
-    final_norm = layer_norm(after_mlp, norm_params[2], norm_params[5]).astype(jnp.bfloat16)
-    head_half = head_weight.astype(jnp.bfloat16)
-    logits = matmul_t(final_norm, head_half)
-    targets = (return_bins, action_bins, reward_bins)
-    loss_local, loss_pull = jax.vjp(
-        lambda values: part_loss(values, targets, valid_flags, token_scale), logits
-    )
-    d_logits = loss_pull(jnp.ones_like(loss_local))[0].astype(jnp.bfloat16)
-    d_final = matmul(d_logits, head_half)
-    d_mlp_in, _, _ = norm_back(after_mlp, norm_params[2], norm_params[5], d_final)
-    d_mlp_out = d_mlp_in.astype(jnp.bfloat16)
+    after_mlp, final_norm, d_logits, d_mlp_in, d_mlp_out, losses, down_all = hidden_out(
+        activated,
+        after_attn,
+        whole("down"),
+        head_half,
+        norm_params[2:3],
+        norm_params[5:6],
+        scales,
+        targets,
+        320,
+    )
+    loss_local = jnp.sum(losses.reshape(-1, 8, 128)[:, 0, 0]) if losses.ndim > 1 else losses[0]
 
     def leave(names, left, right, rows, widths, block):
         by_columns = names.split()[0] in ("entry_a", "up")
@@ -1137,8 +1275,7 @@
     down_rows = down_weight.shape[0]
     entry_widths = (3 * half_wide * 8 // 15, 3 * half_wide - 3 * half_wide * 8 // 15)
     leave("down", activated, d_mlp_out, down_rows, [wide], 1280)
-    head_rows = head_weight.shape[0]
-    d_head = jnp.pad(contract(d_logits, final_norm), ((0, head_rows % 2), (0, 0)))
+    d_head = contract(d_logits, final_norm)[: head_rows + head_rows % 2]
     paths["head"] = Travel("sum_head", total_steps(plan, d_head, halves=True))
     (d_mlp_out,) = start("down head", d_mlp_out)
     d_up_pre = hidden_back(d_mlp_out, slope, down_all, 512)
@@ -1147,11 +1284,10 @@
     leave("up", normed_two, d_up_pre, rows_here, [up_weight.shape[1]], 2560)
     (d_up_pre,) = wait("down head", d_up_pre)
     (d_up_pre,) = start("down up head", d_up_pre)
-    d_normed_two = project_back(d_up_pre, up_all, 256)
-    d_ln_two, _, _ = norm_back(after_attn, norm_params[1], norm_params[4], d_normed_two)
-    d_attn_out = (d_mlp_in + d_ln_two).astype(jnp.bfloat16)
+    d_normed_two, d_attn_out, d_context = context_back(
+        d_up_pre, up_all, after_attn, norm_params[1:2], d_mlp_in, exit_all, 320
+    )
     leave("exit", context, d_attn_out, exit_rows, [wide], 1280)
-    d_context = matmul_t(d_attn_out, exit_all).astype(jnp.bfloat16)
     (d_context,) = wait("down up head", d_context)
     (d_context,) = start("down up exit", d_context)
     d_projected = attend_call(
@@ -1171,8 +1307,9 @@
     d_gain_one, d_shift_one, reds, down_square = wait(
         "entry_a entry_b up head", d_gain_one, d_shift_one, reds, down_square
     )
-    late = start("entry_a up exit", after_mlp, d_final, after_attn, d_normed_two)
-    _, d_gain_three, d_shift_three = norm_back(late[0], norm_params[2], norm_params[5], late[1])
+    late = start("entry_a up exit", after_mlp, d_logits, after_attn, d_normed_two)
+    d_final = matmul(late[1], head_half)
+    _, d_gain_three, d_shift_three = norm_back(late[0], norm_params[2], norm_params[5], d_final)
     _, d_gain_two, d_shift_two = norm_back(late[2], norm_params[1], norm_params[4], late[3])
     late = wait("entry_a up exit", d_gain_two, d_shift_two, d_gain_three, d_shift_three)
     d_gain_two, d_shift_two, d_gain_three, d_shift_three = late
@@ -1209,14 +1346,10 @@
             ]
         ),
     )
-    red_norms = small[:6]
-    loss_sum, grad_total, weight_sums = small[6, 0], small[6, 1], small[6, 2:6]
-    small_square = jnp.sum(red_head * red_head) + jnp.sum(red_norms * red_norms)
-    grad_norm = jnp.sqrt(grad_total + small_square)
-    clip_factor = jnp.minimum(1.0, clip_limit / grad_norm)
-    step_float = step_count[0].astype(jnp.float32)
-    corr_first = 1.0 - jnp.power(beta_first, step_float)
-    corr_second = 1.0 - jnp.power(beta_second, step_float)
+    step_float = step_count.astype(jnp.float32)
+    corrections = jnp.concatenate(
+        [1.0 - jnp.power(beta_first, step_float), 1.0 - jnp.power(beta_second, step_float)]
+    )
     gradients = [
         [jnp.concatenate([reds["entry_a"], reds["entry_b"]], 1)],
         [reds["exit"]],
@@ -1224,28 +1357,15 @@
         [reds["down"]],
         [red_head],
     ]
-    moments, directions, norm_moments, norm_new, squares = moments_and_directions(
-        jnp.stack([clip_factor, corr_first, corr_second]),
-        gradients,
-        states,
-        masters,
-        (red_norms, norm_state, norm_params),
-    )
-    update_sums, late = total_over_devices(plan, squares[:4], (moments[4], norm_moments))
+    moments, directions, norm_moments, norm_new, row = moments_and_directions(
+        corrections, small, gradients, states, masters, (norm_state, norm_params)
+    )
+    summed, late = total_over_devices(plan, row, (moments[4], norm_moments))
     moments[4], norm_moments = late
-    weight_norms = jnp.sqrt(weight_sums)
-    update_norms = jnp.sqrt(update_sums)
-    head_wnorm = jnp.sqrt(jnp.sum(head_weight * head_weight))
-    head_unorm = jnp.sqrt(squares[4])
-    matrix_norms = jnp.stack(
-        [
-            jnp.concatenate([weight_norms, head_wnorm[None]]),
-            jnp.concatenate([update_norms, head_unorm[None]]),
-        ]
-    )
-    new, rounded = new_weights(
-        learn_rate * (matrix_norms[0] / matrix_norms[1]), masters, directions
-    )
+    new, rounded, norms = new_weights(
+        jnp.sum(head_weight * head_weight)[None], small, row, summed, masters, directions
+    )
+    loss_sum, grad_norm, matrix_norms = small[6, LOSS], row[0, GRAD_NORM], norms[:, :5]
     return (
         new[0],
         moments[0],

time: 674 us -> 657 us (0.975)
  Pallas kernels: 240 us -> 259 us
  other arithmetic: 75.6 us -> 60.6 us
  waiting for transfers between devices: 169 us -> 161 us
    pallas_call x3, Pallas kernels: 43.6 us -> 52.9 us  [by_blocks(): pl.pallas_call(body, out_shape=[jax.ShapeDtypeStruct(shape, dtype) for sh...]
    unnamed x159 -> x106, local copies, waits for them, and re-layouts: 26.7 us -> 17.7 us
    ppermute x86, waiting for transfers between devices: 169 us -> 161 us  [send(): return lax.ppermute(value, AXES, pairs)]
  transfers between devices with their start and end apart: 87 -> 87, of which waited for: 34 -> 32; matrix products, arithmetic and copies ran while one was open for 12% -> 11% of each run, Pallas kernels for 23% -> 25%
where the time goes in v4:
time: 657 us; the launch traced here: 651 us
  Pallas kernels  259 us (39%)
  waiting for transfers between devices  161 us (25%)
  starting transfers between devices  109 us (17%)
  other arithmetic  60.6 us (9%)
  local copies, waits for them, and re-layouts  30.8 us (5%)
  between operations  19.5 us (3%)
  matrix products  11.8 us (2%)
    ppermute x86, waiting for transfers between devices, send(): return lax.ppermute(value, AXES, pairs)  161 us
    ppermute x86, starting transfers between devices, send(): return lax.ppermute(value, AXES, pairs)  109 us
    pallas_call x3, Pallas kernels, with_matrices(): pl.pallas_call(kernel, out_shape=[jax.ShapeDtypeStruct(shape, dtype) for...  67.5 us
    pallas_call x3, Pallas kernels, by_blocks(): pl.pallas_call(body, out_shape=[jax.ShapeDtypeStruct(shape, dtype) for sh...  52.9 us
    pallas_call x3, Pallas kernels, weight_grad(): pl.pallas_call(kernel, out_shape=[jax.ShapeDtypeStruct((count, rows, widt...  49.8 us
    pallas_call x9, Pallas kernels, make_sums(): pl.pallas_call(kernel, out_shape=[jax.ShapeDtypeStruct((job.count,) + job...  36.2 us
    pallas_call x2, Pallas kernels, attend_call(): pl.pallas_call(functools.partial(kernel, groups, pairs), out_shape=jax.Sh...  30.4 us
    unnamed x106, local copies, waits for them, and re-layouts  17.7 us
  transfers between devices with their start and end apart: 87, of which 32 were waited for; matrix products, arithmetic and copies ran while one was open for 11% of the time, Pallas kernels for 25%

profile of v4, /device:TPU:0, one launch (start us, length us, event | category | flops | bytes accessed | tf_op | source)
XLA Modules:
  0.0 651.4 jit_solution(8093074566182871661)
XLA Ops:
  28.4 12.7 %collective-permute-done.1 = bf16[1,80,1920]{2,1,0:T(8,128)(2,1)} collective-permute-done((bf16[1,80,1920]{2,1,0:T(8,128)(2,1)}, bf16[1,80,1920]{2,1,0:T(8,128)(2,1)}, u32[]{:S(2)}, u32[]{:S(2)}) %collective-permute-start.1) | collective-permute-done | bytes 307232 | tf_op jit(solution)/shard_map/gather_entry/ppermute | solution.py:108
  47.3 6.8 %collective-permute-start.5 = (bf16[1,80,2560]{2,1,0:T(8,128)(2,1)S(1)}, bf16[1,80,2560]{2,1,0:T(8,128)(2,1)S(1)}, u32[]{:S(2)}, u32[]{:S(2)}) collective-permute-start(bf16[1,80,2560]{2,1,0:T(8,128)(2,1)S(1)} %convert_bitcast_fusion), channel_id=1, source_target_pairs={{0,8},{1,9},{2,10},{3,11},{4,12},{5,13},{6,14},{7,15},{8,0},{9,1},... | collective-permute-start | bytes 1228808 | tf_op jit(solution)/shard_map/gather_up/ppermute | solution.py:108
  55.0 20.7 %collective-permute-done.5 = bf16[1,80,2560]{2,1,0:T(8,128)(2,1)S(1)} collective-permute-done((bf16[1,80,2560]{2,1,0:T(8,128)(2,1)S(1)}, bf16[1,80,2560]{2,1,0:T(8,128)(2,1)S(1)}, u32[]{:S(2)}, u32[]{:S(2)}) %collective-permute-start.5) | collective-permute-done | bytes 409632 | tf_op jit(solution)/shard_map/gather_up/ppermute | solution.py:108
  80.9 18.3 %collective-permute-done.10 = bf16[1,80,2560]{2,1,0:T(8,128)(2,1)S(1)} collective-permute-done((bf16[1,80,2560]{2,1,0:T(8,128)(2,1)S(1)}, bf16[1,80,2560]{2,1,0:T(8,128)(2,1)S(1)}, u32[]{:S(2)}, u32[]{:S(2)}) %collective-permute-start.10) | collective-permute-done | bytes 409632 | tf_op jit(solution)/shard_map/gather_up/ppermute | solution.py:108
  111.4 11.3 %collective-permute-start.15 = (bf16[1,160,1280]{2,1,0:T(8,128)(2,1)S(1)}, bf16[1,160,1280]{2,1,0:T(8,128)(2,1)}, u32[]{:S(2)}, u32[]{:S(2)}) collective-permute-start(bf16[1,160,1280]{2,1,0:T(8,128)(2,1)S(1)} %convert_bitcast_fusion.1), channel_id=1, source_target_pairs={{0,8},{1,9},{2,10},{3,11},{4,12},{5,13},{6,14},{7,15},{8,0},{9,1},... | collective-permute-start | bytes 1228808 | tf_op jit(solution)/shard_map/gather_down/ppermute | solution.py:108
  125.1 16.0 %shard_map.348 = (bf16[640,3840]{1,0:T(8,128)(2,1)}, bf16[1280,3840]{1,0:T(8,128)(2,1)}) custom-call(s32[32]{0:T(128)} %dynamic-slice_bitcast_fusion.slots_ref, bf16[640,1280]{1,0:T(8,128)(2,1)} %add_convert_fusion.1.refs_0_.left_ref, bf16[4,80,1920]{2,1,0:T(8,128)(2,1)} %copy-done.34, bf16[4,80,1920]{2,1,0:T(8,128)(2,1)} %copy-done.43, ...), custom_call_target="tpu_custom_call" | custom-call | flops 6291456000 | bytes 16384000 | tf_op jit(solution)/shard_map/pallas_call | solution.py:623
  141.1 12.5 %collective-permute-done.16 = bf16[1,160,1280]{2,1,0:T(8,128)(2,1)} collective-permute-done((bf16[1,160,1280]{2,1,0:T(8,128)(2,1)S(1)}, bf16[1,160,1280]{2,1,0:T(8,128)(2,1)}, u32[]{:S(2)}, u32[]{:S(2)}) %collective-permute-start.16) | collective-permute-done | bytes 409632 | tf_op jit(solution)/shard_map/gather_down/ppermute | solution.py:108
  154.8 11.3 %shard_map.349 = bf16[640,1280]{1,0:T(8,128)(2,1)} custom-call(s32[4,160,1]{2,1,0:T(8,128)} %copy.67.column_ref, s32[4,1,320]{2,1,0:T(1,128)} %tile.5.row_ref, bf16[640,3840]{1,0:T(8,128)(2,1)} %get-tuple-element.408.qkv_ref), custom_call_target="tpu_custom_call" | custom-call | flops 524288000 | bytes 9830400 | tf_op jit(solution)/shard_map/pallas_call | solution.py:514
  183.6 25.9 %shard_map.350 = (bf16[640,5120]{1,0:T(8,128)(2,1)}, bf16[640,5120]{1,0:T(8,128)(2,1)}, bf16[1280,5120]{1,0:T(8,128)(2,1)}) custom-call(s32[32]{0:T(128)} %dynamic-slice_bitcast_fusion.slots_ref, bf16[640,1280]{1,0:T(8,128)(2,1)} %add_convert_fusion.refs_0_.left_ref, bf16[4,80,2560]{2,1,0:T(8,128)(2,1)} %pad_maximum_fusion.refs_1_, ...), custom_call_target="tpu_custom_call" | custom-call | flops 8388608000 | bytes 27852800 | tf_op jit(solution)/shard_map/pallas_call | solution.py:623
  209.5 7.1 %collective-permute-done.23.refs_8_ = bf16[4,160,1280]{2,1,0:T(8,128)(2,1)} collective-permute-done((bf16[4,160,1280]{2,1,0:T(8,128)(2,1)}, bf16[4,160,1280]{2,1,0:T(8,128)(2,1)}, u32[]{:S(2)}, u32[]{:S(2)}) %collective-permute-start.23) | collective-permute-done | bytes 1638432 | tf_op jit(solution)/shard_map/gather_down/ppermute | solution.py:108
  229.0 9.0 %collective-permute-done.25.refs_10_ = bf16[4,160,1280]{2,1,0:T(8,128)(2,1)} collective-permute-done((bf16[4,160,1280]{2,1,0:T(8,128)(2,1)}, bf16[4,160,1280]{2,1,0:T(8,128)(2,1)}, u32[]{:S(2)}, u32[]{:S(2)}) %collective-permute-start.25) | collective-permute-done | bytes 1638432 | tf_op jit(solution)/shard_map/gather_down/ppermute | solution.py:108
  244.2 25.6 %shard_map.351 = (f32[640,1280]{1,0:T(8,128)}, bf16[640,1280]{1,0:T(8,128)(2,1)}, bf16[640,256]{1,0:T(8,128)(2,1)}, f32[640,1280]{1,0:T(8,128)}, bf16[640,1280]{...) custom-call(s32[32]{0:T(128)} %dynamic-slice_bitcast_fusion.slots_ref, ...), custom_call_target="tpu_custom_call" | custom-call | flops 8388608000 | bytes 33784832 | tf_op jit(solution)/shard_map/pallas_call | solution.py:623
  269.8 17.1 %shard_map.352 = (bf16[16,160,1280]{2,1,0:T(8,128)(2,1)}, bf16[12,160,1280]{2,1,0:T(8,128)(2,1)}, bf16[4,160,1280]{2,1,0:T(8,128)(2,1)}) custom-call(s32[32]{0:T(128)} %dynamic-slice_bitcast_fusion.slots_ref, bf16[640,5120]{1,0:T(8,128)(2,1)} %get-tuple-element.431.refs_0_.left_ref, bf16[640,1280]{1,0:T(8,128)(2,1)} %get-tuple-element.466.right_ref.d_out_ref), custom_call_target="tpu_custom_call" | custom-call | flops 8388608000 | bytes 21299200 | tf_op jit(solution)/shard_map/pallas_call | solution.py:977
  291.4 17.1 %shard_map.353.right_ref.d_up_ref = bf16[640,5120]{1,0:T(8,128)(2,1)} custom-call(bf16[640,1280]{1,0:T(8,128)(2,1)} %get-tuple-element.466.right_ref.d_out_ref, bf16[5120,1280]{1,0:T(8,128)(2,1)} %get-tuple-element.467.matrix_ref, bf16[640,5120]{1,0:T(8,128)(2,1)} %get-tuple-element.468.slope_ref), custom_call_target="tpu_custom_call" | custom-call | flops 8388608000 | bytes 27852800 | tf_op jit(solution)/shard_map/pallas_call | solution.py:692
  315.0 7.4 %collective-permute-start.34 = (f32[71,1280]{1,0:T(8,128)S(1)}, f32[71,1280]{1,0:T(8,128)}, u32[]{:S(2)}, u32[]{:S(2)}) collective-permute-start(f32[71,1280]{1,0:T(8,128)S(1)} %select_add_fusion), channel_id=1, source_target_pairs={{0,8},{1,9},{2,10},{3,11},{4,12},{5,13},{6,14},{7,15},{8,0},{9,1},... | collective-permute-start | bytes 1090568 | tf_op jit(solution)/shard_map/sum_head/ppermute | solution.py:108
  322.4 17.6 %shard_map.355 = (bf16[16,80,2560]{2,1,0:T(8,128)(2,1)}, bf16[12,80,2560]{2,1,0:T(8,128)(2,1)}, bf16[4,80,2560]{2,1,0:T(8,128)(2,1)}) custom-call(s32[32]{0:T(128)} %dynamic-slice_bitcast_fusion.slots_ref, bf16[640,1280]{1,0:T(8,128)(2,1)} %add_convert_fusion.refs_0_.left_ref, bf16[640,5120]{1,0:T(8,128)(2,1)} %shard_map.353.right_ref.d_up_ref), custom_call_target="tpu_custom_call" | custom-call | flops 8388608000 | bytes 21299200 | tf_op jit(solution)/shard_map/pallas_call | solution.py:977
  341.2 4.9 shard_map.356
  351.1 23.8 %shard_map.357 = (f32[640,1280]{1,0:T(8,128)}, bf16[640,1280]{1,0:T(8,128)(2,1)}, bf16[640,1280]{1,0:T(8,128)(2,1)}) custom-call(bf16[640,5120]{1,0:T(8,128)(2,1)} %shard_map.353.right_ref.d_up_ref, bf16[1280,5120]{1,0:T(8,128)(2,1)} %get-tuple-element.494.up_ref, f32[640,1280]{1,0:T(8,128)} %copy-done.2, f32[1,1280]{1,0:T(1,128)} %get-tuple-element.777.gain_ref, ...), custom_call_target="tpu_custom_call" | custom-call | flops 10485760000 | bytes 36049920 | tf_op jit(solution)/shard_map/pallas_call | solution.py:692
  375.0 6.4 convolution_convert_fusion
  381.3 4.3 shard_map.359
  385.8 4.4 shard_map.358
  393.9 19.0 %shard_map.360.right_ref.rows_ref = bf16[640,3840]{1,0:T(8,128)(2,1)} custom-call(s32[4,160,1]{2,1,0:T(8,128)} %copy.67.column_ref, s32[4,1,320]{2,1,0:T(1,128)} %tile.5.row_ref, bf16[640,3840]{1,0:T(8,128)(2,1)} %get-tuple-element.408.qkv_ref, bf16[640,1280]{1,0:T(8,128)(2,1)} %get-tuple-element.515.d_context_ref), custom_call_target="tpu_custom_call" | custom-call | flops 1310720000 | bytes 24576000 | tf_op jit(solution)/shard_map/pallas_call | solution.py:514
  415.0 4.6 shard_map.361
  426.7 15.2 %shard_map.362 = (bf16[16,80,1024]{2,1,0:T(8,128)(2,1)}, bf16[12,80,1024]{2,1,0:T(8,128)(2,1)}, bf16[4,80,1024]{2,1,0:T(8,128)(2,1)}, bf16[16,80,896]{2,1,0:T(8,...) custom-call(s32[64]{0:T(128)} %pad_add_fusion.1.slots_ref, ...), custom_call_target="tpu_custom_call" | custom-call | flops 6291456000 | bytes 16384000 | tf_op jit(solution)/shard_map/pallas_call | solution.py:977
  451.6 11.9 %shard_map.364 = f32[640,1280]{1,0:T(8,128)} custom-call(bf16[640,3840]{1,0:T(8,128)(2,1)} %shard_map.360.right_ref.rows_ref, bf16[1280,3840]{1,0:T(8,128)(2,1)} %get-tuple-element.543.matrix_ref), custom_call_target="tpu_custom_call" | custom-call | flops 6291456000 | bytes 18022400 | tf_op jit(solution)/shard_map/pallas_call | solution.py:692
  481.7 14.9 %collective-permute-done.57 = f32[71,1280]{1,0:T(8,128)S(1)} collective-permute-done((f32[71,1280]{1,0:T(8,128)S(1)}, f32[71,1280]{1,0:T(8,128)S(1)}, u32[]{:S(2)}, u32[]{:S(2)}) %collective-permute-start.57) | collective-permute-done | bytes 363552 | tf_op jit(solution)/shard_map/sum_head/ppermute | solution.py:108
  497.3 4.5 shard_map.366
  520.0 7.8 %collective-permute-done.61.refs_14_.refs_18_.refs_22_ = bf16[4,40,1280]{2,1,0:T(8,128)(2,1)S(1)} collective-permute-done((bf16[4,40,1280]{2,1,0:T(8,128)(2,1)S(1)}, bf16[4,40,1280]{2,1,0:T(8,128)(2,1)S(1)}, u32[]{:S(2)}, u32[]{:S(2)}) %collective-permute-start.61) | collective-permute-done | bytes 409632 | tf_op jit(solution)/shard_map/scatter_exit/ppermute | solution.py:108
  569.6 4.9 collective-permute-done.74
  583.9 4.8 collective-permute-start.77
  605.1 12.2 %shard_map.369 = (f32[2,3,80,640]{3,2,1,0:T(8,128)}, f32[2,40,1280]{2,1,0:T(8,128)}, f32[2,80,2560]{2,1,0:T(8,128)}, f32[2,160,1280]{2,1,0:T(8,128)}, f32[2,142,...) custom-call(f32[2]{0:T(128)} %pad_maximum_fusion.5.corrections_ref, ...), custom_call_target="tpu_custom_call" | custom-call | tf_op jit(solution)/shard_map/pallas_call | solution.py:1090
  638.2 5.9 shard_map.370
  (377 shorter events, 245.7 us)
Async XLA Ops:
  7.2 161.5 %all-gather.3.cloned.1.call-start = ((), (), s32[]{:S(2)}) async-start(), calls=%async_computation | async-start | bytes 4055040 | tf_op jit(solution)/shard_map/all_gather | solution.py:1191
  15.0 26.2 %collective-permute-start.1 = (bf16[1,80,1920]{2,1,0:T(8,128)(2,1)}, bf16[1,80,1920]{2,1,0:T(8,128)(2,1)}, u32[]{:S(2)}, u32[]{:S(2)}) collective-permute-start(bf16[1,80,1920]{2,1,0:T(8,128)(2,1)} %broadcast_in_dim_reshape.2), channel_id=1, source_target_pairs={{0,16},{1,17},{2,18},{3,19},{4,20},{5,21},{6,22},{7,23},{8,24},{9,... | collective-permute-start | bytes 921608 | tf_op jit(solution)/shard_map/gather_entry/ppermute | solution.py:108
  17.6 23.6 %collective-permute-start.2 = (bf16[1,80,1920]{2,1,0:T(8,128)(2,1)}, bf16[1,80,1920]{2,1,0:T(8,128)(2,1)}, u32[]{:S(2)}, u32[]{:S(2)}) collective-permute-start(bf16[1,80,1920]{2,1,0:T(8,128)(2,1)} %broadcast_in_dim_reshape.2), channel_id=1, source_target_pairs={{0,24},{1,25},{2,26},{3,27},{4,28},{5,29},{6,30},{7,31},{8,16},{9,... | collective-permute-start | bytes 921608 | tf_op jit(solution)/shard_map/gather_entry/ppermute | solution.py:108
  44.2 31.6 %collective-permute-start.3 = (bf16[4,80,1920]{2,1,0:T(8,128)(2,1)S(1)}, bf16[4,80,1920]{2,1,0:T(8,128)(2,1)S(1)}, u32[]{:S(2)}, u32[]{:S(2)}) collective-permute-start(bf16[4,80,1920]{2,1,0:T(8,128)(2,1)S(1)} %constant_dynamic-update-slice_fusion.refs_1_), channel_id=1, source_target_pairs={{0,4},{1,5},{2,3},{3,2},{4,0},{5,1},{6,7},{7,6},{8,12},{9,13},{10,... | collective-permute-start | bytes 3686408 | tf_op jit(solution)/shard_map/gather_entry/ppermute | solution.py:108
  45.8 30.0 %collective-permute-start.4 = (bf16[4,80,1920]{2,1,0:T(8,128)(2,1)S(1)}, bf16[4,80,1920]{2,1,0:T(8,128)(2,1)}, u32[]{:S(2)}, u32[]{:S(2)}) collective-permute-start(bf16[4,80,1920]{2,1,0:T(8,128)(2,1)S(1)} %constant_dynamic-update-slice_fusion.refs_1_), channel_id=1, source_target_pairs={{0,1},{1,0},{2,6},{3,7},{4,5},{5,4},{6,2},{7,3},{8,9},{9,8},{10,14... | collective-permute-start | bytes 3686408 | tf_op jit(solution)/shard_map/gather_entry/ppermute | solution.py:108
  47.3 28.5 %collective-permute-start.5 = (bf16[1,80,2560]{2,1,0:T(8,128)(2,1)S(1)}, bf16[1,80,2560]{2,1,0:T(8,128)(2,1)S(1)}, u32[]{:S(2)}, u32[]{:S(2)}) collective-permute-start(bf16[1,80,2560]{2,1,0:T(8,128)(2,1)S(1)} %convert_bitcast_fusion), channel_id=1, source_target_pairs={{0,8},{1,9},{2,10},{3,11},{4,12},{5,13},{6,14},{7,15},{8,0},{9,1},... | collective-permute-start | bytes 1228808 | tf_op jit(solution)/shard_map/gather_up/ppermute | solution.py:108
  75.8 24.8 %collective-permute-start.7 = (bf16[4,80,1920]{2,1,0:T(8,128)(2,1)S(1)}, bf16[4,80,1920]{2,1,0:T(8,128)(2,1)}, u32[]{:S(2)}, u32[]{:S(2)}) collective-permute-start(bf16[4,80,1920]{2,1,0:T(8,128)(2,1)S(1)} %collective-permute-done.3.refs_2_), channel_id=1, source_target_pairs={{0,1},{1,0},{2,6},{3,7},{4,5},{5,4},{6,2},{7,3},{8,9},{9,8},{10,14... | collective-permute-start | bytes 3686408 | tf_op jit(solution)/shard_map/gather_entry/ppermute | solution.py:108
  78.8 22.9 %collective-permute-start.9 = (bf16[4,80,1920]{2,1,0:T(8,128)(2,1)S(1)}, bf16[4,80,1920]{2,1,0:T(8,128)(2,1)}, u32[]{:S(2)}, u32[]{:S(2)}) collective-permute-start(bf16[4,80,1920]{2,1,0:T(8,128)(2,1)S(1)} %collective-permute-done.3.refs_2_), channel_id=1, source_target_pairs={{0,2},{1,3},{2,0},{3,1},{4,6},{5,7},{6,4},{7,5},{8,10},{9,11},{10,... | collective-permute-start | bytes 3686408 | tf_op jit(solution)/shard_map/gather_entry/ppermute | solution.py:108
  103.6 50.0 %collective-permute-start.13 = (bf16[4,80,2560]{2,1,0:T(8,128)(2,1)}, bf16[4,80,2560]{2,1,0:T(8,128)(2,1)}, u32[]{:S(2)}, u32[]{:S(2)}) collective-permute-start(bf16[4,80,2560]{2,1,0:T(8,128)(2,1)} %pad_maximum_fusion.refs_1_), channel_id=1, source_target_pairs={{0,4},{1,5},{2,3},{3,2},{4,0},{5,1},{6,7},{7,6},{8,12},{9,13},{10,... | collective-permute-start | bytes 4915208 | tf_op jit(solution)/shard_map/gather_up/ppermute | solution.py:108
  105.6 48.0 %collective-permute-start.14 = (bf16[4,80,2560]{2,1,0:T(8,128)(2,1)}, bf16[4,80,2560]{2,1,0:T(8,128)(2,1)}, u32[]{:S(2)}, u32[]{:S(2)}) collective-permute-start(bf16[4,80,2560]{2,1,0:T(8,128)(2,1)} %pad_maximum_fusion.refs_1_), channel_id=1, source_target_pairs={{0,1},{1,0},{2,6},{3,7},{4,5},{5,4},{6,2},{7,3},{8,9},{9,8},{10,14... | collective-permute-start | bytes 4915208 | tf_op jit(solution)/shard_map/gather_up/ppermute | solution.py:108
  111.4 29.7 %collective-permute-start.15 = (bf16[1,160,1280]{2,1,0:T(8,128)(2,1)S(1)}, bf16[1,160,1280]{2,1,0:T(8,128)(2,1)}, u32[]{:S(2)}, u32[]{:S(2)}) collective-permute-start(bf16[1,160,1280]{2,1,0:T(8,128)(2,1)S(1)} %convert_bitcast_fusion.1), channel_id=1, source_target_pairs={{0,8},{1,9},{2,10},{3,11},{4,12},{5,13},{6,14},{7,15},{8,0},{9,1},... | collective-permute-start | bytes 1228808 | tf_op jit(solution)/shard_map/gather_down/ppermute | solution.py:108
  122.7 31.0 %collective-permute-start.16 = (bf16[1,160,1280]{2,1,0:T(8,128)(2,1)S(1)}, bf16[1,160,1280]{2,1,0:T(8,128)(2,1)}, u32[]{:S(2)}, u32[]{:S(2)}) collective-permute-start(bf16[1,160,1280]{2,1,0:T(8,128)(2,1)S(1)} %convert_bitcast_fusion.1), channel_id=1, source_target_pairs={{0,16},{1,17},{2,18},{3,19},{4,20},{5,21},{6,22},{7,23},{8,24},{9,... | collective-permute-start | bytes 1228808 | tf_op jit(solution)/shard_map/gather_down/ppermute | solution.py:108
  122.8 30.8 %collective-permute-start.17 = (bf16[1,160,1280]{2,1,0:T(8,128)(2,1)S(1)}, bf16[1,160,1280]{2,1,0:T(8,128)(2,1)}, u32[]{:S(2)}, u32[]{:S(2)}) collective-permute-start(bf16[1,160,1280]{2,1,0:T(8,128)(2,1)S(1)} %convert_bitcast_fusion.1), channel_id=1, source_target_pairs={{0,24},{1,25},{2,26},{3,27},{4,28},{5,29},{6,30},{7,31},{8,16},{9,... | collective-permute-start | bytes 1228808 | tf_op jit(solution)/shard_map/gather_down/ppermute | solution.py:108
  153.7 23.6 %collective-permute-start.18 = (bf16[4,80,2560]{2,1,0:T(8,128)(2,1)}, bf16[4,80,2560]{2,1,0:T(8,128)(2,1)}, u32[]{:S(2)}, u32[]{:S(2)}) collective-permute-start(bf16[4,80,2560]{2,1,0:T(8,128)(2,1)} %collective-permute-done.13.refs_2_), channel_id=1, source_target_pairs={{0,1},{1,0},{2,6},{3,7},{4,5},{5,4},{6,2},{7,3},{8,9},{9,8},{10,14... | collective-permute-start | bytes 4915208 | tf_op jit(solution)/shard_map/gather_up/ppermute | solution.py:108
  154.3 23.0 %collective-permute-start.19 = (bf16[4,80,2560]{2,1,0:T(8,128)(2,1)}, bf16[4,80,2560]{2,1,0:T(8,128)(2,1)}, u32[]{:S(2)}, u32[]{:S(2)}) collective-permute-start(bf16[4,80,2560]{2,1,0:T(8,128)(2,1)} %pad_maximum_fusion.refs_1_), channel_id=1, source_target_pairs={{0,2},{1,3},{2,0},{3,1},{4,6},{5,7},{6,4},{7,5},{8,10},{9,11},{10,... | collective-permute-start | bytes 4915208 | tf_op jit(solution)/shard_map/gather_up/ppermute | solution.py:108
  154.3 23.0 %collective-permute-start.20 = (bf16[4,80,2560]{2,1,0:T(8,128)(2,1)}, bf16[4,80,2560]{2,1,0:T(8,128)(2,1)}, u32[]{:S(2)}, u32[]{:S(2)}) collective-permute-start(bf16[4,80,2560]{2,1,0:T(8,128)(2,1)} %collective-permute-done.13.refs_2_), channel_id=1, source_target_pairs={{0,2},{1,3},{2,0},{3,1},{4,6},{5,7},{6,4},{7,5},{8,10},{9,11},{10,... | collective-permute-start | bytes 4915208 | tf_op jit(solution)/shard_map/gather_up/ppermute | solution.py:108
  177.9 38.7 %collective-permute-start.23 = (bf16[4,160,1280]{2,1,0:T(8,128)(2,1)}, bf16[4,160,1280]{2,1,0:T(8,128)(2,1)}, u32[]{:S(2)}, u32[]{:S(2)}) collective-permute-start(bf16[4,160,1280]{2,1,0:T(8,128)(2,1)} %pad_maximum_fusion.1.refs_7_), channel_id=1, source_target_pairs={{0,4},{1,5},{2,3},{3,2},{4,0},{5,1},{6,7},{7,6},{8,12},{9,13},{10,... | collective-permute-start | bytes 4915208 | tf_op jit(solution)/shard_map/gather_down/ppermute | solution.py:108
  179.4 37.2 %collective-permute-start.24 = (bf16[4,160,1280]{2,1,0:T(8,128)(2,1)}, bf16[4,160,1280]{2,1,0:T(8,128)(2,1)}, u32[]{:S(2)}, u32[]{:S(2)}) collective-permute-start(bf16[4,160,1280]{2,1,0:T(8,128)(2,1)} %pad_maximum_fusion.1.refs_7_), channel_id=1, source_target_pairs={{0,1},{1,0},{2,6},{3,7},{4,5},{5,4},{6,2},{7,3},{8,9},{9,8},{10,14... | collective-permute-start | bytes 4915208 | tf_op jit(solution)/shard_map/gather_down/ppermute | solution.py:108
  313.7 26.3 %collective-permute-start.33 = (bf16[4,160,1280]{2,1,0:T(8,128)(2,1)}, bf16[4,160,1280]{2,1,0:T(8,128)(2,1)}, u32[]{:S(2)}, u32[]{:S(2)}) collective-permute-start(bf16[4,160,1280]{2,1,0:T(8,128)(2,1)} %shard_map.354), channel_id=1, source_target_pairs={{0,1},{1,0},{2,6},{3,7},{4,5},{5,4},{6,2},{7,3},{8,9},{9,8},{10,14... | collective-permute-start | bytes 4915208 | tf_op jit(solution)/shard_map/scatter_down/ppermute | solution.py:108
  315.0 25.1 %collective-permute-start.34 = (f32[71,1280]{1,0:T(8,128)S(1)}, f32[71,1280]{1,0:T(8,128)}, u32[]{:S(2)}, u32[]{:S(2)}) collective-permute-start(f32[71,1280]{1,0:T(8,128)S(1)} %select_add_fusion), channel_id=1, source_target_pairs={{0,8},{1,9},{2,10},{3,11},{4,12},{5,13},{6,14},{7,15},{8,0},{9,1},... | collective-permute-start | bytes 1090568 | tf_op jit(solution)/shard_map/sum_head/ppermute | solution.py:108
  346.0 39.7 %collective-permute-start.38 = (bf16[12,80,2560]{2,1,0:T(8,128)(2,1)}, bf16[12,80,2560]{2,1,0:T(8,128)(2,1)}, u32[]{:S(2)}, u32[]{:S(2)}) collective-permute-start(bf16[12,80,2560]{2,1,0:T(8,128)(2,1)} %get-tuple-element.491), channel_id=1, source_target_pairs={{0,2},{1,3},{2,0},{3,1},{4,6},{5,7},{6,4},{7,5},{8,10},{9,11},{10,... | collective-permute-start | bytes 14745608 | tf_op jit(solution)/shard_map/scatter_up/ppermute | solution.py:108
  346.0 39.7 %collective-permute-start.35 = (bf16[4,160,1280]{2,1,0:T(8,128)(2,1)}, bf16[4,160,1280]{2,1,0:T(8,128)(2,1)}, u32[]{:S(2)}, u32[]{:S(2)}) collective-permute-start(bf16[4,160,1280]{2,1,0:T(8,128)(2,1)} %get-tuple-element.488), channel_id=1, source_target_pairs={{0,4},{1,5},{2,3},{3,2},{4,0},{5,1},{6,7},{7,6},{8,12},{9,13},{10,... | collective-permute-start | bytes 4915208 | tf_op jit(solution)/shard_map/scatter_down/ppermute | solution.py:108
  346.7 39.0 %collective-permute-start.36 = (bf16[4,160,1280]{2,1,0:T(8,128)(2,1)}, bf16[4,160,1280]{2,1,0:T(8,128)(2,1)}, u32[]{:S(2)}, u32[]{:S(2)}) collective-permute-start(bf16[4,160,1280]{2,1,0:T(8,128)(2,1)} %get-tuple-element.489), channel_id=1, source_target_pairs={{0,1},{1,0},{2,6},{3,7},{4,5},{5,4},{6,2},{7,3},{8,9},{9,8},{10,14... | collective-permute-start | bytes 4915208 | tf_op jit(solution)/shard_map/scatter_down/ppermute | solution.py:108
  348.0 37.8 %collective-permute-start.37 = (bf16[4,80,2560]{2,1,0:T(8,128)(2,1)}, bf16[4,80,2560]{2,1,0:T(8,128)(2,1)}, u32[]{:S(2)}, u32[]{:S(2)}) collective-permute-start(bf16[4,80,2560]{2,1,0:T(8,128)(2,1)} %get-tuple-element.490), channel_id=1, source_target_pairs={{0,2},{1,3},{2,0},{3,1},{4,6},{5,7},{6,4},{7,5},{8,10},{9,11},{10,... | collective-permute-start | bytes 4915208 | tf_op jit(solution)/shard_map/scatter_up/ppermute | solution.py:108
  348.0 37.7 %collective-permute-start.39 = (f32[71,1280]{1,0:T(8,128)S(1)}, f32[71,1280]{1,0:T(8,128)}, u32[]{:S(2)}, u32[]{:S(2)}) collective-permute-start(f32[71,1280]{1,0:T(8,128)S(1)} %add.262), channel_id=1, source_target_pairs={{0,16},{1,17},{2,18},{3,19},{4,20},{5,21},{6,22},{7,23},{8,24},{9,... | collective-permute-start | bytes 1090568 | tf_op jit(solution)/shard_map/sum_head/ppermute | solution.py:108
  390.2 24.8 %collective-permute-start.42 = (bf16[4,80,2560]{2,1,0:T(8,128)(2,1)}, bf16[4,80,2560]{2,1,0:T(8,128)(2,1)}, u32[]{:S(2)}, u32[]{:S(2)}) collective-permute-start(bf16[4,80,2560]{2,1,0:T(8,128)(2,1)} %get-tuple-element.512), channel_id=1, source_target_pairs={{0,1},{1,0},{2,6},{3,7},{4,5},{5,4},{6,2},{7,3},{8,9},{9,8},{10,14... | collective-permute-start | bytes 4915208 | tf_op jit(solution)/shard_map/scatter_up/ppermute | solution.py:108
  391.2 23.7 %collective-permute-start.44 = (bf16[12,40,1280]{2,1,0:T(8,128)(2,1)}, bf16[12,40,1280]{2,1,0:T(8,128)(2,1)}, u32[]{:S(2)}, u32[]{:S(2)}) collective-permute-start(bf16[12,40,1280]{2,1,0:T(8,128)(2,1)} %get-tuple-element.514), channel_id=1, source_target_pairs={{0,2},{1,3},{2,0},{3,1},{4,6},{5,7},{6,4},{7,5},{8,10},{9,11},{10,... | collective-permute-start | bytes 3686408 | tf_op jit(solution)/shard_map/scatter_exit/ppermute | solution.py:108
  419.5 25.9 %collective-permute-start.45 = (bf16[4,80,2560]{2,1,0:T(8,128)(2,1)}, bf16[4,80,2560]{2,1,0:T(8,128)(2,1)}, u32[]{:S(2)}, u32[]{:S(2)}) collective-permute-start(bf16[4,80,2560]{2,1,0:T(8,128)(2,1)} %get-tuple-element.531), channel_id=1, source_target_pairs={{0,4},{1,5},{2,3},{3,2},{4,0},{5,1},{6,7},{7,6},{8,12},{9,13},{10,... | collective-permute-start | bytes 4915208 | tf_op jit(solution)/shard_map/scatter_up/ppermute | solution.py:108
  471.7 25.7 %collective-permute-start.53 = (bf16[4,80,1024]{2,1,0:T(8,128)(2,1)}, bf16[4,80,1024]{2,1,0:T(8,128)(2,1)}, u32[]{:S(2)}, u32[]{:S(2)}) collective-permute-start(bf16[4,80,1024]{2,1,0:T(8,128)(2,1)} %get-tuple-element.560), channel_id=1, source_target_pairs={{0,1},{1,0},{2,6},{3,7},{4,5},{5,4},{6,2},{7,3},{8,9},{9,8},{10,14... | collective-permute-start | bytes 1966088 | tf_op jit(solution)/shard_map/scatter_entry_a/ppermute | solution.py:108
  472.1 25.2 %collective-permute-start.54 = (bf16[4,80,896]{2,1,0:T(8,128)(2,1)}, bf16[4,80,896]{2,1,0:T(8,128)(2,1)}, u32[]{:S(2)}, u32[]{:S(2)}) collective-permute-start(bf16[4,80,896]{2,1,0:T(8,128)(2,1)} %get-tuple-element.561), channel_id=1, source_target_pairs={{0,1},{1,0},{2,6},{3,7},{4,5},{5,4},{6,2},{7,3},{8,9},{9,8},{10,14... | collective-permute-start | bytes 1720328 | tf_op jit(solution)/shard_map/scatter_entry_b/ppermute | solution.py:108
  473.8 23.6 %collective-permute-start.55 = (bf16[1,80,2560]{2,1,0:T(8,128)(2,1)}, bf16[1,80,2560]{2,1,0:T(8,128)(2,1)}, u32[]{:S(2)}, u32[]{:S(2)}) collective-permute-start(bf16[1,80,2560]{2,1,0:T(8,128)(2,1)} %get-tuple-element.562), channel_id=1, source_target_pairs={{0,8},{1,9},{2,10},{3,11},{4,12},{5,13},{6,14},{7,15},{8,0},{9,1},... | collective-permute-start | bytes 1228808 | tf_op jit(solution)/shard_map/scatter_up/ppermute | solution.py:108
  473.8 23.6 %collective-permute-start.56 = (bf16[1,80,2560]{2,1,0:T(8,128)(2,1)}, bf16[1,80,2560]{2,1,0:T(8,128)(2,1)}, u32[]{:S(2)}, u32[]{:S(2)}) collective-permute-start(bf16[1,80,2560]{2,1,0:T(8,128)(2,1)} %get-tuple-element.563), channel_id=1, source_target_pairs={{0,16},{1,17},{2,18},{3,19},{4,20},{5,21},{6,22},{7,23},{8,24},{9,... | collective-permute-start | bytes 1228808 | tf_op jit(solution)/shard_map/scatter_up/ppermute | solution.py:108
  (104 other events, 1216.8 us)
Sparse Core Ops, SparseCore 0:
  20.9 89.0 all-gather.2

commit v5 on v4

--- a/solution.py
+++ b/solution.py
@@ -1072,8 +1072,12 @@
                     corr_first,
                     corr_second,
                 )
-                fresh[k][(0,) + spot] = first
-                fresh[k][(1,) + spot] = root
+                if k < count - 1:
+                    fresh[k][(0,) + spot] = first
+                    fresh[k][(1,) + spot] = root
+                else:
+                    fresh[k][:, 0, :] = first
+                    fresh[k][:, 1, :] = root
                 direction = direction + weight_decay * weights[k][spot]
                 ways[k][spot] = direction
                 total = total + jnp.sum(direction * direction, keepdims=True)
@@ -1087,16 +1091,19 @@
         row_ref[...] = row_of(numbers)
 
     like = lambda value: jax.ShapeDtypeStruct(value.shape, jnp.float32)
+    head_rows, wide = masters[-1].shape
     found = pl.pallas_call(
         kernel,
-        out_shape=[like(state) for state in states]
+        out_shape=[like(state) for state in states[:-1]]
+        + [jax.ShapeDtypeStruct((head_rows, 2, wide), jnp.float32)]
         + [like(master) for master in masters]
         + [like(norms[0]), like(norms[1]), jax.ShapeDtypeStruct((1, 128), jnp.float32)],
         in_specs=[smem] + [vmem] * (len(flat) + 2 * count + 3),
         out_specs=[vmem] * (2 * count + 3),
         compiler_params=pltpu.CompilerParams(vmem_limit_bytes=VMEM_LIMIT),
     )(corrections, small, *flat, *states, *masters, *norms)
-    return list(found[:count]), found[count : 2 * count], *found[2 * count :]
+    fresh = list(found[: count - 1]) + [found[count - 1].transpose(1, 0, 2)]
+    return fresh, found[count : 2 * count], *found[2 * count :]
 
 
 def new_weights(head_square, small, row, summed, masters, directions):
@@ -1178,7 +1185,7 @@
         for name, shard, split in (
             ("entry", entry_shard, ()),
             ("up", halves["up"], ((0, 1), (2,))),
-            ("down", halves["down"], ()),
+            ("down", halves["down"], ((0, 1), (2,))),
         )
     }
     game_match = (row_games[:, None] == jnp.arange(GAMES)[None, :]).astype(jnp.float32)
@@ -1188,38 +1195,38 @@
     tens = jnp.floor(local_counts / 64.0)
     pair = jnp.concatenate([tens, local_counts - 64.0 * tens]).astype(jnp.bfloat16)
     below = jnp.zeros((16 - exit_rows % 16, wide), jnp.bfloat16).at[0, : 2 * GAMES].set(pair)
-    gathered = lax.all_gather(jnp.concatenate([halves["exit"], below]), ("mp", "dp"), axis=0)
+    exit_shard = jnp.concatenate([halves["exit"], below])
+    slots = jnp.asarray(path_table(plan), jnp.int32)[here]
+
+    def chosen(names):
+        return [paths[name] for name in names.split() if paths[name].wanted]
+
+    def start(names, *more):
+        return clock.start(chosen(names), more)
+
+    def wait(names, *more):
+        return clock.wait([path for path in chosen(names) if path.going], more)
+
+    def finish(name):
+        while paths[name].wanted:
+            start(name)
+            wait(name)
+        return paths[name].result
+
+    def whole(name):
+        return Spread(plan, [(finish(name), slots)], name in BY_COLUMNS)
+
+
+    resid, gains = start("entry", tokens.astype(jnp.float32), norm_params)
+    normed_one = layer_norm(resid, gains[0], gains[3]).astype(jnp.bfloat16)
+    (normed_one,) = wait("entry", normed_one)
+    (exit_shard,) = start("entry up", exit_shard)
+    gathered = lax.all_gather(exit_shard, ("mp", "dp"), axis=0)
     exit_all = gathered[:, :exit_rows].reshape(-1, wide)
     pairs_all = jnp.sum(gathered[:, exit_rows, : 2 * GAMES].astype(jnp.float32), 0)
     counts_all = 64.0 * pairs_all[:GAMES] + pairs_all[GAMES:]
     inverse = 1.0 / (GAMES * jnp.maximum(counts_all, 1.0))
     token_scale = jnp.sum(game_match * inverse[None, :], -1)
-
-    slots = jnp.asarray(path_table(plan), jnp.int32)[here]
-
-    def chosen(names):
-        return [paths[name] for name in names.split() if paths[name].wanted]
-
-    def start(names, *more):
-        return clock.start(chosen(names), more)
-
-    def wait(names, *more):
-        return clock.wait([path for path in chosen(names) if path.going], more)
-
-    def finish(name):
-        while paths[name].wanted:
-            start(name)
-            wait(name)
-        return paths[name].result
-
-    def whole(name):
-        return Spread(plan, [(finish(name), slots)], name in BY_COLUMNS)
-
-
-    resid, gains = start("entry", tokens.astype(jnp.float32), norm_params)
-    normed_one = layer_norm(resid, gains[0], gains[3]).astype(jnp.bfloat16)
-    (normed_one,) = wait("entry", normed_one)
-    start("entry up")
     wait("entry up")
     start("entry up")
     wait("entry up")
@@ -1228,13 +1235,13 @@
     (normed_one,) = start("down", normed_one)
     projected, entry_all = project(normed_one, whole("entry"), 768)
     (projected,) = wait("up down", projected)
-    (projected,) = start("up", projected)
+    (projected,) = start("up down", projected)
     context = attend_call(
         attend_kernel, segments, projected, [], tokens.shape[1], plan.mp, 2
     )
     after_attn = resid + matmul(context, exit_all)
     normed_two = layer_norm(after_attn, norm_params[1], norm_params[4]).astype(jnp.bfloat16)
-    after_attn, normed_two = wait("up", after_attn, normed_two)
+    after_attn, normed_two = wait("up down", after_attn, normed_two)
     (normed_two,) = start("up down", normed_two)
     wait("up")
     (normed_two,) = start("", normed_two)
@@ -1318,14 +1325,15 @@
     up_square = jnp.sum(reds["up"] * reds["up"])
     reds, up_square = wait("entry_b entry_a head", reds, up_square)
     start("entry_b exit head")
-    wait("entry_b exit head")
+    reds["entry_a"] = finish("entry_a")
+    entry_square = jnp.sum(reds["entry_a"] * reds["entry_a"])
+    reds, entry_square = wait("entry_b exit head", reds, entry_square)
     reds["exit"] = finish("exit")
     exit_square = jnp.sum(reds["exit"] * reds["exit"])
     red_head = finish("head")[:head_rows]
-    reds["entry_a"], reds["entry_b"] = finish("entry_a"), finish("entry_b")
-    local_square = down_square + up_square + exit_square
-    for name in ("entry_a", "entry_b"):
-        local_square = local_square + jnp.sum(reds[name] * reds[name])
+    reds["entry_b"] = finish("entry_b")
+    local_square = down_square + up_square + exit_square + entry_square
+    local_square = local_square + jnp.sum(reds["entry_b"] * reds["entry_b"])
     masters = [entry_weight, exit_weight, up_weight, down_weight, head_weight]
     states = [entry_state, exit_state, up_state, down_state, head_state]
     wide = norm_params.shape[1]

time: 657 us -> 646 us (0.983)
  waiting for transfers between devices: 161 us -> 144 us
    ppermute x86, waiting for transfers between devices: 161 us -> 144 us  [send(): return lax.ppermute(value, AXES, pairs)]
    unnamed x106 -> x95, local copies, waits for them, and re-layouts: 17.7 us -> 16.3 us
  transfers between devices with their start and end apart: 87 -> 87, of which waited for: 32 -> 35; matrix products, arithmetic and copies ran while one was open for 11% -> 12% of each run, Pallas kernels for 25% -> 26%
where the time goes in v5:
time: 646 us; the launch traced here: 640 us
  Pallas kernels  260 us (40%)
  waiting for transfers between devices  144 us (22%)
  starting transfers between devices  106 us (16%)
  other arithmetic  65.1 us (10%)
  local copies, waits for them, and re-layouts  33.2 us (5%)
  between operations  19.5 us (3%)
  matrix products  11.8 us (2%)
    ppermute x86, waiting for transfers between devices, send(): return lax.ppermute(value, AXES, pairs)  144 us
    ppermute x86, starting transfers between devices, send(): return lax.ppermute(value, AXES, pairs)  106 us
    pallas_call x3, Pallas kernels, with_matrices(): pl.pallas_call(kernel, out_shape=[jax.ShapeDtypeStruct(shape, dtype) for...  67.8 us
    pallas_call x3, Pallas kernels, by_blocks(): pl.pallas_call(body, out_shape=[jax.ShapeDtypeStruct(shape, dtype) for sh...  52.9 us
    pallas_call x3, Pallas kernels, weight_grad(): pl.pallas_call(kernel, out_shape=[jax.ShapeDtypeStruct((count, rows, widt...  49.8 us
    pallas_call x9, Pallas kernels, make_sums(): pl.pallas_call(kernel, out_shape=[jax.ShapeDtypeStruct((job.count,) + job...  36.5 us
    pallas_call x2, Pallas kernels, attend_call(): pl.pallas_call(functools.partial(kernel, groups, pairs), out_shape=jax.Sh...  30.4 us
    unnamed x95, local copies, waits for them, and re-layouts  16.3 us
  transfers between devices with their start and end apart: 87, of which 35 were waited for; matrix products, arithmetic and copies ran while one was open for 12% of the time, Pallas kernels for 26%

profile of v5, /device:TPU:0, one launch (start us, length us, event | category | flops | bytes accessed | tf_op | source)
XLA Modules:
  0.0 639.8 jit_solution(6209039198319204599)
XLA Ops:
  31.7 7.8 %collective-permute-done.1 = bf16[1,80,1920]{2,1,0:T(8,128)(2,1)} collective-permute-done((bf16[1,80,1920]{2,1,0:T(8,128)(2,1)}, bf16[1,80,1920]{2,1,0:T(8,128)(2,1)}, u32[]{:S(2)}, u32[]{:S(2)}) %collective-permute-start.1) | collective-permute-done | bytes 307232 | tf_op jit(solution)/shard_map/gather_entry/ppermute | solution.py:108
  47.7 5.7 collective-permute-start.5
  54.5 18.2 %collective-permute-done.5 = bf16[1,80,2560]{2,1,0:T(8,128)(2,1)S(1)} collective-permute-done((bf16[1,80,2560]{2,1,0:T(8,128)(2,1)}, bf16[1,80,2560]{2,1,0:T(8,128)(2,1)S(1)}, u32[]{:S(2)}, u32[]{:S(2)}) %collective-permute-start.5) | collective-permute-done | bytes 409632 | tf_op jit(solution)/shard_map/gather_up/ppermute | solution.py:108
  78.8 13.8 %collective-permute-done.10 = bf16[1,80,2560]{2,1,0:T(8,128)(2,1)S(1)} collective-permute-done((bf16[1,80,2560]{2,1,0:T(8,128)(2,1)}, bf16[1,80,2560]{2,1,0:T(8,128)(2,1)S(1)}, u32[]{:S(2)}, u32[]{:S(2)}) %collective-permute-start.10) | collective-permute-done | bytes 409632 | tf_op jit(solution)/shard_map/gather_up/ppermute | solution.py:108
  105.6 9.7 %collective-permute-start.15 = (bf16[1,160,1280]{2,1,0:T(8,128)(2,1)}, bf16[1,160,1280]{2,1,0:T(8,128)(2,1)}, u32[]{:S(2)}, u32[]{:S(2)}) collective-permute-start(bf16[1,160,1280]{2,1,0:T(8,128)(2,1)} %convert_bitcast_fusion.1), channel_id=1, source_target_pairs={{0,8},{1,9},{2,10},{3,11},{4,12},{5,13},{6,14},{7,15},{8,0},{9,1},... | collective-permute-start | bytes 1228808 | tf_op jit(solution)/shard_map/gather_down/ppermute | solution.py:108
  116.3 16.1 %shard_map.348 = (bf16[640,3840]{1,0:T(8,128)(2,1)}, bf16[1280,3840]{1,0:T(8,128)(2,1)}) custom-call(s32[32]{0:T(128)} %dynamic-slice_bitcast_fusion.slots_ref, bf16[640,1280]{1,0:T(8,128)(2,1)} %add_convert_fusion.1.refs_0_.left_ref, bf16[4,80,1920]{2,1,0:T(8,128)(2,1)} %constant_dynamic-update-slice_fusion.refs_1_, bf16[4,80,1920]{2,1,0:T(8,128)(2,1)} %copy-done.39, ...), custom_call_target="tpu_custom_call" | custom-call | flops 6291456000 | bytes 16384000 | tf_op jit(solution)/shard_map/pallas_call | solution.py:623
  132.4 5.5 collective-permute-done.15
  137.9 6.0 collective-permute-done.13.refs_2_
  147.9 11.3 %shard_map.349 = bf16[640,1280]{1,0:T(8,128)(2,1)} custom-call(s32[4,160,1]{2,1,0:T(8,128)} %copy.65.column_ref, s32[4,1,320]{2,1,0:T(1,128)} %tile.5.row_ref, bf16[640,3840]{1,0:T(8,128)(2,1)} %get-tuple-element.413.qkv_ref), custom_call_target="tpu_custom_call" | custom-call | flops 524288000 | bytes 9830400 | tf_op jit(solution)/shard_map/pallas_call | solution.py:514
  176.5 26.0 %shard_map.350 = (bf16[640,5120]{1,0:T(8,128)(2,1)}, bf16[640,5120]{1,0:T(8,128)(2,1)}, bf16[1280,5120]{1,0:T(8,128)(2,1)}) custom-call(s32[32]{0:T(128)} %dynamic-slice_bitcast_fusion.slots_ref, bf16[640,1280]{1,0:T(8,128)(2,1)} %add_convert_fusion.refs_0_.left_ref, bf16[4,80,2560]{2,1,0:T(8,128)(2,1)} %pad_maximum_fusion.refs_1_, ...), custom_call_target="tpu_custom_call" | custom-call | flops 8388608000 | bytes 27852800 | tf_op jit(solution)/shard_map/pallas_call | solution.py:623
  202.6 7.1 %collective-permute-done.23.refs_8_ = bf16[4,160,1280]{2,1,0:T(8,128)(2,1)} collective-permute-done((bf16[4,160,1280]{2,1,0:T(8,128)(2,1)}, bf16[4,160,1280]{2,1,0:T(8,128)(2,1)}, u32[]{:S(2)}, u32[]{:S(2)}) %collective-permute-start.23) | collective-permute-done | bytes 1638432 | tf_op jit(solution)/shard_map/gather_down/ppermute | solution.py:108
  221.8 9.2 %collective-permute-done.25.refs_10_ = bf16[4,160,1280]{2,1,0:T(8,128)(2,1)} collective-permute-done((bf16[4,160,1280]{2,1,0:T(8,128)(2,1)}, bf16[4,160,1280]{2,1,0:T(8,128)(2,1)}, u32[]{:S(2)}, u32[]{:S(2)}) %collective-permute-start.25) | collective-permute-done | bytes 1638432 | tf_op jit(solution)/shard_map/gather_down/ppermute | solution.py:108
  237.3 25.8 %shard_map.351 = (f32[640,1280]{1,0:T(8,128)}, bf16[640,1280]{1,0:T(8,128)(2,1)}, bf16[640,256]{1,0:T(8,128)(2,1)}, f32[640,1280]{1,0:T(8,128)}, bf16[640,1280]{...) custom-call(s32[32]{0:T(128)} %dynamic-slice_bitcast_fusion.slots_ref, ...), custom_call_target="tpu_custom_call" | custom-call | flops 8388608000 | bytes 33784832 | tf_op jit(solution)/shard_map/pallas_call | solution.py:623
  263.0 17.0 %shard_map.352 = (bf16[16,160,1280]{2,1,0:T(8,128)(2,1)}, bf16[12,160,1280]{2,1,0:T(8,128)(2,1)}, bf16[4,160,1280]{2,1,0:T(8,128)(2,1)}) custom-call(s32[32]{0:T(128)} %dynamic-slice_bitcast_fusion.slots_ref, bf16[640,5120]{1,0:T(8,128)(2,1)} %get-tuple-element.437.refs_0_.left_ref, bf16[640,1280]{1,0:T(8,128)(2,1)} %get-tuple-element.472.right_ref.d_out_ref), custom_call_target="tpu_custom_call" | custom-call | flops 8388608000 | bytes 21299200 | tf_op jit(solution)/shard_map/pallas_call | solution.py:977
  284.6 17.1 %shard_map.353.right_ref.d_up_ref = bf16[640,5120]{1,0:T(8,128)(2,1)} custom-call(bf16[640,1280]{1,0:T(8,128)(2,1)} %get-tuple-element.472.right_ref.d_out_ref, bf16[5120,1280]{1,0:T(8,128)(2,1)} %get-tuple-element.473.matrix_ref, bf16[640,5120]{1,0:T(8,128)(2,1)} %get-tuple-element.474.slope_ref), custom_call_target="tpu_custom_call" | custom-call | flops 8388608000 | bytes 27852800 | tf_op jit(solution)/shard_map/pallas_call | solution.py:692
  308.0 5.2 collective-permute-start.34
  313.2 17.6 %shard_map.355 = (bf16[16,80,2560]{2,1,0:T(8,128)(2,1)}, bf16[12,80,2560]{2,1,0:T(8,128)(2,1)}, bf16[4,80,2560]{2,1,0:T(8,128)(2,1)}) custom-call(s32[32]{0:T(128)} %dynamic-slice_bitcast_fusion.slots_ref, bf16[640,1280]{1,0:T(8,128)(2,1)} %add_convert_fusion.refs_0_.left_ref, bf16[640,5120]{1,0:T(8,128)(2,1)} %shard_map.353.right_ref.d_up_ref), custom_call_target="tpu_custom_call" | custom-call | flops 8388608000 | bytes 21299200 | tf_op jit(solution)/shard_map/pallas_call | solution.py:977
  332.0 4.9 shard_map.356
  341.9 23.9 %shard_map.357 = (f32[640,1280]{1,0:T(8,128)}, bf16[640,1280]{1,0:T(8,128)(2,1)}, bf16[640,1280]{1,0:T(8,128)(2,1)}) custom-call(bf16[640,5120]{1,0:T(8,128)(2,1)} %shard_map.353.right_ref.d_up_ref, bf16[1280,5120]{1,0:T(8,128)(2,1)} %get-tuple-element.500.up_ref, f32[640,1280]{1,0:T(8,128)} %copy-done.2, f32[1,1280]{1,0:T(1,128)} %get-tuple-element.787.gain_ref, ...), custom_call_target="tpu_custom_call" | custom-call | flops 10485760000 | bytes 36049920 | tf_op jit(solution)/shard_map/pallas_call | solution.py:692
  365.8 6.4 convolution_convert_fusion
  376.5 4.4 shard_map.358
  384.9 19.0 %shard_map.360.right_ref.rows_ref = bf16[640,3840]{1,0:T(8,128)(2,1)} custom-call(s32[4,160,1]{2,1,0:T(8,128)} %copy.65.column_ref, s32[4,1,320]{2,1,0:T(1,128)} %tile.5.row_ref, bf16[640,3840]{1,0:T(8,128)(2,1)} %get-tuple-element.413.qkv_ref, bf16[640,1280]{1,0:T(8,128)(2,1)} %get-tuple-element.521.d_context_ref), custom_call_target="tpu_custom_call" | custom-call | flops 1310720000 | bytes 24576000 | tf_op jit(solution)/shard_map/pallas_call | solution.py:514
  405.6 4.6 shard_map.361
  417.7 15.2 %shard_map.362 = (bf16[16,80,1024]{2,1,0:T(8,128)(2,1)}, bf16[12,80,1024]{2,1,0:T(8,128)(2,1)}, bf16[4,80,1024]{2,1,0:T(8,128)(2,1)}, bf16[16,80,896]{2,1,0:T(8,...) custom-call(s32[64]{0:T(128)} %pad_add_fusion.1.slots_ref, ...), custom_call_target="tpu_custom_call" | custom-call | flops 6291456000 | bytes 16384000 | tf_op jit(solution)/shard_map/pallas_call | solution.py:977
  442.8 11.9 %shard_map.364 = f32[640,1280]{1,0:T(8,128)} custom-call(bf16[640,3840]{1,0:T(8,128)(2,1)} %shard_map.360.right_ref.rows_ref, bf16[1280,3840]{1,0:T(8,128)(2,1)} %get-tuple-element.549.matrix_ref), custom_call_target="tpu_custom_call" | custom-call | flops 6291456000 | bytes 18022400 | tf_op jit(solution)/shard_map/pallas_call | solution.py:692
  472.1 15.1 %collective-permute-done.57 = f32[71,1280]{1,0:T(8,128)S(1)} collective-permute-done((f32[71,1280]{1,0:T(8,128)S(1)}, f32[71,1280]{1,0:T(8,128)S(1)}, u32[]{:S(2)}, u32[]{:S(2)}) %collective-permute-start.57) | collective-permute-done | bytes 363552 | tf_op jit(solution)/shard_map/sum_head/ppermute | solution.py:108
  487.9 4.8 shard_map.366
  511.1 7.5 %collective-permute-done.61.refs_14_.refs_18_.refs_22_ = bf16[4,40,1280]{2,1,0:T(8,128)(2,1)S(1)} collective-permute-done((bf16[4,40,1280]{2,1,0:T(8,128)(2,1)S(1)}, bf16[4,40,1280]{2,1,0:T(8,128)(2,1)S(1)}, u32[]{:S(2)}, u32[]{:S(2)}) %collective-permute-start.61) | collective-permute-done | bytes 409632 | tf_op jit(solution)/shard_map/scatter_exit/ppermute | solution.py:108
  559.9 5.0 collective-permute-done.74
  574.9 5.1 collective-permute-start.77
  595.5 12.2 %shard_map.369 = (f32[2,3,80,640]{3,2,1,0:T(8,128)}, f32[2,40,1280]{2,1,0:T(8,128)}, f32[2,80,2560]{2,1,0:T(8,128)}, f32[2,160,1280]{2,1,0:T(8,128)}, f32[142,2,...) custom-call(f32[2]{0:T(128)} %pad_maximum_fusion.5.corrections_ref, ...), custom_call_target="tpu_custom_call" | custom-call | tf_op jit(solution)/shard_map/pallas_call | solution.py:1095
  626.6 5.8 shard_map.370
  (366 shorter events, 255.6 us)
Async XLA Ops:
  7.2 152.0 %all-gather.3.cloned.1.call-start = ((), (), s32[]{:S(2)}) async-start(), calls=%async_computation | async-start | bytes 4055040 | tf_op jit(solution)/shard_map/all_gather | solution.py:1224
  14.9 24.6 %collective-permute-start.1 = (bf16[1,80,1920]{2,1,0:T(8,128)(2,1)}, bf16[1,80,1920]{2,1,0:T(8,128)(2,1)}, u32[]{:S(2)}, u32[]{:S(2)}) collective-permute-start(bf16[1,80,1920]{2,1,0:T(8,128)(2,1)} %broadcast_in_dim_reshape.2), channel_id=1, source_target_pairs={{0,16},{1,17},{2,18},{3,19},{4,20},{5,21},{6,22},{7,23},{8,24},{9,... | collective-permute-start | bytes 921608 | tf_op jit(solution)/shard_map/gather_entry/ppermute | solution.py:108
  17.5 22.0 %collective-permute-start.2 = (bf16[1,80,1920]{2,1,0:T(8,128)(2,1)}, bf16[1,80,1920]{2,1,0:T(8,128)(2,1)}, u32[]{:S(2)}, u32[]{:S(2)}) collective-permute-start(bf16[1,80,1920]{2,1,0:T(8,128)(2,1)} %broadcast_in_dim_reshape.2), channel_id=1, source_target_pairs={{0,24},{1,25},{2,26},{3,27},{4,28},{5,29},{6,30},{7,31},{8,16},{9,... | collective-permute-start | bytes 921608 | tf_op jit(solution)/shard_map/gather_entry/ppermute | solution.py:108
  44.7 30.6 %collective-permute-start.3 = (bf16[4,80,1920]{2,1,0:T(8,128)(2,1)}, bf16[4,80,1920]{2,1,0:T(8,128)(2,1)S(1)}, u32[]{:S(2)}, u32[]{:S(2)}) collective-permute-start(bf16[4,80,1920]{2,1,0:T(8,128)(2,1)} %constant_dynamic-update-slice_fusion.refs_1_), channel_id=1, source_target_pairs={{0,4},{1,5},{2,3},{3,2},{4,0},{5,1},{6,7},{7,6},{8,12},{9,13},{10,... | collective-permute-start | bytes 3686408 | tf_op jit(solution)/shard_map/gather_entry/ppermute | solution.py:108
  46.3 29.0 %collective-permute-start.4 = (bf16[4,80,1920]{2,1,0:T(8,128)(2,1)}, bf16[4,80,1920]{2,1,0:T(8,128)(2,1)}, u32[]{:S(2)}, u32[]{:S(2)}) collective-permute-start(bf16[4,80,1920]{2,1,0:T(8,128)(2,1)} %constant_dynamic-update-slice_fusion.refs_1_), channel_id=1, source_target_pairs={{0,1},{1,0},{2,6},{3,7},{4,5},{5,4},{6,2},{7,3},{8,9},{9,8},{10,14... | collective-permute-start | bytes 3686408 | tf_op jit(solution)/shard_map/gather_entry/ppermute | solution.py:108
  47.7 24.9 %collective-permute-start.5 = (bf16[1,80,2560]{2,1,0:T(8,128)(2,1)}, bf16[1,80,2560]{2,1,0:T(8,128)(2,1)S(1)}, u32[]{:S(2)}, u32[]{:S(2)}) collective-permute-start(bf16[1,80,2560]{2,1,0:T(8,128)(2,1)} %convert_bitcast_fusion), channel_id=1, source_target_pairs={{0,8},{1,9},{2,10},{3,11},{4,12},{5,13},{6,14},{7,15},{8,0},{9,1},... | collective-permute-start | bytes 1228808 | tf_op jit(solution)/shard_map/gather_up/ppermute | solution.py:108
  98.6 45.3 %collective-permute-start.13 = (bf16[4,80,2560]{2,1,0:T(8,128)(2,1)}, bf16[4,80,2560]{2,1,0:T(8,128)(2,1)}, u32[]{:S(2)}, u32[]{:S(2)}) collective-permute-start(bf16[4,80,2560]{2,1,0:T(8,128)(2,1)} %pad_maximum_fusion.refs_1_), channel_id=1, source_target_pairs={{0,4},{1,5},{2,3},{3,2},{4,0},{5,1},{6,7},{7,6},{8,12},{9,13},{10,... | collective-permute-start | bytes 4915208 | tf_op jit(solution)/shard_map/gather_up/ppermute | solution.py:108
  99.0 44.8 %collective-permute-start.14 = (bf16[4,80,2560]{2,1,0:T(8,128)(2,1)}, bf16[4,80,2560]{2,1,0:T(8,128)(2,1)}, u32[]{:S(2)}, u32[]{:S(2)}) collective-permute-start(bf16[4,80,2560]{2,1,0:T(8,128)(2,1)} %pad_maximum_fusion.refs_1_), channel_id=1, source_target_pairs={{0,1},{1,0},{2,6},{3,7},{4,5},{5,4},{6,2},{7,3},{8,9},{9,8},{10,14... | collective-permute-start | bytes 4915208 | tf_op jit(solution)/shard_map/gather_up/ppermute | solution.py:108
  105.6 32.3 %collective-permute-start.15 = (bf16[1,160,1280]{2,1,0:T(8,128)(2,1)}, bf16[1,160,1280]{2,1,0:T(8,128)(2,1)}, u32[]{:S(2)}, u32[]{:S(2)}) collective-permute-start(bf16[1,160,1280]{2,1,0:T(8,128)(2,1)} %convert_bitcast_fusion.1), channel_id=1, source_target_pairs={{0,8},{1,9},{2,10},{3,11},{4,12},{5,13},{6,14},{7,15},{8,0},{9,1},... | collective-permute-start | bytes 1228808 | tf_op jit(solution)/shard_map/gather_down/ppermute | solution.py:108
  115.2 22.6 %collective-permute-start.16 = (bf16[1,160,1280]{2,1,0:T(8,128)(2,1)}, bf16[1,160,1280]{2,1,0:T(8,128)(2,1)}, u32[]{:S(2)}, u32[]{:S(2)}) collective-permute-start(bf16[1,160,1280]{2,1,0:T(8,128)(2,1)} %convert_bitcast_fusion.1), channel_id=1, source_target_pairs={{0,16},{1,17},{2,18},{3,19},{4,20},{5,21},{6,22},{7,23},{8,24},{9,... | collective-permute-start | bytes 1228808 | tf_op jit(solution)/shard_map/gather_down/ppermute | solution.py:108
  143.8 23.7 %collective-permute-start.17 = (bf16[4,80,2560]{2,1,0:T(8,128)(2,1)}, bf16[4,80,2560]{2,1,0:T(8,128)(2,1)}, u32[]{:S(2)}, u32[]{:S(2)}) collective-permute-start(bf16[4,80,2560]{2,1,0:T(8,128)(2,1)} %collective-permute-done.13.refs_2_), channel_id=1, source_target_pairs={{0,1},{1,0},{2,6},{3,7},{4,5},{5,4},{6,2},{7,3},{8,9},{9,8},{10,14... | collective-permute-start | bytes 4915208 | tf_op jit(solution)/shard_map/gather_up/ppermute | solution.py:108
  144.8 22.7 %collective-permute-start.18 = (bf16[4,80,2560]{2,1,0:T(8,128)(2,1)}, bf16[4,80,2560]{2,1,0:T(8,128)(2,1)}, u32[]{:S(2)}, u32[]{:S(2)}) collective-permute-start(bf16[4,80,2560]{2,1,0:T(8,128)(2,1)} %pad_maximum_fusion.refs_1_), channel_id=1, source_target_pairs={{0,2},{1,3},{2,0},{3,1},{4,6},{5,7},{6,4},{7,5},{8,10},{9,11},{10,... | collective-permute-start | bytes 4915208 | tf_op jit(solution)/shard_map/gather_up/ppermute | solution.py:108
  144.8 22.8 %collective-permute-start.19 = (bf16[4,80,2560]{2,1,0:T(8,128)(2,1)}, bf16[4,80,2560]{2,1,0:T(8,128)(2,1)}, u32[]{:S(2)}, u32[]{:S(2)}) collective-permute-start(bf16[4,80,2560]{2,1,0:T(8,128)(2,1)} %collective-permute-done.13.refs_2_), channel_id=1, source_target_pairs={{0,2},{1,3},{2,0},{3,1},{4,6},{5,7},{6,4},{7,5},{8,10},{9,11},{10,... | collective-permute-start | bytes 4915208 | tf_op jit(solution)/shard_map/gather_up/ppermute | solution.py:108
  145.3 22.2 %collective-permute-start.20 = (bf16[1,160,1280]{2,1,0:T(8,128)(2,1)}, bf16[1,160,1280]{2,1,0:T(8,128)(2,1)}, u32[]{:S(2)}, u32[]{:S(2)}) collective-permute-start(bf16[1,160,1280]{2,1,0:T(8,128)(2,1)} %convert_bitcast_fusion.1), channel_id=1, source_target_pairs={{0,24},{1,25},{2,26},{3,27},{4,28},{5,29},{6,30},{7,31},{8,16},{9,... | collective-permute-start | bytes 1228808 | tf_op jit(solution)/shard_map/gather_down/ppermute | solution.py:108
  170.8 38.8 %collective-permute-start.23 = (bf16[4,160,1280]{2,1,0:T(8,128)(2,1)}, bf16[4,160,1280]{2,1,0:T(8,128)(2,1)}, u32[]{:S(2)}, u32[]{:S(2)}) collective-permute-start(bf16[4,160,1280]{2,1,0:T(8,128)(2,1)} %pad_maximum_fusion.1.refs_7_), channel_id=1, source_target_pairs={{0,4},{1,5},{2,3},{3,2},{4,0},{5,1},{6,7},{7,6},{8,12},{9,13},{10,... | collective-permute-start | bytes 4915208 | tf_op jit(solution)/shard_map/gather_down/ppermute | solution.py:108
  171.4 38.3 %collective-permute-start.24 = (bf16[4,160,1280]{2,1,0:T(8,128)(2,1)}, bf16[4,160,1280]{2,1,0:T(8,128)(2,1)}, u32[]{:S(2)}, u32[]{:S(2)}) collective-permute-start(bf16[4,160,1280]{2,1,0:T(8,128)(2,1)} %pad_maximum_fusion.1.refs_7_), channel_id=1, source_target_pairs={{0,1},{1,0},{2,6},{3,7},{4,5},{5,4},{6,2},{7,3},{8,9},{9,8},{10,14... | collective-permute-start | bytes 4915208 | tf_op jit(solution)/shard_map/gather_down/ppermute | solution.py:108
  306.9 23.9 %collective-permute-start.33 = (bf16[4,160,1280]{2,1,0:T(8,128)(2,1)}, bf16[4,160,1280]{2,1,0:T(8,128)(2,1)}, u32[]{:S(2)}, u32[]{:S(2)}) collective-permute-start(bf16[4,160,1280]{2,1,0:T(8,128)(2,1)} %shard_map.354), channel_id=1, source_target_pairs={{0,1},{1,0},{2,6},{3,7},{4,5},{5,4},{6,2},{7,3},{8,9},{9,8},{10,14... | collective-permute-start | bytes 4915208 | tf_op jit(solution)/shard_map/scatter_down/ppermute | solution.py:108
  308.0 22.9 %collective-permute-start.34 = (f32[71,1280]{1,0:T(8,128)S(1)}, f32[71,1280]{1,0:T(8,128)}, u32[]{:S(2)}, u32[]{:S(2)}) collective-permute-start(f32[71,1280]{1,0:T(8,128)S(1)} %select_add_fusion), channel_id=1, source_target_pairs={{0,8},{1,9},{2,10},{3,11},{4,12},{5,13},{6,14},{7,15},{8,0},{9,1},... | collective-permute-start | bytes 1090568 | tf_op jit(solution)/shard_map/sum_head/ppermute | solution.py:108
  336.9 39.7 %collective-permute-start.38 = (bf16[12,80,2560]{2,1,0:T(8,128)(2,1)}, bf16[12,80,2560]{2,1,0:T(8,128)(2,1)}, u32[]{:S(2)}, u32[]{:S(2)}) collective-permute-start(bf16[12,80,2560]{2,1,0:T(8,128)(2,1)} %get-tuple-element.497), channel_id=1, source_target_pairs={{0,2},{1,3},{2,0},{3,1},{4,6},{5,7},{6,4},{7,5},{8,10},{9,11},{10,... | collective-permute-start | bytes 14745608 | tf_op jit(solution)/shard_map/scatter_up/ppermute | solution.py:108
  336.9 39.7 %collective-permute-start.35 = (bf16[4,160,1280]{2,1,0:T(8,128)(2,1)}, bf16[4,160,1280]{2,1,0:T(8,128)(2,1)}, u32[]{:S(2)}, u32[]{:S(2)}) collective-permute-start(bf16[4,160,1280]{2,1,0:T(8,128)(2,1)} %get-tuple-element.494), channel_id=1, source_target_pairs={{0,4},{1,5},{2,3},{3,2},{4,0},{5,1},{6,7},{7,6},{8,12},{9,13},{10,... | collective-permute-start | bytes 4915208 | tf_op jit(solution)/shard_map/scatter_down/ppermute | solution.py:108
  338.0 38.5 %collective-permute-start.36 = (bf16[4,160,1280]{2,1,0:T(8,128)(2,1)}, bf16[4,160,1280]{2,1,0:T(8,128)(2,1)}, u32[]{:S(2)}, u32[]{:S(2)}) collective-permute-start(bf16[4,160,1280]{2,1,0:T(8,128)(2,1)} %get-tuple-element.495), channel_id=1, source_target_pairs={{0,1},{1,0},{2,6},{3,7},{4,5},{5,4},{6,2},{7,3},{8,9},{9,8},{10,14... | collective-permute-start | bytes 4915208 | tf_op jit(solution)/shard_map/scatter_down/ppermute | solution.py:108
  339.1 37.4 %collective-permute-start.37 = (bf16[4,80,2560]{2,1,0:T(8,128)(2,1)}, bf16[4,80,2560]{2,1,0:T(8,128)(2,1)}, u32[]{:S(2)}, u32[]{:S(2)}) collective-permute-start(bf16[4,80,2560]{2,1,0:T(8,128)(2,1)} %get-tuple-element.496), channel_id=1, source_target_pairs={{0,2},{1,3},{2,0},{3,1},{4,6},{5,7},{6,4},{7,5},{8,10},{9,11},{10,... | collective-permute-start | bytes 4915208 | tf_op jit(solution)/shard_map/scatter_up/ppermute | solution.py:108
  339.1 37.4 %collective-permute-start.39 = (f32[71,1280]{1,0:T(8,128)S(1)}, f32[71,1280]{1,0:T(8,128)}, u32[]{:S(2)}, u32[]{:S(2)}) collective-permute-start(f32[71,1280]{1,0:T(8,128)S(1)} %add.262), channel_id=1, source_target_pairs={{0,16},{1,17},{2,18},{3,19},{4,20},{5,21},{6,22},{7,23},{8,24},{9,... | collective-permute-start | bytes 1090568 | tf_op jit(solution)/shard_map/sum_head/ppermute | solution.py:108
  381.0 24.6 %collective-permute-start.42 = (bf16[4,80,2560]{2,1,0:T(8,128)(2,1)}, bf16[4,80,2560]{2,1,0:T(8,128)(2,1)}, u32[]{:S(2)}, u32[]{:S(2)}) collective-permute-start(bf16[4,80,2560]{2,1,0:T(8,128)(2,1)} %get-tuple-element.518), channel_id=1, source_target_pairs={{0,1},{1,0},{2,6},{3,7},{4,5},{5,4},{6,2},{7,3},{8,9},{9,8},{10,14... | collective-permute-start | bytes 4915208 | tf_op jit(solution)/shard_map/scatter_up/ppermute | solution.py:108
  382.1 23.4 %collective-permute-start.44 = (bf16[12,40,1280]{2,1,0:T(8,128)(2,1)}, bf16[12,40,1280]{2,1,0:T(8,128)(2,1)}, u32[]{:S(2)}, u32[]{:S(2)}) collective-permute-start(bf16[12,40,1280]{2,1,0:T(8,128)(2,1)} %get-tuple-element.520), channel_id=1, source_target_pairs={{0,2},{1,3},{2,0},{3,1},{4,6},{5,7},{6,4},{7,5},{8,10},{9,11},{10,... | collective-permute-start | bytes 3686408 | tf_op jit(solution)/shard_map/scatter_exit/ppermute | solution.py:108
  410.2 25.9 %collective-permute-start.45 = (bf16[4,80,2560]{2,1,0:T(8,128)(2,1)}, bf16[4,80,2560]{2,1,0:T(8,128)(2,1)}, u32[]{:S(2)}, u32[]{:S(2)}) collective-permute-start(bf16[4,80,2560]{2,1,0:T(8,128)(2,1)} %get-tuple-element.537), channel_id=1, source_target_pairs={{0,4},{1,5},{2,3},{3,2},{4,0},{5,1},{6,7},{7,6},{8,12},{9,13},{10,... | collective-permute-start | bytes 4915208 | tf_op jit(solution)/shard_map/scatter_up/ppermute | solution.py:108
  436.0 22.0 %collective-permute-start.50 = (bf16[12,80,1024]{2,1,0:T(8,128)(2,1)}, bf16[12,80,1024]{2,1,0:T(8,128)(2,1)}, u32[]{:S(2)}, u32[]{:S(2)}) collective-permute-start(bf16[12,80,1024]{2,1,0:T(8,128)(2,1)} %get-tuple-element.545), channel_id=1, source_target_pairs={{0,2},{1,3},{2,0},{3,1},{4,6},{5,7},{6,4},{7,5},{8,10},{9,11},{10,... | collective-permute-start | bytes 5898248 | tf_op jit(solution)/shard_map/scatter_entry_a/ppermute | solution.py:108
  436.0 21.9 %collective-permute-start.52 = (bf16[12,80,896]{2,1,0:T(8,128)(2,1)}, bf16[12,80,896]{2,1,0:T(8,128)(2,1)}, u32[]{:S(2)}, u32[]{:S(2)}) collective-permute-start(bf16[12,80,896]{2,1,0:T(8,128)(2,1)} %get-tuple-element.547), channel_id=1, source_target_pairs={{0,2},{1,3},{2,0},{3,1},{4,6},{5,7},{6,4},{7,5},{8,10},{9,11},{10,... | collective-permute-start | bytes 5160968 | tf_op jit(solution)/shard_map/scatter_entry_b/ppermute | solution.py:108
  462.3 25.7 %collective-permute-start.53 = (bf16[4,80,1024]{2,1,0:T(8,128)(2,1)}, bf16[4,80,1024]{2,1,0:T(8,128)(2,1)}, u32[]{:S(2)}, u32[]{:S(2)}) collective-permute-start(bf16[4,80,1024]{2,1,0:T(8,128)(2,1)} %get-tuple-element.566), channel_id=1, source_target_pairs={{0,1},{1,0},{2,6},{3,7},{4,5},{5,4},{6,2},{7,3},{8,9},{9,8},{10,14... | collective-permute-start | bytes 1966088 | tf_op jit(solution)/shard_map/scatter_entry_a/ppermute | solution.py:108
  463.4 24.6 %collective-permute-start.54 = (bf16[4,80,896]{2,1,0:T(8,128)(2,1)}, bf16[4,80,896]{2,1,0:T(8,128)(2,1)}, u32[]{:S(2)}, u32[]{:S(2)}) collective-permute-start(bf16[4,80,896]{2,1,0:T(8,128)(2,1)} %get-tuple-element.567), channel_id=1, source_target_pairs={{0,1},{1,0},{2,6},{3,7},{4,5},{5,4},{6,2},{7,3},{8,9},{9,8},{10,14... | collective-permute-start | bytes 1720328 | tf_op jit(solution)/shard_map/scatter_entry_b/ppermute | solution.py:108
  464.4 23.6 %collective-permute-start.55 = (bf16[1,80,2560]{2,1,0:T(8,128)(2,1)}, bf16[1,80,2560]{2,1,0:T(8,128)(2,1)}, u32[]{:S(2)}, u32[]{:S(2)}) collective-permute-start(bf16[1,80,2560]{2,1,0:T(8,128)(2,1)} %get-tuple-element.568), channel_id=1, source_target_pairs={{0,8},{1,9},{2,10},{3,11},{4,12},{5,13},{6,14},{7,15},{8,0},{9,1},... | collective-permute-start | bytes 1228808 | tf_op jit(solution)/shard_map/scatter_up/ppermute | solution.py:108
  464.4 23.6 %collective-permute-start.56 = (bf16[1,80,2560]{2,1,0:T(8,128)(2,1)}, bf16[1,80,2560]{2,1,0:T(8,128)(2,1)}, u32[]{:S(2)}, u32[]{:S(2)}) collective-permute-start(bf16[1,80,2560]{2,1,0:T(8,128)(2,1)} %get-tuple-element.569), channel_id=1, source_target_pairs={{0,16},{1,17},{2,18},{3,19},{4,20},{5,21},{6,22},{7,23},{8,24},{9,... | collective-permute-start | bytes 1228808 | tf_op jit(solution)/shard_map/scatter_up/ppermute | solution.py:108
  (99 other events, 1095.0 us)
Sparse Core Ops, SparseCore 0:
  44.8 90.1 all-gather.2

commit v6 on v5

--- a/solution.py
+++ b/solution.py
@@ -1267,7 +1267,7 @@
         norm_params[5:6],
         scales,
         targets,
-        320,
+        160,
     )
     loss_local = jnp.sum(losses.reshape(-1, 8, 128)[:, 0, 0]) if losses.ndim > 1 else losses[0]
 
@@ -1285,7 +1285,7 @@
     d_head = contract(d_logits, final_norm)[: head_rows + head_rows % 2]
     paths["head"] = Travel("sum_head", total_steps(plan, d_head, halves=True))
     (d_mlp_out,) = start("down head", d_mlp_out)
-    d_up_pre = hidden_back(d_mlp_out, slope, down_all, 512)
+    d_up_pre = hidden_back(d_mlp_out, slope, down_all, 1024)
     (d_up_pre,) = wait("down head", d_up_pre)
     (d_up_pre,) = start("down head", d_up_pre)
     leave("up", normed_two, d_up_pre, rows_here, [up_weight.shape[1]], 2560)

time: 646 us -> 644 us (level)
  no operation moved by 1% of the time
where the time goes in v6:
time: 644 us; the launch traced here: 638 us
  Pallas kernels  258 us (40%)
  waiting for transfers between devices  144 us (22%)
  starting transfers between devices  106 us (16%)
  other arithmetic  65.1 us (10%)
  local copies, waits for them, and re-layouts  33.2 us (5%)
  between operations  19.5 us (3%)
  matrix products  11.8 us (2%)
    ppermute x86, waiting for transfers between devices, send(): return lax.ppermute(value, AXES, pairs)  144 us
    ppermute x86, starting transfers between devices, send(): return lax.ppermute(value, AXES, pairs)  106 us
    pallas_call x3, Pallas kernels, with_matrices(): pl.pallas_call(kernel, out_shape=[jax.ShapeDtypeStruct(shape, dtype) for...  68 us
    pallas_call x3, Pallas kernels, by_blocks(): pl.pallas_call(body, out_shape=[jax.ShapeDtypeStruct(shape, dtype) for sh...  51.2 us
    pallas_call x3, Pallas kernels, weight_grad(): pl.pallas_call(kernel, out_shape=[jax.ShapeDtypeStruct((count, rows, widt...  49.8 us
    pallas_call x9, Pallas kernels, make_sums(): pl.pallas_call(kernel, out_shape=[jax.ShapeDtypeStruct((job.count,) + job...  36.5 us
    pallas_call x2, Pallas kernels, attend_call(): pl.pallas_call(functools.partial(kernel, groups, pairs), out_shape=jax.Sh...  30.3 us
    unnamed x95, local copies, waits for them, and re-layouts  16.3 us
  transfers between devices with their start and end apart: 87, of which 35 were waited for; matrix products, arithmetic and copies ran while one was open for 12% of the time, Pallas kernels for 26%

profile of v6, /device:TPU:0, one launch (start us, length us, event | category | flops | bytes accessed | tf_op | source)
XLA Modules:
  0.0 638.3 jit_solution(16428834160784570921)
XLA Ops:
  31.7 7.8 %collective-permute-done.1 = bf16[1,80,1920]{2,1,0:T(8,128)(2,1)} collective-permute-done((bf16[1,80,1920]{2,1,0:T(8,128)(2,1)}, bf16[1,80,1920]{2,1,0:T(8,128)(2,1)}, u32[]{:S(2)}, u32[]{:S(2)}) %collective-permute-start.1) | collective-permute-done | bytes 307232 | tf_op jit(solution)/shard_map/gather_entry/ppermute | solution.py:108
  47.7 5.7 collective-permute-start.5
  54.5 18.2 %collective-permute-done.5 = bf16[1,80,2560]{2,1,0:T(8,128)(2,1)S(1)} collective-permute-done((bf16[1,80,2560]{2,1,0:T(8,128)(2,1)}, bf16[1,80,2560]{2,1,0:T(8,128)(2,1)S(1)}, u32[]{:S(2)}, u32[]{:S(2)}) %collective-permute-start.5) | collective-permute-done | bytes 409632 | tf_op jit(solution)/shard_map/gather_up/ppermute | solution.py:108
  78.8 13.8 %collective-permute-done.10 = bf16[1,80,2560]{2,1,0:T(8,128)(2,1)S(1)} collective-permute-done((bf16[1,80,2560]{2,1,0:T(8,128)(2,1)}, bf16[1,80,2560]{2,1,0:T(8,128)(2,1)S(1)}, u32[]{:S(2)}, u32[]{:S(2)}) %collective-permute-start.10) | collective-permute-done | bytes 409632 | tf_op jit(solution)/shard_map/gather_up/ppermute | solution.py:108
  105.6 9.7 %collective-permute-start.15 = (bf16[1,160,1280]{2,1,0:T(8,128)(2,1)}, bf16[1,160,1280]{2,1,0:T(8,128)(2,1)}, u32[]{:S(2)}, u32[]{:S(2)}) collective-permute-start(bf16[1,160,1280]{2,1,0:T(8,128)(2,1)} %convert_bitcast_fusion.1), channel_id=1, source_target_pairs={{0,8},{1,9},{2,10},{3,11},{4,12},{5,13},{6,14},{7,15},{8,0},{9,1},... | collective-permute-start | bytes 1228808 | tf_op jit(solution)/shard_map/gather_down/ppermute | solution.py:108
  116.3 16.1 %shard_map.348 = (bf16[640,3840]{1,0:T(8,128)(2,1)}, bf16[1280,3840]{1,0:T(8,128)(2,1)}) custom-call(s32[32]{0:T(128)} %dynamic-slice_bitcast_fusion.slots_ref, bf16[640,1280]{1,0:T(8,128)(2,1)} %add_convert_fusion.1.refs_0_.left_ref, bf16[4,80,1920]{2,1,0:T(8,128)(2,1)} %constant_dynamic-update-slice_fusion.refs_1_, bf16[4,80,1920]{2,1,0:T(8,128)(2,1)} %copy-done.39, ...), custom_call_target="tpu_custom_call" | custom-call | flops 6291456000 | bytes 16384000 | tf_op jit(solution)/shard_map/pallas_call | solution.py:623
  132.4 5.5 collective-permute-done.15
  137.9 6.0 collective-permute-done.13.refs_2_
  147.9 11.3 %shard_map.349 = bf16[640,1280]{1,0:T(8,128)(2,1)} custom-call(s32[4,160,1]{2,1,0:T(8,128)} %copy.65.column_ref, s32[4,1,320]{2,1,0:T(1,128)} %tile.5.row_ref, bf16[640,3840]{1,0:T(8,128)(2,1)} %get-tuple-element.413.qkv_ref), custom_call_target="tpu_custom_call" | custom-call | flops 524288000 | bytes 9830400 | tf_op jit(solution)/shard_map/pallas_call | solution.py:514
  176.5 26.0 %shard_map.350 = (bf16[640,5120]{1,0:T(8,128)(2,1)}, bf16[640,5120]{1,0:T(8,128)(2,1)}, bf16[1280,5120]{1,0:T(8,128)(2,1)}) custom-call(s32[32]{0:T(128)} %dynamic-slice_bitcast_fusion.slots_ref, bf16[640,1280]{1,0:T(8,128)(2,1)} %add_convert_fusion.refs_0_.left_ref, bf16[4,80,2560]{2,1,0:T(8,128)(2,1)} %pad_maximum_fusion.refs_1_, ...), custom_call_target="tpu_custom_call" | custom-call | flops 8388608000 | bytes 27852800 | tf_op jit(solution)/shard_map/pallas_call | solution.py:623
  202.6 7.1 %collective-permute-done.23.refs_8_ = bf16[4,160,1280]{2,1,0:T(8,128)(2,1)} collective-permute-done((bf16[4,160,1280]{2,1,0:T(8,128)(2,1)}, bf16[4,160,1280]{2,1,0:T(8,128)(2,1)}, u32[]{:S(2)}, u32[]{:S(2)}) %collective-permute-start.23) | collective-permute-done | bytes 1638432 | tf_op jit(solution)/shard_map/gather_down/ppermute | solution.py:108
  221.8 9.2 %collective-permute-done.25.refs_10_ = bf16[4,160,1280]{2,1,0:T(8,128)(2,1)} collective-permute-done((bf16[4,160,1280]{2,1,0:T(8,128)(2,1)}, bf16[4,160,1280]{2,1,0:T(8,128)(2,1)}, u32[]{:S(2)}, u32[]{:S(2)}) %collective-permute-start.25) | collective-permute-done | bytes 1638432 | tf_op jit(solution)/shard_map/gather_down/ppermute | solution.py:108
  237.3 26.0 %shard_map.351 = (f32[640,1280]{1,0:T(8,128)}, bf16[640,1280]{1,0:T(8,128)(2,1)}, bf16[640,256]{1,0:T(8,128)(2,1)}, f32[640,1280]{1,0:T(8,128)}, bf16[640,1280]{...) custom-call(s32[32]{0:T(128)} %dynamic-slice_bitcast_fusion.slots_ref, ...), custom_call_target="tpu_custom_call" | custom-call | flops 8388608000 | bytes 33793024 | tf_op jit(solution)/shard_map/pallas_call | solution.py:623
  263.3 17.0 %shard_map.352 = (bf16[16,160,1280]{2,1,0:T(8,128)(2,1)}, bf16[12,160,1280]{2,1,0:T(8,128)(2,1)}, bf16[4,160,1280]{2,1,0:T(8,128)(2,1)}) custom-call(s32[32]{0:T(128)} %dynamic-slice_bitcast_fusion.slots_ref, bf16[640,5120]{1,0:T(8,128)(2,1)} %get-tuple-element.437.refs_0_.left_ref, bf16[640,1280]{1,0:T(8,128)(2,1)} %get-tuple-element.472.right_ref.d_out_ref), custom_call_target="tpu_custom_call" | custom-call | flops 8388608000 | bytes 21299200 | tf_op jit(solution)/shard_map/pallas_call | solution.py:977
  284.8 15.4 %shard_map.353.right_ref.d_up_ref = bf16[640,5120]{1,0:T(8,128)(2,1)} custom-call(bf16[640,1280]{1,0:T(8,128)(2,1)} %get-tuple-element.472.right_ref.d_out_ref, bf16[5120,1280]{1,0:T(8,128)(2,1)} %get-tuple-element.473.matrix_ref, bf16[640,5120]{1,0:T(8,128)(2,1)} %get-tuple-element.474.slope_ref), custom_call_target="tpu_custom_call" | custom-call | flops 8388608000 | bytes 27852800 | tf_op jit(solution)/shard_map/pallas_call | solution.py:692
  306.5 5.2 collective-permute-start.34
  311.7 17.6 %shard_map.355 = (bf16[16,80,2560]{2,1,0:T(8,128)(2,1)}, bf16[12,80,2560]{2,1,0:T(8,128)(2,1)}, bf16[4,80,2560]{2,1,0:T(8,128)(2,1)}) custom-call(s32[32]{0:T(128)} %dynamic-slice_bitcast_fusion.slots_ref, bf16[640,1280]{1,0:T(8,128)(2,1)} %add_convert_fusion.refs_0_.left_ref, bf16[640,5120]{1,0:T(8,128)(2,1)} %shard_map.353.right_ref.d_up_ref), custom_call_target="tpu_custom_call" | custom-call | flops 8388608000 | bytes 21299200 | tf_op jit(solution)/shard_map/pallas_call | solution.py:977
  330.5 4.9 shard_map.356
  340.4 23.9 %shard_map.357 = (f32[640,1280]{1,0:T(8,128)}, bf16[640,1280]{1,0:T(8,128)(2,1)}, bf16[640,1280]{1,0:T(8,128)(2,1)}) custom-call(bf16[640,5120]{1,0:T(8,128)(2,1)} %shard_map.353.right_ref.d_up_ref, bf16[1280,5120]{1,0:T(8,128)(2,1)} %get-tuple-element.500.up_ref, f32[640,1280]{1,0:T(8,128)} %copy-done.2, f32[1,1280]{1,0:T(1,128)} %get-tuple-element.787.gain_ref, ...), custom_call_target="tpu_custom_call" | custom-call | flops 10485760000 | bytes 36049920 | tf_op jit(solution)/shard_map/pallas_call | solution.py:692
  364.2 6.4 convolution_convert_fusion
  375.0 4.4 shard_map.358
  383.3 19.0 %shard_map.360.right_ref.rows_ref = bf16[640,3840]{1,0:T(8,128)(2,1)} custom-call(s32[4,160,1]{2,1,0:T(8,128)} %copy.65.column_ref, s32[4,1,320]{2,1,0:T(1,128)} %tile.5.row_ref, bf16[640,3840]{1,0:T(8,128)(2,1)} %get-tuple-element.413.qkv_ref, bf16[640,1280]{1,0:T(8,128)(2,1)} %get-tuple-element.521.d_context_ref), custom_call_target="tpu_custom_call" | custom-call | flops 1310720000 | bytes 24576000 | tf_op jit(solution)/shard_map/pallas_call | solution.py:514
  404.0 4.6 shard_map.361
  416.2 15.2 %shard_map.362 = (bf16[16,80,1024]{2,1,0:T(8,128)(2,1)}, bf16[12,80,1024]{2,1,0:T(8,128)(2,1)}, bf16[4,80,1024]{2,1,0:T(8,128)(2,1)}, bf16[16,80,896]{2,1,0:T(8,...) custom-call(s32[64]{0:T(128)} %pad_add_fusion.1.slots_ref, ...), custom_call_target="tpu_custom_call" | custom-call | flops 6291456000 | bytes 16384000 | tf_op jit(solution)/shard_map/pallas_call | solution.py:977
  441.3 11.9 %shard_map.364 = f32[640,1280]{1,0:T(8,128)} custom-call(bf16[640,3840]{1,0:T(8,128)(2,1)} %shard_map.360.right_ref.rows_ref, bf16[1280,3840]{1,0:T(8,128)(2,1)} %get-tuple-element.549.matrix_ref), custom_call_target="tpu_custom_call" | custom-call | flops 6291456000 | bytes 18022400 | tf_op jit(solution)/shard_map/pallas_call | solution.py:692
  470.6 15.1 %collective-permute-done.57 = f32[71,1280]{1,0:T(8,128)S(1)} collective-permute-done((f32[71,1280]{1,0:T(8,128)S(1)}, f32[71,1280]{1,0:T(8,128)S(1)}, u32[]{:S(2)}, u32[]{:S(2)}) %collective-permute-start.57) | collective-permute-done | bytes 363552 | tf_op jit(solution)/shard_map/sum_head/ppermute | solution.py:108
  486.4 4.8 shard_map.366
  509.6 7.5 %collective-permute-done.61.refs_14_.refs_18_.refs_22_ = bf16[4,40,1280]{2,1,0:T(8,128)(2,1)S(1)} collective-permute-done((bf16[4,40,1280]{2,1,0:T(8,128)(2,1)S(1)}, bf16[4,40,1280]{2,1,0:T(8,128)(2,1)S(1)}, u32[]{:S(2)}, u32[]{:S(2)}) %collective-permute-start.61) | collective-permute-done | bytes 409632 | tf_op jit(solution)/shard_map/scatter_exit/ppermute | solution.py:108
  558.3 5.1 collective-permute-done.74
  573.3 5.1 collective-permute-start.77
  594.0 12.2 %shard_map.369 = (f32[2,3,80,640]{3,2,1,0:T(8,128)}, f32[2,40,1280]{2,1,0:T(8,128)}, f32[2,80,2560]{2,1,0:T(8,128)}, f32[2,160,1280]{2,1,0:T(8,128)}, f32[142,2,...) custom-call(f32[2]{0:T(128)} %pad_maximum_fusion.5.corrections_ref, ...), custom_call_target="tpu_custom_call" | custom-call | tf_op jit(solution)/shard_map/pallas_call | solution.py:1095
  625.2 5.8 shard_map.370
  (366 shorter events, 255.6 us)
Async XLA Ops:
  7.2 152.0 %all-gather.3.cloned.1.call-start = ((), (), s32[]{:S(2)}) async-start(), calls=%async_computation | async-start | bytes 4055040 | tf_op jit(solution)/shard_map/all_gather | solution.py:1224
  14.9 24.6 %collective-permute-start.1 = (bf16[1,80,1920]{2,1,0:T(8,128)(2,1)}, bf16[1,80,1920]{2,1,0:T(8,128)(2,1)}, u32[]{:S(2)}, u32[]{:S(2)}) collective-permute-start(bf16[1,80,1920]{2,1,0:T(8,128)(2,1)} %broadcast_in_dim_reshape.2), channel_id=1, source_target_pairs={{0,16},{1,17},{2,18},{3,19},{4,20},{5,21},{6,22},{7,23},{8,24},{9,... | collective-permute-start | bytes 921608 | tf_op jit(solution)/shard_map/gather_entry/ppermute | solution.py:108
  17.5 22.0 %collective-permute-start.2 = (bf16[1,80,1920]{2,1,0:T(8,128)(2,1)}, bf16[1,80,1920]{2,1,0:T(8,128)(2,1)}, u32[]{:S(2)}, u32[]{:S(2)}) collective-permute-start(bf16[1,80,1920]{2,1,0:T(8,128)(2,1)} %broadcast_in_dim_reshape.2), channel_id=1, source_target_pairs={{0,24},{1,25},{2,26},{3,27},{4,28},{5,29},{6,30},{7,31},{8,16},{9,... | collective-permute-start | bytes 921608 | tf_op jit(solution)/shard_map/gather_entry/ppermute | solution.py:108
  44.7 30.6 %collective-permute-start.3 = (bf16[4,80,1920]{2,1,0:T(8,128)(2,1)}, bf16[4,80,1920]{2,1,0:T(8,128)(2,1)S(1)}, u32[]{:S(2)}, u32[]{:S(2)}) collective-permute-start(bf16[4,80,1920]{2,1,0:T(8,128)(2,1)} %constant_dynamic-update-slice_fusion.refs_1_), channel_id=1, source_target_pairs={{0,4},{1,5},{2,3},{3,2},{4,0},{5,1},{6,7},{7,6},{8,12},{9,13},{10,... | collective-permute-start | bytes 3686408 | tf_op jit(solution)/shard_map/gather_entry/ppermute | solution.py:108
  46.3 29.0 %collective-permute-start.4 = (bf16[4,80,1920]{2,1,0:T(8,128)(2,1)}, bf16[4,80,1920]{2,1,0:T(8,128)(2,1)}, u32[]{:S(2)}, u32[]{:S(2)}) collective-permute-start(bf16[4,80,1920]{2,1,0:T(8,128)(2,1)} %constant_dynamic-update-slice_fusion.refs_1_), channel_id=1, source_target_pairs={{0,1},{1,0},{2,6},{3,7},{4,5},{5,4},{6,2},{7,3},{8,9},{9,8},{10,14... | collective-permute-start | bytes 3686408 | tf_op jit(solution)/shard_map/gather_entry/ppermute | solution.py:108
  47.7 24.9 %collective-permute-start.5 = (bf16[1,80,2560]{2,1,0:T(8,128)(2,1)}, bf16[1,80,2560]{2,1,0:T(8,128)(2,1)S(1)}, u32[]{:S(2)}, u32[]{:S(2)}) collective-permute-start(bf16[1,80,2560]{2,1,0:T(8,128)(2,1)} %convert_bitcast_fusion), channel_id=1, source_target_pairs={{0,8},{1,9},{2,10},{3,11},{4,12},{5,13},{6,14},{7,15},{8,0},{9,1},... | collective-permute-start | bytes 1228808 | tf_op jit(solution)/shard_map/gather_up/ppermute | solution.py:108
  98.6 45.3 %collective-permute-start.13 = (bf16[4,80,2560]{2,1,0:T(8,128)(2,1)}, bf16[4,80,2560]{2,1,0:T(8,128)(2,1)}, u32[]{:S(2)}, u32[]{:S(2)}) collective-permute-start(bf16[4,80,2560]{2,1,0:T(8,128)(2,1)} %pad_maximum_fusion.refs_1_), channel_id=1, source_target_pairs={{0,4},{1,5},{2,3},{3,2},{4,0},{5,1},{6,7},{7,6},{8,12},{9,13},{10,... | collective-permute-start | bytes 4915208 | tf_op jit(solution)/shard_map/gather_up/ppermute | solution.py:108
  99.0 44.8 %collective-permute-start.14 = (bf16[4,80,2560]{2,1,0:T(8,128)(2,1)}, bf16[4,80,2560]{2,1,0:T(8,128)(2,1)}, u32[]{:S(2)}, u32[]{:S(2)}) collective-permute-start(bf16[4,80,2560]{2,1,0:T(8,128)(2,1)} %pad_maximum_fusion.refs_1_), channel_id=1, source_target_pairs={{0,1},{1,0},{2,6},{3,7},{4,5},{5,4},{6,2},{7,3},{8,9},{9,8},{10,14... | collective-permute-start | bytes 4915208 | tf_op jit(solution)/shard_map/gather_up/ppermute | solution.py:108
  105.6 32.3 %collective-permute-start.15 = (bf16[1,160,1280]{2,1,0:T(8,128)(2,1)}, bf16[1,160,1280]{2,1,0:T(8,128)(2,1)}, u32[]{:S(2)}, u32[]{:S(2)}) collective-permute-start(bf16[1,160,1280]{2,1,0:T(8,128)(2,1)} %convert_bitcast_fusion.1), channel_id=1, source_target_pairs={{0,8},{1,9},{2,10},{3,11},{4,12},{5,13},{6,14},{7,15},{8,0},{9,1},... | collective-permute-start | bytes 1228808 | tf_op jit(solution)/shard_map/gather_down/ppermute | solution.py:108
  115.2 22.6 %collective-permute-start.16 = (bf16[1,160,1280]{2,1,0:T(8,128)(2,1)}, bf16[1,160,1280]{2,1,0:T(8,128)(2,1)}, u32[]{:S(2)}, u32[]{:S(2)}) collective-permute-start(bf16[1,160,1280]{2,1,0:T(8,128)(2,1)} %convert_bitcast_fusion.1), channel_id=1, source_target_pairs={{0,16},{1,17},{2,18},{3,19},{4,20},{5,21},{6,22},{7,23},{8,24},{9,... | collective-permute-start | bytes 1228808 | tf_op jit(solution)/shard_map/gather_down/ppermute | solution.py:108
  143.8 23.7 %collective-permute-start.17 = (bf16[4,80,2560]{2,1,0:T(8,128)(2,1)}, bf16[4,80,2560]{2,1,0:T(8,128)(2,1)}, u32[]{:S(2)}, u32[]{:S(2)}) collective-permute-start(bf16[4,80,2560]{2,1,0:T(8,128)(2,1)} %collective-permute-done.13.refs_2_), channel_id=1, source_target_pairs={{0,1},{1,0},{2,6},{3,7},{4,5},{5,4},{6,2},{7,3},{8,9},{9,8},{10,14... | collective-permute-start | bytes 4915208 | tf_op jit(solution)/shard_map/gather_up/ppermute | solution.py:108
  144.8 22.7 %collective-permute-start.18 = (bf16[4,80,2560]{2,1,0:T(8,128)(2,1)}, bf16[4,80,2560]{2,1,0:T(8,128)(2,1)}, u32[]{:S(2)}, u32[]{:S(2)}) collective-permute-start(bf16[4,80,2560]{2,1,0:T(8,128)(2,1)} %pad_maximum_fusion.refs_1_), channel_id=1, source_target_pairs={{0,2},{1,3},{2,0},{3,1},{4,6},{5,7},{6,4},{7,5},{8,10},{9,11},{10,... | collective-permute-start | bytes 4915208 | tf_op jit(solution)/shard_map/gather_up/ppermute | solution.py:108
  144.8 22.8 %collective-permute-start.19 = (bf16[4,80,2560]{2,1,0:T(8,128)(2,1)}, bf16[4,80,2560]{2,1,0:T(8,128)(2,1)}, u32[]{:S(2)}, u32[]{:S(2)}) collective-permute-start(bf16[4,80,2560]{2,1,0:T(8,128)(2,1)} %collective-permute-done.13.refs_2_), channel_id=1, source_target_pairs={{0,2},{1,3},{2,0},{3,1},{4,6},{5,7},{6,4},{7,5},{8,10},{9,11},{10,... | collective-permute-start | bytes 4915208 | tf_op jit(solution)/shard_map/gather_up/ppermute | solution.py:108
  145.3 22.2 %collective-permute-start.20 = (bf16[1,160,1280]{2,1,0:T(8,128)(2,1)}, bf16[1,160,1280]{2,1,0:T(8,128)(2,1)}, u32[]{:S(2)}, u32[]{:S(2)}) collective-permute-start(bf16[1,160,1280]{2,1,0:T(8,128)(2,1)} %convert_bitcast_fusion.1), channel_id=1, source_target_pairs={{0,24},{1,25},{2,26},{3,27},{4,28},{5,29},{6,30},{7,31},{8,16},{9,... | collective-permute-start | bytes 1228808 | tf_op jit(solution)/shard_map/gather_down/ppermute | solution.py:108
  170.8 38.8 %collective-permute-start.23 = (bf16[4,160,1280]{2,1,0:T(8,128)(2,1)}, bf16[4,160,1280]{2,1,0:T(8,128)(2,1)}, u32[]{:S(2)}, u32[]{:S(2)}) collective-permute-start(bf16[4,160,1280]{2,1,0:T(8,128)(2,1)} %pad_maximum_fusion.1.refs_7_), channel_id=1, source_target_pairs={{0,4},{1,5},{2,3},{3,2},{4,0},{5,1},{6,7},{7,6},{8,12},{9,13},{10,... | collective-permute-start | bytes 4915208 | tf_op jit(solution)/shard_map/gather_down/ppermute | solution.py:108
  171.4 38.3 %collective-permute-start.24 = (bf16[4,160,1280]{2,1,0:T(8,128)(2,1)}, bf16[4,160,1280]{2,1,0:T(8,128)(2,1)}, u32[]{:S(2)}, u32[]{:S(2)}) collective-permute-start(bf16[4,160,1280]{2,1,0:T(8,128)(2,1)} %pad_maximum_fusion.1.refs_7_), channel_id=1, source_target_pairs={{0,1},{1,0},{2,6},{3,7},{4,5},{5,4},{6,2},{7,3},{8,9},{9,8},{10,14... | collective-permute-start | bytes 4915208 | tf_op jit(solution)/shard_map/gather_down/ppermute | solution.py:108
  305.4 23.9 %collective-permute-start.33 = (bf16[4,160,1280]{2,1,0:T(8,128)(2,1)}, bf16[4,160,1280]{2,1,0:T(8,128)(2,1)}, u32[]{:S(2)}, u32[]{:S(2)}) collective-permute-start(bf16[4,160,1280]{2,1,0:T(8,128)(2,1)} %shard_map.354), channel_id=1, source_target_pairs={{0,1},{1,0},{2,6},{3,7},{4,5},{5,4},{6,2},{7,3},{8,9},{9,8},{10,14... | collective-permute-start | bytes 4915208 | tf_op jit(solution)/shard_map/scatter_down/ppermute | solution.py:108
  306.5 22.9 %collective-permute-start.34 = (f32[71,1280]{1,0:T(8,128)S(1)}, f32[71,1280]{1,0:T(8,128)}, u32[]{:S(2)}, u32[]{:S(2)}) collective-permute-start(f32[71,1280]{1,0:T(8,128)S(1)} %select_add_fusion), channel_id=1, source_target_pairs={{0,8},{1,9},{2,10},{3,11},{4,12},{5,13},{6,14},{7,15},{8,0},{9,1},... | collective-permute-start | bytes 1090568 | tf_op jit(solution)/shard_map/sum_head/ppermute | solution.py:108
  335.3 39.7 %collective-permute-start.38 = (bf16[12,80,2560]{2,1,0:T(8,128)(2,1)}, bf16[12,80,2560]{2,1,0:T(8,128)(2,1)}, u32[]{:S(2)}, u32[]{:S(2)}) collective-permute-start(bf16[12,80,2560]{2,1,0:T(8,128)(2,1)} %get-tuple-element.497), channel_id=1, source_target_pairs={{0,2},{1,3},{2,0},{3,1},{4,6},{5,7},{6,4},{7,5},{8,10},{9,11},{10,... | collective-permute-start | bytes 14745608 | tf_op jit(solution)/shard_map/scatter_up/ppermute | solution.py:108
  335.3 39.7 %collective-permute-start.35 = (bf16[4,160,1280]{2,1,0:T(8,128)(2,1)}, bf16[4,160,1280]{2,1,0:T(8,128)(2,1)}, u32[]{:S(2)}, u32[]{:S(2)}) collective-permute-start(bf16[4,160,1280]{2,1,0:T(8,128)(2,1)} %get-tuple-element.494), channel_id=1, source_target_pairs={{0,4},{1,5},{2,3},{3,2},{4,0},{5,1},{6,7},{7,6},{8,12},{9,13},{10,... | collective-permute-start | bytes 4915208 | tf_op jit(solution)/shard_map/scatter_down/ppermute | solution.py:108
  336.5 38.5 %collective-permute-start.36 = (bf16[4,160,1280]{2,1,0:T(8,128)(2,1)}, bf16[4,160,1280]{2,1,0:T(8,128)(2,1)}, u32[]{:S(2)}, u32[]{:S(2)}) collective-permute-start(bf16[4,160,1280]{2,1,0:T(8,128)(2,1)} %get-tuple-element.495), channel_id=1, source_target_pairs={{0,1},{1,0},{2,6},{3,7},{4,5},{5,4},{6,2},{7,3},{8,9},{9,8},{10,14... | collective-permute-start | bytes 4915208 | tf_op jit(solution)/shard_map/scatter_down/ppermute | solution.py:108
  337.6 37.5 %collective-permute-start.37 = (bf16[4,80,2560]{2,1,0:T(8,128)(2,1)}, bf16[4,80,2560]{2,1,0:T(8,128)(2,1)}, u32[]{:S(2)}, u32[]{:S(2)}) collective-permute-start(bf16[4,80,2560]{2,1,0:T(8,128)(2,1)} %get-tuple-element.496), channel_id=1, source_target_pairs={{0,2},{1,3},{2,0},{3,1},{4,6},{5,7},{6,4},{7,5},{8,10},{9,11},{10,... | collective-permute-start | bytes 4915208 | tf_op jit(solution)/shard_map/scatter_up/ppermute | solution.py:108
  337.6 37.4 %collective-permute-start.39 = (f32[71,1280]{1,0:T(8,128)S(1)}, f32[71,1280]{1,0:T(8,128)}, u32[]{:S(2)}, u32[]{:S(2)}) collective-permute-start(f32[71,1280]{1,0:T(8,128)S(1)} %add.262), channel_id=1, source_target_pairs={{0,16},{1,17},{2,18},{3,19},{4,20},{5,21},{6,22},{7,23},{8,24},{9,... | collective-permute-start | bytes 1090568 | tf_op jit(solution)/shard_map/sum_head/ppermute | solution.py:108
  379.5 24.6 %collective-permute-start.42 = (bf16[4,80,2560]{2,1,0:T(8,128)(2,1)}, bf16[4,80,2560]{2,1,0:T(8,128)(2,1)}, u32[]{:S(2)}, u32[]{:S(2)}) collective-permute-start(bf16[4,80,2560]{2,1,0:T(8,128)(2,1)} %get-tuple-element.518), channel_id=1, source_target_pairs={{0,1},{1,0},{2,6},{3,7},{4,5},{5,4},{6,2},{7,3},{8,9},{9,8},{10,14... | collective-permute-start | bytes 4915208 | tf_op jit(solution)/shard_map/scatter_up/ppermute | solution.py:108
  380.6 23.4 %collective-permute-start.44 = (bf16[12,40,1280]{2,1,0:T(8,128)(2,1)}, bf16[12,40,1280]{2,1,0:T(8,128)(2,1)}, u32[]{:S(2)}, u32[]{:S(2)}) collective-permute-start(bf16[12,40,1280]{2,1,0:T(8,128)(2,1)} %get-tuple-element.520), channel_id=1, source_target_pairs={{0,2},{1,3},{2,0},{3,1},{4,6},{5,7},{6,4},{7,5},{8,10},{9,11},{10,... | collective-permute-start | bytes 3686408 | tf_op jit(solution)/shard_map/scatter_exit/ppermute | solution.py:108
  408.6 25.9 %collective-permute-start.45 = (bf16[4,80,2560]{2,1,0:T(8,128)(2,1)}, bf16[4,80,2560]{2,1,0:T(8,128)(2,1)}, u32[]{:S(2)}, u32[]{:S(2)}) collective-permute-start(bf16[4,80,2560]{2,1,0:T(8,128)(2,1)} %get-tuple-element.537), channel_id=1, source_target_pairs={{0,4},{1,5},{2,3},{3,2},{4,0},{5,1},{6,7},{7,6},{8,12},{9,13},{10,... | collective-permute-start | bytes 4915208 | tf_op jit(solution)/shard_map/scatter_up/ppermute | solution.py:108
  434.5 22.0 %collective-permute-start.50 = (bf16[12,80,1024]{2,1,0:T(8,128)(2,1)}, bf16[12,80,1024]{2,1,0:T(8,128)(2,1)}, u32[]{:S(2)}, u32[]{:S(2)}) collective-permute-start(bf16[12,80,1024]{2,1,0:T(8,128)(2,1)} %get-tuple-element.545), channel_id=1, source_target_pairs={{0,2},{1,3},{2,0},{3,1},{4,6},{5,7},{6,4},{7,5},{8,10},{9,11},{10,... | collective-permute-start | bytes 5898248 | tf_op jit(solution)/shard_map/scatter_entry_a/ppermute | solution.py:108
  434.5 21.9 %collective-permute-start.52 = (bf16[12,80,896]{2,1,0:T(8,128)(2,1)}, bf16[12,80,896]{2,1,0:T(8,128)(2,1)}, u32[]{:S(2)}, u32[]{:S(2)}) collective-permute-start(bf16[12,80,896]{2,1,0:T(8,128)(2,1)} %get-tuple-element.547), channel_id=1, source_target_pairs={{0,2},{1,3},{2,0},{3,1},{4,6},{5,7},{6,4},{7,5},{8,10},{9,11},{10,... | collective-permute-start | bytes 5160968 | tf_op jit(solution)/shard_map/scatter_entry_b/ppermute | solution.py:108
  460.7 25.7 %collective-permute-start.53 = (bf16[4,80,1024]{2,1,0:T(8,128)(2,1)}, bf16[4,80,1024]{2,1,0:T(8,128)(2,1)}, u32[]{:S(2)}, u32[]{:S(2)}) collective-permute-start(bf16[4,80,1024]{2,1,0:T(8,128)(2,1)} %get-tuple-element.566), channel_id=1, source_target_pairs={{0,1},{1,0},{2,6},{3,7},{4,5},{5,4},{6,2},{7,3},{8,9},{9,8},{10,14... | collective-permute-start | bytes 1966088 | tf_op jit(solution)/shard_map/scatter_entry_a/ppermute | solution.py:108
  461.9 24.5 %collective-permute-start.54 = (bf16[4,80,896]{2,1,0:T(8,128)(2,1)}, bf16[4,80,896]{2,1,0:T(8,128)(2,1)}, u32[]{:S(2)}, u32[]{:S(2)}) collective-permute-start(bf16[4,80,896]{2,1,0:T(8,128)(2,1)} %get-tuple-element.567), channel_id=1, source_target_pairs={{0,1},{1,0},{2,6},{3,7},{4,5},{5,4},{6,2},{7,3},{8,9},{9,8},{10,14... | collective-permute-start | bytes 1720328 | tf_op jit(solution)/shard_map/scatter_entry_b/ppermute | solution.py:108
  462.8 23.6 %collective-permute-start.55 = (bf16[1,80,2560]{2,1,0:T(8,128)(2,1)}, bf16[1,80,2560]{2,1,0:T(8,128)(2,1)}, u32[]{:S(2)}, u32[]{:S(2)}) collective-permute-start(bf16[1,80,2560]{2,1,0:T(8,128)(2,1)} %get-tuple-element.568), channel_id=1, source_target_pairs={{0,8},{1,9},{2,10},{3,11},{4,12},{5,13},{6,14},{7,15},{8,0},{9,1},... | collective-permute-start | bytes 1228808 | tf_op jit(solution)/shard_map/scatter_up/ppermute | solution.py:108
  462.8 23.6 %collective-permute-start.56 = (bf16[1,80,2560]{2,1,0:T(8,128)(2,1)}, bf16[1,80,2560]{2,1,0:T(8,128)(2,1)}, u32[]{:S(2)}, u32[]{:S(2)}) collective-permute-start(bf16[1,80,2560]{2,1,0:T(8,128)(2,1)} %get-tuple-element.569), channel_id=1, source_target_pairs={{0,16},{1,17},{2,18},{3,19},{4,20},{5,21},{6,22},{7,23},{8,24},{9,... | collective-permute-start | bytes 1228808 | tf_op jit(solution)/shard_map/scatter_up/ppermute | solution.py:108
  (99 other events, 1089.9 us)
Sparse Core Ops, SparseCore 0:
  44.8 90.1 all-gather.2
